TPU v7x, 256 devices: a whole 4x4x8 slice. The times are simulated.
256 devices in a mesh: gx: 64 (over y_lo, z, x), gy: 4 (over y_hi, core).
Axes of the slice: x: 4, y: 4 (y_hi: 2, y_lo: 2; y = y_hi * 2 + y_lo), z: 8, core: 2. Of those that a mesh axis runs over, the one named last changes fastest.
Arguments:
- populations: float32 [19, 128, 128, 128], P(None, 'gx', 'gy'), may hold values from 0 to 1, as said below
- fluid: int32 [128, 128, 128], P('gx', 'gy'), may hold values 0 or 1
- label: int32 [128, 128, 128], P('gx', 'gy'), may hold values from 0 to 16383, as said below
- wall_wetting: float32 [16384], P('gx'), may hold values from 0.3 to 1
- target: float32 [128, 128, 128], P('gx', 'gy'), may hold values from 0.8 to 1.6
Outputs:
- population_grad: float32 [19, 128, 128, 128], P(None, 'gx', 'gy')
- wetting_grad: float32 [16384], P('gx')
Inputs may be any that keep to these rules, and one draw needn't show every extreme that they name: Cells of x slab j (x from j * 2 to j * 2 + 1) carry labels from j * 256 to j * 256 + 255 only; labels are constant on aligned blocks of 2 x 2 x 4 cells, and every label marks exactly 8 such blocks. `populations`: every entry is positive; the 19 entries of a cell sum to between 0.5 and 2.1.
All inputs are finite; a program needn't handle non-finite values. No bound on the sum of `fluid` on one device may be relied on, other than what follows from the above.
Results may differ from a plain program's by a relative error of at most 0.0003.
Values sent between devices are 32-bit elements; how exact they have to be, the bound alone decides.
No kernel may reach another device: no remote copies, remote signals or barrier semaphores. Data moves between devices by JAX's collectives and lax.ppermute only.
A program may use at most 64 MiB of HBM per device.

v0:
```python
import functools

import jax
import jax.numpy as jnp
from jax import lax
from jax.experimental import pallas as pl
from jax.experimental.pallas import tpu as pltpu
from jax.sharding import PartitionSpec as P

HALO = 8
PAD = 8
OWN = 32
ROWS = OWN + 2 * HALO
TALL = ROWS + 2 * PAD
DEPTH = 128
CHUNKS = ROWS // 8
LABELS = 256

VECTORS = (
    (0, 0, 0), (1, 0, 0), (-1, 0, 0), (0, 1, 0), (0, -1, 0), (0, 0, 1), (0, 0, -1),
    (1, 1, 0), (-1, -1, 0), (1, -1, 0), (-1, 1, 0), (1, 0, 1), (-1, 0, -1), (1, 0, -1), (-1, 0, 1),
    (0, 1, 1), (0, -1, -1), (0, 1, -1), (0, -1, 1),
)
OPPOSITE = (0, 2, 1, 4, 3, 6, 5, 8, 7, 10, 9, 12, 11, 14, 13, 16, 15, 18, 17)
INDEX = {v: i for i, v in enumerate(VECTORS)}
RIGHTWARD = tuple(i for i in range(19) if VECTORS[i][0] == 1)
LEFTWARD = tuple(i for i in range(19) if VECTORS[i][0] == -1)
TURNED = tuple(i for i in range(19) if VECTORS[i][2] != 0)
PLANES = ((0, 1), (1, 2), (0, 2))
COUPLING = 5.0
SHEAR = 1.2
BULK = 1.19
THIRD = 1.5
FOURTH = 1.4
TRACE = (BULK - SHEAR) / 3.0
PULL = COUPLING / 36.0


def axis_index_of(axis, sign):
    v = [0, 0, 0]
    v[axis] = sign
    return INDEX[tuple(v)]


def edge_index_of(a, b, sa, sb):
    v = [0, 0, 0]
    v[a], v[b] = sa, sb
    return INDEX[tuple(v)]


def add(*terms):
    total = None
    for term in terms:
        if term is not None:
            total = term if total is None else total + term
    return total


def sub(a, b):
    if b is None:
        return a
    return -b if a is None else a - b


def scale(c, a):
    return None if a is None else c * a


def mul(a, b):
    return None if a is None or b is None else a * b


def moments(f):
    fourth, mixed, third = {}, {}, {}
    for a, b in PLANES:
        pp, mm = f[edge_index_of(a, b, 1, 1)], f[edge_index_of(a, b, -1, -1)]
        pm, mp = f[edge_index_of(a, b, 1, -1)], f[edge_index_of(a, b, -1, 1)]
        even, odd, cross, skew = pp + mm, pp - mm, pm + mp, pm - mp
        fourth[a, b] = even + cross
        mixed[a, b] = even - cross
        third[a, b] = odd + skew
        third[b, a] = odd - skew
    first, diagonal, total = [], [], f[0]
    for a in range(3):
        b, c = [k for k in range(3) if k != a]
        plus, minus = f[axis_index_of(a, 1)], f[axis_index_of(a, -1)]
        both = plus + minus
        total = total + both
        diagonal.append(both + fourth[tuple(sorted((a, b)))] + fourth[tuple(sorted((a, c)))])
        first.append((plus - minus) + third[a, b] + third[a, c])
    total = total + fourth[0, 1] + fourth[1, 2] + fourth[0, 2]
    return total, first, diagonal, mixed, third, fourth


def from_moments(first, diagonal, mixed, third, fourth, which):
    out = {}
    for i in which:
        v = VECTORS[i]
        axes = [a for a in range(3) if v[a] != 0]
        if not axes:
            out[i] = (fourth[0, 1] + fourth[1, 2] + fourth[0, 2]) - (diagonal[0] + diagonal[1] + diagonal[2])
        elif len(axes) == 1:
            a = axes[0]
            b, c = [k for k in range(3) if k != a]
            even = diagonal[a] - fourth[tuple(sorted((a, b)))] - fourth[tuple(sorted((a, c)))]
            odd = first[a] - third[a, b] - third[a, c]
            out[i] = 0.5 * (even + odd if v[a] > 0 else even - odd)
        else:
            a, b = axes
            value = fourth[a, b] + mixed[a, b] if v[a] * v[b] > 0 else fourth[a, b] - mixed[a, b]
            value = value + third[a, b] if v[a] > 0 else value - third[a, b]
            value = value + third[b, a] if v[b] > 0 else value - third[b, a]
            out[i] = 0.25 * value
    return out


def rated(first, diagonal, mixed, third, fourth):
    trace = TRACE * (diagonal[0] + diagonal[1] + diagonal[2])
    return (
        [SHEAR * m for m in first],
        [SHEAR * m + trace for m in diagonal],
        {k: SHEAR * m for k, m in mixed.items()},
        {k: THIRD * m for k, m in third.items()},
        {k: FOURTH * m for k, m in fourth.items()},
    )


def linear_part(f, share, which):
    total, first, diagonal, mixed, third, fourth = moments(f)
    change = from_moments(*rated(first, diagonal, mixed, third, fourth), which)
    return total, first, {i: f[i] - share * change[i] for i in which}


def balance_part(density, flow, velocity, share, which):
    d = density * share
    m = [flow[a] * share for a in range(3)]
    square = [m[a] * velocity[a] for a in range(3)]
    diagonal = [d * (1.0 / 3.0) + square[a] for a in range(3)]
    mixed = {(a, b): m[a] * velocity[b] for a, b in PLANES}
    third = {}
    fourth = {}
    for a, b in PLANES:
        c = 3 - a - b
        third[a, b] = m[a] * (1.0 / 3.0)
        third[b, a] = m[b] * (1.0 / 3.0)
        fourth[a, b] = d * (1.0 / 9.0) + (square[a] + square[b]) * (1.0 / 3.0) - square[c] * (1.0 / 6.0)
    return from_moments(*rated(m, diagonal, mixed, third, fourth), which)


def dual(r):
    get = lambda i: r.get(i)
    first, diagonal = [], []
    plus_of, minus_of = [], []
    for a in range(3):
        p, m = get(axis_index_of(a, 1)), get(axis_index_of(a, -1))
        even = scale(0.5, add(p, m))
        odd = scale(0.5, sub(p, m))
        plus_of.append(even)
        minus_of.append(odd)
        first.append(odd)
        diagonal.append(sub(even, get(0)))
    mixed, third, fourth = {}, {}, {}
    for a, b in PLANES:
        pp, mm = get(edge_index_of(a, b, 1, 1)), get(edge_index_of(a, b, -1, -1))
        pm, mp = get(edge_index_of(a, b, 1, -1)), get(edge_index_of(a, b, -1, 1))
        even, odd, cross, skew = add(pp, mm), sub(pp, mm), add(pm, mp), sub(pm, mp)
        fourth[a, b] = add(sub(sub(scale(0.25, add(even, cross)), plus_of[a]), plus_of[b]), get(0))
        mixed[a, b] = scale(0.25, sub(even, cross))
        third[a, b] = sub(scale(0.25, add(odd, skew)), minus_of[a])
        third[b, a] = sub(scale(0.25, sub(odd, skew)), minus_of[b])
    trace = scale(TRACE, add(*diagonal))
    return (
        [scale(SHEAR, m) for m in first],
        [add(scale(SHEAR, m), trace) for m in diagonal],
        {k: scale(SHEAR, m) for k, m in mixed.items()},
        {k: scale(THIRD, m) for k, m in third.items()},
        {k: scale(FOURTH, m) for k, m in fourth.items()},
    )


def flow_adjoint(first, diagonal, mixed, third, fourth, u):
    q = []
    for a in range(3):
        b, c = [k for k in range(3) if k != a]
        ab, ac, bc = tuple(sorted((a, b))), tuple(sorted((a, c))), tuple(sorted((b, c)))
        along = add(
            scale(2.0, diagonal[a]),
            scale(2.0 / 3.0, add(fourth[ab], fourth[ac])),
            scale(-1.0 / 3.0, fourth[bc]),
        )
        q.append(
            add(
                first[a],
                scale(1.0 / 3.0, add(third[a, b], third[a, c])),
                mul(u[a], along),
                mul(u[b], mixed[ab]),
                mul(u[c], mixed[ac]),
            )
        )
    return q


def collide_adjoint(r, u):
    t = dual(r)
    first, diagonal, mixed, third, fourth = t
    q = flow_adjoint(*t, u)
    square = [u[a] * u[a] for a in range(3)]
    by_density = None
    for a in range(3):
        b, c = [k for k in range(3) if k != a]
        by_density = add(
            by_density,
            u[a] * (first[a] + (1.0 / 3.0) * (third[a, b] + third[a, c]) - q[a]),
            diagonal[a] * (1.0 / 3.0 + square[a]),
        )
    for a, b in PLANES:
        c = 3 - a - b
        by_density = by_density + mixed[a, b] * (u[a] * u[b])
        by_density = by_density + fourth[a, b] * (
            1.0 / 9.0 + (square[a] + square[b]) * (1.0 / 3.0) - square[c] * (1.0 / 6.0)
        )
    drift = [q[a] - first[a] for a in range(3)]
    base = {0: r[0]}
    for a in range(3):
        base[axis_index_of(a, 1)] = r[axis_index_of(a, 1)] + (drift[a] - diagonal[a])
        base[axis_index_of(a, -1)] = r[axis_index_of(a, -1)] - (drift[a] + diagonal[a])
    for a, b in PLANES:
        along = drift[a] - third[a, b]
        across = drift[b] - third[b, a]
        even = diagonal[a] + diagonal[b] + fourth[a, b]
        same, cross = even + mixed[a, b], even - mixed[a, b]
        both, gap = along + across, along - across
        base[edge_index_of(a, b, 1, 1)] = r[edge_index_of(a, b, 1, 1)] + (both - same)
        base[edge_index_of(a, b, -1, -1)] = r[edge_index_of(a, b, -1, -1)] - (both + same)
        base[edge_index_of(a, b, 1, -1)] = r[edge_index_of(a, b, 1, -1)] + (gap - cross)
        base[edge_index_of(a, b, -1, 1)] = r[edge_index_of(a, b, -1, 1)] - (gap + cross)
    return base, by_density, q


def rolled(x, step):
    return x if step == 0 else pltpu.roll(x, step % DEPTH, 1)


def rows_at(t, shift, offset):
    if shift == 0:
        return pl.ds(pl.multiple_of(t * 8 + offset, 8), 8)
    return pl.ds(t * 8 + (offset + shift), 8)


def flat(t):
    return rows_at(t, 0, 0)


def tall(t, shift=0):
    return rows_at(t, shift, PAD)


def each_chunk(body, first=0, last=CHUNKS):
    def step(t, carry):
        body(t)
        return carry

    lax.fori_loop(first, last, step, 0)


def gradient_of(field, doubled, p, t):
    at = lambda dp, dy: field[p + dp, tall(t, dy), :]
    rp, rm, lp, lm = at(1, 1), at(1, -1), at(-1, 1), at(-1, -1)
    along_x = doubled[p + 1, tall(t), :] - doubled[p - 1, tall(t), :] + (rp + rm) - (lp + lm)
    along_y = doubled[p, tall(t, 1), :] - doubled[p, tall(t, -1), :] + (rp + lp) - (rm + lm)
    star = 2.0 * at(0, 0) + at(1, 0) + at(-1, 0) + at(0, 1) + at(0, -1)
    return [along_x, along_y, rolled(star, -1) - rolled(star, 1)]


def with_sides(x):
    return 2.0 * x + rolled(x, 1) + rolled(x, -1)


def edges_kernel(pops, fluid, label, target, low, high):
    low[0:19] = pops[:, :, 0:HALO, :]
    high[0:19] = pops[:, :, OWN - HALO : OWN, :]
    low[19] = fluid[:, 0:HALO, :].astype(jnp.float32)
    high[19] = fluid[:, OWN - HALO : OWN, :].astype(jnp.float32)
    low[20] = label[:, 0:HALO, :].astype(jnp.float32)
    high[20] = label[:, OWN - HALO : OWN, :].astype(jnp.float32)
    low[21] = target[:, 0:HALO, :]
    high[21] = target[:, OWN - HALO : OWN, :]


def put_sends(send_left, send_right, t, lin, first, chosen, effective):
    for k, i in enumerate(LEFTWARD):
        send_left[k, flat(t), :] = lin[0][i]
    for k, i in enumerate(RIGHTWARD):
        send_right[k, flat(t), :] = lin[1][i]
    for a in range(3):
        send_left[5 + a, flat(t), :] = first[0][a]
        send_right[5 + a, flat(t), :] = first[1][a]
    send_left[8, flat(t), :] = chosen[0]
    send_right[8, flat(t), :] = chosen[1]
    send_left[9, flat(t), :] = effective[1]
    send_right[9, flat(t), :] = effective[0]


def start_kernel(
    pops, fluid, label, target, wetting, below, above,
    lin_out, flow_out, density_out, effective_out, share_out, target_out, send_left, send_right,
    wide, label_wide,
):
    wide[:, :, HALO : HALO + OWN, :] = pops[...]
    wide[:, :, 0:HALO, :] = below[0:19]
    wide[:, :, HALO + OWN : ROWS, :] = above[0:19]
    share_out[:, HALO : HALO + OWN, :] = fluid[...].astype(jnp.float32)
    share_out[:, 0:HALO, :] = below[19]
    share_out[:, HALO + OWN : ROWS, :] = above[19]
    label_wide[:, HALO : HALO + OWN, :] = label[...]
    label_wide[:, 0:HALO, :] = below[20].astype(jnp.int32)
    label_wide[:, HALO + OWN : ROWS, :] = above[20].astype(jnp.int32)
    target_out[:, HALO : HALO + OWN, :] = target[...]
    target_out[:, 0:HALO, :] = below[21]
    target_out[:, HALO + OWN : ROWS, :] = above[21]
    half_low = jnp.broadcast_to(wetting[0:1, :], (8, DEPTH))
    half_high = jnp.broadcast_to(wetting[1:2, :], (8, DEPTH))

    def body(t):
        lin, first, chosen, effective = [], [], [], []
        for x in range(2):
            f = {i: wide[i, x, flat(t), :] for i in range(19)}
            share = share_out[x, flat(t), :]
            marks = label_wide[x, flat(t), :]
            spot = jnp.bitwise_and(marks, DEPTH - 1)
            wall = jnp.where(
                jnp.bitwise_and(marks, DEPTH) == 0,
                jnp.take_along_axis(half_low, spot, axis=1),
                jnp.take_along_axis(half_high, spot, axis=1),
            )
            total, momentum, linear = linear_part(f, share, range(19))
            eff = jnp.where(share > 0, 1.0 - jnp.exp(-total), wall)
            for i in range(19):
                lin_out[i, x, flat(t), :] = linear[i]
            for a in range(3):
                flow_out[a, x, flat(t), :] = momentum[a]
            density_out[x, flat(t), :] = total
            effective_out[x, flat(t), :] = eff
            lin.append(linear)
            first.append(momentum)
            chosen.append(jnp.where(share > 0, total, wall))
            effective.append(eff)
        put_sends(send_left, send_right, t, lin, first, chosen, effective)
        send_left[10, flat(t), :] = share_out[0, flat(t), :]
        send_left[11, flat(t), :] = share_out[1, flat(t), :]
        send_right[10, flat(t), :] = share_out[1, flat(t), :]
        send_right[11, flat(t), :] = share_out[0, flat(t), :]

    each_chunk(body)


def step_kernel(is_first, *refs):
    if is_first:
        (lin, flow, density, effective, share, from_left, from_right,
         masks, field, speed, pull_out, lin_out, flow_out, density_out, effective_out, send_left, send_right,
         doubled, relaxed, turned) = refs
    else:
        (lin, flow, density, effective, share, target, masks, from_left, from_right,
         field, speed, pull_out, misfit_out,
         doubled, relaxed, turned) = refs
    sides = ((1, from_left, 0), (4, from_right, 5))

    def place(t):
        def put(p, x, s):
            field[p, tall(t), :] = x
            doubled[p, tall(t), :] = with_sides(x)
            if is_first:
                masks[0, p, tall(t), :] = s
                masks[1, p, tall(t), :] = rolled(s, 1)
                masks[2, p, tall(t), :] = rolled(s, -1)

        for x in range(2):
            put(2 + x, effective[x, flat(t), :], share[x, flat(t), :])
        for near, come, far in sides:
            if is_first:
                s_near, s_far = come[10, flat(t), :], come[11, flat(t), :]
            else:
                s_near, s_far = masks[0, near, tall(t), :], None
            chosen = come[8, flat(t), :]
            put(near, jnp.where(s_near > 0, 1.0 - jnp.exp(-chosen), chosen), s_near)
            put(far, come[9, flat(t), :], s_far)

    each_chunk(place)

    def collide(t):
        for p in range(1, 5):
            own = p in (2, 3)
            pull = gradient_of(field, doubled, p, t)
            psi = field[p, tall(t), :]
            s = masks[0, p, tall(t), :]
            if own:
                rho = density[p - 2, flat(t), :]
                mom = [flow[a, p - 2, flat(t), :] for a in range(3)]
                which = range(19)
                lin_at = {i: lin[i, p - 2, flat(t), :] for i in which}
                for a in range(3):
                    pull_out[a, p - 2, flat(t), :] = pull[a]
            else:
                come = from_left if p == 1 else from_right
                rho = come[8, flat(t), :]
                mom = [come[5 + a, flat(t), :] for a in range(3)]
                which = RIGHTWARD if p == 1 else LEFTWARD
                lin_at = {i: come[k, flat(t), :] for k, i in enumerate(which)}
            push = psi * (PULL / SHEAR)
            full = [mom[a] + push * pull[a] for a in range(3)]
            inverse = 1.0 / rho
            u = [full[a] * inverse for a in range(3)]
            for a in range(3):
                speed[a, p - 1, flat(t), :] = u[a]
            part = balance_part(rho, full, u, s, which)
            for i in which:
                value = lin_at[i] + part[i]
                relaxed[i, p - 1, tall(t), :] = value
                if i in TURNED:
                    turned[TURNED.index(i), p - 1, tall(t), :] = rolled(value, VECTORS[i][2])

    each_chunk(collide)

    def stream(t):
        lin_sent, first_sent, chosen_sent, effective_sent = [], [], [], []
        for x in range(2):
            f = {}
            for i in range(19):
                cx, cy, cz = VECTORS[i]
                if i == 0:
                    f[i] = relaxed[0, 1 + x, tall(t), :]
                    continue
                if cz:
                    source = turned[TURNED.index(i), 1 + x - cx, tall(t, -cy), :]
                else:
                    source = relaxed[i, 1 + x - cx, tall(t, -cy), :]
                open_ = masks[cz % 3, 2 + x - cx, tall(t, -cy), :] > 0
                f[i] = jnp.where(open_, source, relaxed[OPPOSITE[i], 1 + x, tall(t), :])
            s = share[x, flat(t), :]
            if is_first:
                total, momentum, linear = linear_part(f, s, range(19))
                held = effective[x, flat(t), :]
                eff = jnp.where(s > 0, 1.0 - jnp.exp(-total), held)
                for i in range(19):
                    lin_out[i, x, flat(t), :] = linear[i]
                for a in range(3):
                    flow_out[a, x, flat(t), :] = momentum[a]
                density_out[x, flat(t), :] = total
                effective_out[x, flat(t), :] = eff
                lin_sent.append(linear)
                first_sent.append(momentum)
                chosen_sent.append(jnp.where(s > 0, total, held))
                effective_sent.append(eff)
            else:
                total = add(*[f[i] for i in range(19)])
                misfit_out[x, flat(t), :] = s * (total - target[x, flat(t), :])
        if is_first:
            put_sends(send_left, send_right, t, lin_sent, first_sent, chosen_sent, effective_sent)

    each_chunk(stream)


def spread_of(pulled, pulled_doubled, p, t):
    at = lambda a, dp, dy: pulled[a, p + dp, tall(t, dy), :]
    two = lambda a, dp, dy: pulled_doubled[a, p + dp, tall(t, dy), :]
    along_x = two(0, 1, 0) - two(0, -1, 0) + (at(0, 1, 1) + at(0, 1, -1)) - (at(0, -1, 1) + at(0, -1, -1))
    along_y = two(1, 0, 1) - two(1, 0, -1) + (at(1, 1, 1) + at(1, -1, 1)) - (at(1, 1, -1) + at(1, -1, -1))
    star = 2.0 * at(2, 0, 0) + at(2, 1, 0) + at(2, -1, 0) + at(2, 0, 1) + at(2, 0, -1)
    along_z = rolled(star, -1) - rolled(star, 1)
    return (along_x + along_y + along_z) * (-1.0 / 36.0)


def put_pulled(pulled, pulled_doubled, p, t, psi, q):
    for a in range(3):
        s = (COUPLING / SHEAR) * psi * q[a]
        pulled[a, p, tall(t), :] = s
        if a < 2:
            pulled_doubled[a, p, tall(t), :] = with_sides(s)


def mask_ahead(masks, i, p, t):
    cx, cy, cz = VECTORS[i]
    return masks[(-cz) % 3, p + cx, tall(t, cy), :] > 0


def last_reverse_kernel(
    misfit, from_left, from_right, masks, field, speed, pull, early_speed,
    adjoint, turned, wall_out, send_left, send_right,
    ahead, pulled, pulled_doubled, base,
):
    def place(t):
        for p in range(6):
            if p < 2:
                d = from_left[p, flat(t), :]
            elif p < 4:
                d = misfit[p - 2, flat(t), :]
            else:
                d = from_right[p - 4, flat(t), :]
            ahead[0, p, tall(t), :] = d
            ahead[1, p, tall(t), :] = rolled(d, 1)
            ahead[2, p, tall(t), :] = rolled(d, -1)

    each_chunk(place)

    def collide(t):
        for p in range(1, 5):
            s = masks[0, p, tall(t), :]
            here = ahead[0, p, tall(t), :]
            r = {0: here}
            for i in range(1, 19):
                cx, cy, cz = VECTORS[i]
                there = ahead[(-cz) % 3, p + cx, tall(t, cy), :]
                r[i] = s * jnp.where(mask_ahead(masks, i, p, t), there, here)
            psi = field[p, tall(t), :]
            u = [speed[a, p - 1, flat(t), :] for a in range(3)]
            if p in (2, 3):
                rest, by_density, q = collide_adjoint(r, u)
                along = add(*[q[a] * pull[a, p - 2, flat(t), :] for a in range(3)])
                const = by_density + along * ((PULL / SHEAR) * (1.0 - psi))
                for i in range(19):
                    base[i, p - 2, flat(t), :] = rest[i] + const
            else:
                q = flow_adjoint(*dual(r), u)
            put_pulled(pulled, pulled_doubled, p - 1, t, psi, q)

    each_chunk(collide)

    def finish(t):
        for x in range(2):
            s = masks[0, 2 + x, tall(t), :]
            spread = spread_of(pulled, pulled_doubled, 1 + x, t)
            wall_out[x, flat(t), :] = (1.0 - s) * spread
            more = s * spread * (1.0 - field[2 + x, tall(t), :])
            for i in range(19):
                value = base[i, x, flat(t), :] + more
                adjoint[i, x, tall(t), :] = value
                if i in TURNED:
                    turned[TURNED.index(i), x, tall(t), :] = rolled(value, -VECTORS[i][2])

    each_chunk(finish)

    def part(t):
        for x, send, sent, skipped in ((0, send_left, RIGHTWARD, -1), (1, send_right, LEFTWARD, 1)):
            p = 2 + x
            s = masks[0, p, tall(t), :]
            r = {}
            for i in range(19):
                cx, cy, cz = VECTORS[i]
                if cx == skipped:
                    continue
                r[i] = adjoint_ahead(adjoint, turned, masks, i, x, t)
            u = [early_speed[a, p - 1, flat(t), :] for a in range(3)]
            q = flow_adjoint(*dual(r), u)
            for a in range(3):
                send[5 + a, flat(t), :] = s * q[a]
            for k, i in enumerate(sent):
                send[k, flat(t), :] = adjoint[i, x, tall(t), :]

    each_chunk(part)


def adjoint_ahead(adjoint, turned, masks, i, x, t):
    cx, cy, cz = VECTORS[i]
    if i == 0:
        return adjoint[0, x, tall(t), :]
    if cz:
        there = turned[TURNED.index(i), x + cx, tall(t, cy), :]
    else:
        there = adjoint[i, x + cx, tall(t, cy), :]
    return jnp.where(mask_ahead(masks, i, 2 + x, t), there, adjoint[OPPOSITE[i], x, tall(t), :])


def first_reverse_kernel(
    adjoint, turned, wall, from_left, from_right, masks, field, speed, pull, chooser,
    grad, label_part,
    come, pulled, pulled_doubled, base,
):
    sides = ((0, from_left, LEFTWARD), (1, from_right, RIGHTWARD))

    def place(t):
        for side, source, which in sides:
            for k, i in enumerate(which):
                come[side, k, tall(t), :] = rolled(source[k, flat(t), :], -VECTORS[i][2])

    each_chunk(place)

    def collide(t):
        for x in range(2):
            p = 2 + x
            s = masks[0, p, tall(t), :]
            r = {}
            for i in range(19):
                cx, cy, cz = VECTORS[i]
                if (x, cx) in ((0, -1), (1, 1)):
                    side = x
                    there = come[side, sides[side][2].index(i), tall(t, cy), :]
                    value = jnp.where(
                        mask_ahead(masks, i, p, t), there, adjoint[OPPOSITE[i], x, tall(t), :]
                    )
                else:
                    value = adjoint_ahead(adjoint, turned, masks, i, x, t)
                r[i] = s * value
            psi = field[p, tall(t), :]
            u = [speed[a, p - 1, flat(t), :] for a in range(3)]
            rest, by_density, q = collide_adjoint(r, u)
            along = add(*[q[a] * pull[a, x, flat(t), :] for a in range(3)])
            const = by_density + along * ((PULL / SHEAR) * (1.0 - psi))
            for i in range(19):
                base[i, x, flat(t), :] = rest[i] + const
            put_pulled(pulled, pulled_doubled, p - 1, t, psi, q)
        for side, source, which in sides:
            p = 1 if side == 0 else 4
            x = 0 if side == 0 else 1
            s = masks[0, p, tall(t), :]
            r = {}
            for i in [OPPOSITE[j] for j in which]:
                cx, cy, cz = VECTORS[i]
                if cz:
                    there = turned[TURNED.index(i), x, tall(t, cy), :]
                else:
                    there = adjoint[i, x, tall(t, cy), :]
                here = source[which.index(OPPOSITE[i]), flat(t), :]
                r[i] = jnp.where(mask_ahead(masks, i, p, t), there, here)
            u = [speed[a, p - 1, flat(t), :] for a in range(3)]
            more = flow_adjoint(*dual(r), u)
            q = [source[5 + a, flat(t), :] + s * more[a] for a in range(3)]
            put_pulled(pulled, pulled_doubled, p - 1, t, field[p, tall(t), :], q)

    each_chunk(collide)

    def finish(t):
        total = None
        for x in range(2):
            s = masks[0, 2 + x, tall(t), :]
            spread = spread_of(pulled, pulled_doubled, 1 + x, t)
            total = add(total, (1.0 - s) * spread + wall[x, flat(t), :])
            more = s * spread * (1.0 - field[2 + x, tall(t), :])
            for i in range(19):
                grad[i, x, rows_at(t, 0, -HALO), :] = base[i, x, flat(t), :] + more
        base[0, 0, flat(t), :] = total

    each_chunk(finish, HALO // 8, (HALO + OWN) // 8)

    totals = base[0, 0, HALO : HALO + OWN, :]
    blocks = (OWN // 2) * (DEPTH // 4)
    column = lax.broadcasted_iota(jnp.int32, (DEPTH, blocks), 1)
    quad = lax.broadcasted_iota(jnp.int32, (DEPTH, blocks), 0) // 4
    gather = (jnp.bitwise_and(column, DEPTH // 4 - 1) == quad).astype(jnp.bfloat16)
    by_block = exact_dot(totals, gather)
    pair = lax.broadcasted_iota(jnp.int32, (OWN, blocks), 0) // 2
    wanted = lax.broadcasted_iota(jnp.int32, (OWN, blocks), 1) // (DEPTH // 4)
    by_block = jnp.where(pair == wanted, by_block, 0.0)
    by_label = exact_dot(by_block, chooser[...])
    label_part[...] = jnp.sum(by_label, axis=0, keepdims=True)


def exact_dot(values, zero_one):
    high = values.astype(jnp.bfloat16)
    left = values - high.astype(jnp.float32)
    middle = left.astype(jnp.bfloat16)
    low = (left - middle.astype(jnp.float32)).astype(jnp.bfloat16)
    dot = lambda part: jnp.dot(part, zero_one, preferred_element_type=jnp.float32)
    return dot(high) + (dot(middle) + dot(low))


def call(kernel, args, outs, scratch):
    whole = pl.BlockSpec(memory_space=pltpu.VMEM)
    return pl.pallas_call(
        kernel,
        out_shape=[jax.ShapeDtypeStruct(s, jnp.float32) for s in outs],
        in_specs=[whole] * len(args),
        out_specs=[whole] * len(outs),
        scratch_shapes=[pltpu.VMEM(s, d) for s, d in scratch],
        compiler_params=pltpu.CompilerParams(vmem_limit_bytes=40 * 1024 * 1024),
    )(*args)


def ring(axis):
    count = lax.axis_size(axis)
    up = [(i, (i + 1) % count) for i in range(count)]
    return up, [(j, i) for i, j in up]


def both_ways(to_lower, to_upper, axis):
    up, down = ring(axis)
    from_lower = lax.ppermute(to_upper, axis, up)
    from_upper = lax.ppermute(to_lower, axis, down)
    return from_lower, from_upper


def per_device(populations, fluid, label, wall_wetting, target):
    f32 = jnp.float32
    plane = (ROWS, DEPTH)
    two = (2, *plane)
    edge = (22, 2, HALO, DEPTH)
    low, high = call(edges_kernel, (populations, fluid, label, target), (edge, edge), ())
    below, above = both_ways(low, high, "gy")
    marks = jnp.bitwise_and(label[0, ::2, ::4], LABELS - 1).reshape(-1)
    chooser = (marks[:, None] == jnp.arange(LABELS, dtype=jnp.int32)[None, :]).astype(jnp.bfloat16)
    lin, flow, density, effective, share, target_wide, to_left, to_right = call(
        start_kernel,
        (populations, fluid, label, target, wall_wetting.reshape(2, DEPTH), below, above),
        ((19, *two), (3, *two), two, two, two, two, (12, *plane), (12, *plane)),
        (((19, *two), f32), (two, jnp.int32)),
    )
    from_left, from_right = both_ways(to_left, to_right, "gx")
    wide6 = (6, TALL, DEPTH)
    work = ((wide6, f32), ((19, 4, TALL, DEPTH), f32), ((10, 4, TALL, DEPTH), f32))
    masks, field0, speed0, pull0, lin, flow, density, effective, to_left, to_right = call(
        functools.partial(step_kernel, True),
        (lin, flow, density, effective, share, from_left, from_right),
        (
            (3, *wide6), wide6, (3, 4, *plane), (3, *two),
            (19, *two), (3, *two), two, two, (10, *plane), (10, *plane),
        ),
        work,
    )
    from_left, from_right = both_ways(to_left, to_right, "gx")
    field1, speed1, pull1, misfit = call(
        functools.partial(step_kernel, False),
        (lin, flow, density, effective, share, target_wide, masks, from_left, from_right),
        (wide6, (3, 4, *plane), (3, *two), two),
        work,
    )
    from_left, from_right = both_ways(misfit, misfit, "gx")
    pulled = (((3, 4, TALL, DEPTH), f32), ((2, 4, TALL, DEPTH), f32), ((19, *two), f32))
    adjoint, turned, wall, to_left, to_right = call(
        last_reverse_kernel,
        (misfit, from_left, from_right, masks, field1, speed1, pull1, speed0),
        ((19, 2, TALL, DEPTH), (10, 2, TALL, DEPTH), two, (8, *plane), (8, *plane)),
        (((3, *wide6), f32), *pulled),
    )
    from_left, from_right = both_ways(to_left, to_right, "gx")
    grad, label_part = call(
        first_reverse_kernel,
        (adjoint, turned, wall, from_left, from_right, masks, field0, speed0, pull0, chooser),
        (populations.shape, (1, LABELS)),
        (((2, 5, TALL, DEPTH), f32), *pulled),
    )
    count = lax.axis_size("gy")
    wetting_grad = label_part
    for step in range(1, count):
        wetting_grad = wetting_grad + lax.ppermute(
            label_part, "gy", [(i, (i + step) % count) for i in range(count)]
        )
    return (grad, wetting_grad.reshape(-1))


def solution(mesh):
    return jax.shard_map(
        per_device,
        mesh=mesh,
        in_specs=(
            P(None, "gx", "gy", None),
            P("gx", "gy", None),
            P("gx", "gy", None),
            P("gx"),
            P("gx", "gy", None),
        ),
        out_specs=(P(None, "gx", "gy", None), P("gx")),
        check_vma=False,
    )
```

profile of v0, /device:TPU:1, one launch (start us, length us, event | category | flops | bytes accessed | tf_op | source)
XLA Modules:
  0.0 84.4 jit_solution(13679904556934647440)
XLA Ops:
  0.6 0.0 copy-start
  0.6 1.1 %copy-done = f32[19,2,32,128]{3,2,1,0:T(8,128)S(1)} copy-done((f32[19,2,32,128]{3,2,1,0:T(8,128)S(1)}, f32[19,2,32,128]{3,2,1,0:T(8,128)}, u32[]{:S(2)}) %copy-start) | copy-done | bytes 622616
  1.7 0.8 copy-done.1
  2.5 0.8 copy-done.2
  3.2 0.8 copy-done.3
  4.0 4.4 %collective-permute-start = (f32[22,2,8,128]{3,2,1,0:T(8,128)S(1)}, f32[22,2,8,128]{3,2,1,0:T(8,128)S(1)}, u32[]{:S(2)}, u32[]{:S(2)}) collective-permute-start(f32[22,2,8,128]{3,2,1,0:T(8,128)S(1)} %get-tuple-element.33), channel_id=1, source_target_pairs={{0,1},{1,2},{2,3},{3,0},{4,5},{5,6},{6,7},{7,4},{8,9},{9,10},{10,1... | collective-permute-start | bytes 540680 | tf_op jit(solution)/shard_map/ppermute | solution.py:686
  8.4 0.0 collective-permute-start.1
  8.4 2.4 %collective-permute-done.below = f32[22,2,8,128]{3,2,1,0:T(8,128)S(1)} collective-permute-done((f32[22,2,8,128]{3,2,1,0:T(8,128)S(1)}, f32[22,2,8,128]{3,2,1,0:T(8,128)S(1)}, u32[]{:S(2)}, u32[]{:S(2)}) %collective-permute-start) | collective-permute-done | bytes 180256 | tf_op jit(solution)/shard_map/ppermute | solution.py:686
  10.8 4.2 %collective-permute-done.1.above = f32[22,2,8,128]{3,2,1,0:T(8,128)S(1)} collective-permute-done((f32[22,2,8,128]{3,2,1,0:T(8,128)S(1)}, f32[22,2,8,128]{3,2,1,0:T(8,128)S(1)}, u32[]{:S(2)}, u32[]{:S(2)}) %collective-permute-start.1) | collective-permute-done | bytes 180256 | tf_op jit(solution)/shard_map/ppermute | solution.py:687
  15.0 0.7 copy-done.10
  15.7 0.6 shard_map.69
  16.2 0.0 copy-start.4
  16.2 1.1 %collective-permute-start.2 = (f32[12,48,128]{2,1,0:T(8,128)S(1)}, f32[12,48,128]{2,1,0:T(8,128)S(1)}, u32[]{:S(2)}, u32[]{:S(2)}) collective-permute-start(f32[12,48,128]{2,1,0:T(8,128)S(1)} %get-tuple-element.40), channel_id=1, source_target_pairs={{0,4},{4,8},{8,12},{12,16},{16,20},{20,24},{24,28},{28,32},{32,36}... | collective-permute-start | bytes 884744 | tf_op jit(solution)/shard_map/ppermute | solution.py:686
  17.4 6.8 %collective-permute-start.3 = (f32[12,48,128]{2,1,0:T(8,128)S(1)}, f32[12,48,128]{2,1,0:T(8,128)S(1)}, u32[]{:S(2)}, u32[]{:S(2)}) collective-permute-start(f32[12,48,128]{2,1,0:T(8,128)S(1)} %get-tuple-element.41), channel_id=1, source_target_pairs={{4,0},{8,4},{12,8},{16,12},{20,16},{24,20},{28,24},{32,28},{36,32}... | collective-permute-start | bytes 884744 | tf_op jit(solution)/shard_map/ppermute | solution.py:687
  24.1 5.7 %collective-permute-done.2.refs_5_ = f32[12,48,128]{2,1,0:T(8,128)S(1)} collective-permute-done((f32[12,48,128]{2,1,0:T(8,128)S(1)}, f32[12,48,128]{2,1,0:T(8,128)S(1)}, u32[]{:S(2)}, u32[]{:S(2)}) %collective-permute-start.2) | collective-permute-done | bytes 294944 | tf_op jit(solution)/shard_map/ppermute | solution.py:686
  29.8 0.0 collective-permute-done.3.refs_6_
  29.8 3.1 %shard_map.70 = (f32[3,6,64,128]{3,2,1,0:T(8,128)S(1)}, f32[6,64,128]{2,1,0:T(8,128)S(1)}, f32[3,4,48,128]{3,2,1,0:T(8,128)S(1)}, f32[3,2,48,128]{3,2,1,0:T(8,12...) custom-call(f32[19,2,48,128]{3,2,1,0:T(8,128)S(1)} %get-tuple-elemen, ...), custom_call_target="tpu_custom_call" | custom-call | tf_op jit(solution)/shard_map/pallas_call | solution.py:668
  33.0 0.6 copy-done.6
  33.6 0.6 copy-done.8
  34.2 0.0 collective-permute-start.4
  34.2 0.0 copy-done.4
  34.2 6.0 %collective-permute-start.5 = (f32[10,48,128]{2,1,0:T(8,128)S(1)}, f32[10,48,128]{2,1,0:T(8,128)S(1)}, u32[]{:S(2)}, u32[]{:S(2)}) collective-permute-start(f32[10,48,128]{2,1,0:T(8,128)S(1)} %get-tuple-element.49), channel_id=1, source_target_pairs={{4,0},{8,4},{12,8},{16,12},{20,16},{24,20},{28,24},{32,28},{36,32}... | collective-permute-start | bytes 737288 | tf_op jit(solution)/shard_map/ppermute | solution.py:687
  40.2 0.8 slice.3
  41.1 5.2 %collective-permute-done.4.refs_7_ = f32[10,48,128]{2,1,0:T(8,128)S(1)} collective-permute-done((f32[10,48,128]{2,1,0:T(8,128)}, f32[10,48,128]{2,1,0:T(8,128)S(1)}, u32[]{:S(2)}, u32[]{:S(2)}) %collective-permute-start.4) | collective-permute-done | bytes 245792 | tf_op jit(solution)/shard_map/ppermute | solution.py:686
  46.3 0.0 collective-permute-done.5.refs_8_
  46.3 0.8 copy-done.5
  47.1 0.8 copy-done.7
  47.9 0.8 copy-done.9
  48.7 2.1 %shard_map.71 = (f32[6,64,128]{2,1,0:T(8,128)S(1)}, f32[3,4,48,128]{3,2,1,0:T(8,128)S(1)}, f32[3,2,48,128]{3,2,1,0:T(8,128)S(1)}, f32[2,48,128]{2,1,0:T(8,128)S(1)}) custom-call(f32[19,2,48,128]{3,2,1,0:T(8,128)S(1)} %get-tuple-element.42.refs_0_, f32[3,2,48,128]{3,2,1,0:T(8,128)S(1)} %get-tuple-element.43.refs_1_, f32[2,48,128]{2,1,0:T(8,128)S(1)} %copy-done.7, ...), custom_call_target="tpu_custom_call" | custom-call | tf_op jit(solution)/shard_map/pallas_call | solution.py:668
  50.8 0.1 collective-permute-start.6
  50.9 6.0 %collective-permute-start.7 = (f32[2,48,128]{2,1,0:T(8,128)S(1)}, f32[2,48,128]{2,1,0:T(8,128)S(1)}, u32[]{:S(2)}, u32[]{:S(2)}) collective-permute-start(f32[2,48,128]{2,1,0:T(8,128)S(1)} %get-tuple-element.50.misfit), channel_id=1, source_target_pairs={{4,0},{8,4},{12,8},{16,12},{20,16},{24,20},{28,24},{32,28},{36,32}... | collective-permute-start | bytes 147464 | tf_op jit(solution)/shard_map/ppermute | solution.py:687
  56.9 0.1 and.15
  57.0 1.3 %collective-permute-done.6.from_left = f32[2,48,128]{2,1,0:T(8,128)S(1)} collective-permute-done((f32[2,48,128]{2,1,0:T(8,128)S(1)}, f32[2,48,128]{2,1,0:T(8,128)S(1)}, u32[]{:S(2)}, u32[]{:S(2)}) %collective-permute-start.6) | collective-permute-done | bytes 49184 | tf_op jit(solution)/shard_map/ppermute | solution.py:686
  58.3 0.0 collective-permute-done.7.from_right
  58.3 3.4 %shard_map.72 = (f32[19,2,64,128]{3,2,1,0:T(8,128)S(1)}, f32[10,2,64,128]{3,2,1,0:T(8,128)S(1)}, f32[2,48,128]{2,1,0:T(8,128)S(1)}, f32[8,48,128]{2,1,0:T(8,128)S(1)}, f32[8,48,128]{2,1,0:T(8,128)S(1)}) custom-call(f32[2,48,128]{2,1,0:T(8,128)S(1)} %get-tuple-element.50.misfit, f32[2,48,128]{2,1,0:T(8,128)S(1)} %collective-permute-done.6.from_left, ...), custom_call_target="tpu_custom_call" | custom-call | tf_op jit(solution)/shard_map/pallas_call | solution.py:668
  61.8 0.1 collective-permute-start.8
  61.9 5.8 %collective-permute-start.9 = (f32[8,48,128]{2,1,0:T(8,128)S(1)}, f32[8,48,128]{2,1,0:T(8,128)S(1)}, u32[]{:S(2)}, u32[]{:S(2)}) collective-permute-start(f32[8,48,128]{2,1,0:T(8,128)S(1)} %get-tuple-element.59), channel_id=1, source_target_pairs={{4,0},{8,4},{12,8},{16,12},{20,16},{24,20},{28,24},{32,28},{36,32}... | collective-permute-start | bytes 589832 | tf_op jit(solution)/shard_map/ppermute | solution.py:687
  67.7 0.1 fusion.chooser
  67.9 3.4 %collective-permute-done.8.from_left = f32[8,48,128]{2,1,0:T(8,128)S(1)} collective-permute-done((f32[8,48,128]{2,1,0:T(8,128)S(1)}, f32[8,48,128]{2,1,0:T(8,128)S(1)}, u32[]{:S(2)}, u32[]{:S(2)}) %collective-permute-start.8) | collective-permute-done | bytes 196640 | tf_op jit(solution)/shard_map/ppermute | solution.py:686
  71.3 0.0 collective-permute-done.9.from_right
  71.3 3.0 %shard_map.73 = (f32[19,2,32,128]{3,2,1,0:T(8,128)}, f32[1,256]{1,0:T(1,128)S(1)}) custom-call(f32[19,2,64,128]{3,2,1,0:T(8,128)S(1)} %get-tuple-element.55.adjoint, f32[10,2,64,128]{3,2,1,0:T(8,128)S(1)} %get-tuple-element.56.turned, f32[2,48,128]{2,1,0:T(8,128)S(1)} %get-tuple-element.57.wall, f32[8,48,128]{2,1,0:T(8,128)S(1)} %collective-permute-done.8.from_left, ...), custom_call_target="tpu_custom_call" | custom-call | tf_op jit(solution)/shard_map/pallas_call | solution.py:668
  74.3 5.0 %collective-permute-start.10 = (f32[1,256]{1,0:T(1,128)S(1)}, f32[1,256]{1,0:T(1,128)S(1)}, u32[]{:S(2)}, u32[]{:S(2)}) collective-permute-start(f32[1,256]{1,0:T(1,128)S(1)} %get-tuple-element.63), channel_id=1, source_target_pairs={{0,1},{1,2},{2,3},{3,0},{4,5},{5,6},{6,7},{7,4},{8,9},{9,10},{10,1... | collective-permute-start | bytes 3080 | tf_op jit(solution)/shard_map/ppermute | solution.py:743
  79.2 0.1 collective-permute-start.11
  79.3 0.4 collective-permute-start.12
  79.7 0.3 collective-permute-done.10
  80.0 3.2 %collective-permute-done.11 = f32[1,256]{1,0:T(1,128)S(1)} collective-permute-done((f32[1,256]{1,0:T(1,128)S(1)}, f32[1,256]{1,0:T(1,128)S(1)}, u32[]{:S(2)}, u32[]{:S(2)}) %collective-permute-start.11) | collective-permute-done | bytes 1056 | tf_op jit(solution)/shard_map/ppermute | solution.py:743
  83.2 0.6 collective-permute-done.12
  83.8 0.6 add_add_fusion
  (11 shorter events, 0.0 us)
Async XLA Ops:
  0.6 1.1 %copy-start = (f32[19,2,32,128]{3,2,1,0:T(8,128)S(1)}, f32[19,2,32,128]{3,2,1,0:T(8,128)}, u32[]{:S(2)}) copy-start(f32[19,2,32,128]{3,2,1,0:T(8,128)} %pops.3) | copy-start | bytes 1867780
  1.7 0.8 copy-start.1
  2.5 0.8 copy-start.2
  3.2 0.8 copy-start.3
  4.0 6.8 %collective-permute-start = (f32[22,2,8,128]{3,2,1,0:T(8,128)S(1)}, f32[22,2,8,128]{3,2,1,0:T(8,128)S(1)}, u32[]{:S(2)}, u32[]{:S(2)}) collective-permute-start(f32[22,2,8,128]{3,2,1,0:T(8,128)S(1)} %get-tuple-element.33), channel_id=1, source_target_pairs={{0,1},{1,2},{2,3},{3,0},{4,5},{5,6},{6,7},{7,4},{8,9},{9,10},{10,1... | collective-permute-start | bytes 540680 | tf_op jit(solution)/shard_map/ppermute | solution.py:686
  8.4 6.6 %collective-permute-start.1 = (f32[22,2,8,128]{3,2,1,0:T(8,128)S(1)}, f32[22,2,8,128]{3,2,1,0:T(8,128)S(1)}, u32[]{:S(2)}, u32[]{:S(2)}) collective-permute-start(f32[22,2,8,128]{3,2,1,0:T(8,128)S(1)} %get-tuple-element.34), channel_id=1, source_target_pairs={{1,0},{2,1},{3,2},{0,3},{5,4},{6,5},{7,6},{4,7},{9,8},{10,9},{11,1... | collective-permute-start | bytes 540680 | tf_op jit(solution)/shard_map/ppermute | solution.py:687
  15.0 0.7 copy-start.10
  16.2 18.0 %copy-start.4 = (f32[2,48,128]{2,1,0:T(8,128)}, f32[2,48,128]{2,1,0:T(8,128)S(1)}, u32[]{:S(2)}) copy-start(f32[2,48,128]{2,1,0:T(8,128)S(1)} %get-tuple-element.46.refs_5_) | copy-start | bytes 147460
  16.2 13.6 %collective-permute-start.2 = (f32[12,48,128]{2,1,0:T(8,128)S(1)}, f32[12,48,128]{2,1,0:T(8,128)S(1)}, u32[]{:S(2)}, u32[]{:S(2)}) collective-permute-start(f32[12,48,128]{2,1,0:T(8,128)S(1)} %get-tuple-element.40), channel_id=1, source_target_pairs={{0,4},{4,8},{8,12},{12,16},{16,20},{20,24},{24,28},{28,32},{32,36}... | collective-permute-start | bytes 884744 | tf_op jit(solution)/shard_map/ppermute | solution.py:686
  17.4 12.5 %collective-permute-start.3 = (f32[12,48,128]{2,1,0:T(8,128)S(1)}, f32[12,48,128]{2,1,0:T(8,128)S(1)}, u32[]{:S(2)}, u32[]{:S(2)}) collective-permute-start(f32[12,48,128]{2,1,0:T(8,128)S(1)} %get-tuple-element.41), channel_id=1, source_target_pairs={{4,0},{8,4},{12,8},{16,12},{20,16},{24,20},{28,24},{32,28},{36,32}... | collective-permute-start | bytes 884744 | tf_op jit(solution)/shard_map/ppermute | solution.py:687
  33.0 0.6 copy-start.6
  33.6 0.6 copy-start.8
  34.2 12.1 %collective-permute-start.4 = (f32[10,48,128]{2,1,0:T(8,128)}, f32[10,48,128]{2,1,0:T(8,128)S(1)}, u32[]{:S(2)}, u32[]{:S(2)}) collective-permute-start(f32[10,48,128]{2,1,0:T(8,128)} %get-tuple-element.48), channel_id=1, source_target_pairs={{0,4},{4,8},{8,12},{12,16},{16,20},{20,24},{24,28},{28,32},{32,36}... | collective-permute-start | bytes 737288 | tf_op jit(solution)/shard_map/ppermute | solution.py:686
  34.2 12.1 %collective-permute-start.5 = (f32[10,48,128]{2,1,0:T(8,128)S(1)}, f32[10,48,128]{2,1,0:T(8,128)S(1)}, u32[]{:S(2)}, u32[]{:S(2)}) collective-permute-start(f32[10,48,128]{2,1,0:T(8,128)S(1)} %get-tuple-element.49), channel_id=1, source_target_pairs={{4,0},{8,4},{12,8},{16,12},{20,16},{24,20},{28,24},{32,28},{36,32}... | collective-permute-start | bytes 737288 | tf_op jit(solution)/shard_map/ppermute | solution.py:687
  46.3 0.8 copy-start.5
  47.1 0.8 copy-start.7
  47.9 0.8 copy-start.9
  50.8 7.5 %collective-permute-start.6 = (f32[2,48,128]{2,1,0:T(8,128)S(1)}, f32[2,48,128]{2,1,0:T(8,128)S(1)}, u32[]{:S(2)}, u32[]{:S(2)}) collective-permute-start(f32[2,48,128]{2,1,0:T(8,128)S(1)} %get-tuple-element.50.misfit), channel_id=1, source_target_pairs={{0,4},{4,8},{8,12},{12,16},{16,20},{20,24},{24,28},{28,32},{32,36}... | collective-permute-start | bytes 147464 | tf_op jit(solution)/shard_map/ppermute | solution.py:686
  50.9 7.4 %collective-permute-start.7 = (f32[2,48,128]{2,1,0:T(8,128)S(1)}, f32[2,48,128]{2,1,0:T(8,128)S(1)}, u32[]{:S(2)}, u32[]{:S(2)}) collective-permute-start(f32[2,48,128]{2,1,0:T(8,128)S(1)} %get-tuple-element.50.misfit), channel_id=1, source_target_pairs={{4,0},{8,4},{12,8},{16,12},{20,16},{24,20},{28,24},{32,28},{36,32}... | collective-permute-start | bytes 147464 | tf_op jit(solution)/shard_map/ppermute | solution.py:687
  61.8 9.5 %collective-permute-start.8 = (f32[8,48,128]{2,1,0:T(8,128)S(1)}, f32[8,48,128]{2,1,0:T(8,128)S(1)}, u32[]{:S(2)}, u32[]{:S(2)}) collective-permute-start(f32[8,48,128]{2,1,0:T(8,128)S(1)} %get-tuple-element.58), channel_id=1, source_target_pairs={{0,4},{4,8},{8,12},{12,16},{16,20},{20,24},{24,28},{28,32},{32,36}... | collective-permute-start | bytes 589832 | tf_op jit(solution)/shard_map/ppermute | solution.py:686
  61.9 9.4 %collective-permute-start.9 = (f32[8,48,128]{2,1,0:T(8,128)S(1)}, f32[8,48,128]{2,1,0:T(8,128)S(1)}, u32[]{:S(2)}, u32[]{:S(2)}) collective-permute-start(f32[8,48,128]{2,1,0:T(8,128)S(1)} %get-tuple-element.59), channel_id=1, source_target_pairs={{4,0},{8,4},{12,8},{16,12},{20,16},{24,20},{28,24},{32,28},{36,32}... | collective-permute-start | bytes 589832 | tf_op jit(solution)/shard_map/ppermute | solution.py:687
  74.3 5.7 %collective-permute-start.10 = (f32[1,256]{1,0:T(1,128)S(1)}, f32[1,256]{1,0:T(1,128)S(1)}, u32[]{:S(2)}, u32[]{:S(2)}) collective-permute-start(f32[1,256]{1,0:T(1,128)S(1)} %get-tuple-element.63), channel_id=1, source_target_pairs={{0,1},{1,2},{2,3},{3,0},{4,5},{5,6},{6,7},{7,4},{8,9},{9,10},{10,1... | collective-permute-start | bytes 3080 | tf_op jit(solution)/shard_map/ppermute | solution.py:743
  79.2 3.9 %collective-permute-start.11 = (f32[1,256]{1,0:T(1,128)S(1)}, f32[1,256]{1,0:T(1,128)S(1)}, u32[]{:S(2)}, u32[]{:S(2)}) collective-permute-start(f32[1,256]{1,0:T(1,128)S(1)} %get-tuple-element.63), channel_id=1, source_target_pairs={{0,2},{1,3},{2,0},{3,1},{4,6},{5,7},{6,4},{7,5},{8,10},{9,11},{10,... | collective-permute-start | bytes 3080 | tf_op jit(solution)/shard_map/ppermute | solution.py:743
  79.3 4.5 %collective-permute-start.12 = (f32[1,256]{1,0:T(1,128)S(1)}, f32[1,256]{1,0:T(1,128)S(1)}, u32[]{:S(2)}, u32[]{:S(2)}) collective-permute-start(f32[1,256]{1,0:T(1,128)S(1)} %get-tuple-element.63), channel_id=1, source_target_pairs={{0,3},{1,0},{2,1},{3,2},{4,7},{5,4},{6,5},{7,6},{8,11},{9,8},{10,9... | collective-permute-start | bytes 3080 | tf_op jit(solution)/shard_map/ppermute | solution.py:743
where the time goes:
time: 85 us; the launch traced here: 84.4 us
  starting transfers between devices  35.7 us (42%)
  waiting for transfers between devices  26.4 us (31%)
  Pallas kernels  12.2 us (14%)
  local copies, waits for them, and re-layouts  8.57 us (10%)
    ppermute x5, starting transfers between devices, both_ways(): from_upper = lax.ppermute(to_lower, axis, down)  24.7 us
    ppermute x5, waiting for transfers between devices, both_ways(): from_lower = lax.ppermute(to_upper, axis, up)  18.1 us
    pallas_call x6, Pallas kernels, call(): pl.pallas_call(kernel, out_shape=[jax.ShapeDtypeStruct(s, jnp.float32) fo...  12.2 us
    unnamed x22, local copies, waits for them, and re-layouts  7.65 us
    ppermute x5, starting transfers between devices, both_ways(): from_lower = lax.ppermute(to_upper, axis, up)  5.66 us
    ppermute x3, starting transfers between devices, per_device(): lax.ppermute(label_part, 'gy', [(i, (i + step) % count) for i in range(co...  5.4 us
    ppermute x5, waiting for transfers between devices, both_ways(): from_upper = lax.ppermute(to_lower, axis, down)  4.17 us
    ppermute x3, waiting for transfers between devices, per_device(): lax.ppermute(label_part, 'gy', [(i, (i + step) % count) for i in range(co...  4.14 us
  transfers between devices with their start and end apart: 13, of which 9 were waited for; matrix products, arithmetic and copies ran while one was open for 1% of the time, Pallas kernels for 0%

commit v1 on v0

--- a/solution.py
+++ b/solution.py
@@ -2,6 +2,7 @@
 
 import jax
 import jax.numpy as jnp
+import numpy as np
 from jax import lax
 from jax.experimental import pallas as pl
 from jax.experimental.pallas import tpu as pltpu
@@ -242,6 +243,8 @@
 
 
 def rows_at(t, shift, offset):
+    if isinstance(t, int):
+        return pl.ds(t * 8 + offset + shift, 8)
     if shift == 0:
         return pl.ds(pl.multiple_of(t * 8 + offset, 8), 8)
     return pl.ds(t * 8 + (offset + shift), 8)
@@ -276,15 +279,25 @@
     return 2.0 * x + rolled(x, 1) + rolled(x, -1)
 
 
-def edges_kernel(pops, fluid, label, target, low, high):
-    low[0:19] = pops[:, :, 0:HALO, :]
-    high[0:19] = pops[:, :, OWN - HALO : OWN, :]
-    low[19] = fluid[:, 0:HALO, :].astype(jnp.float32)
-    high[19] = fluid[:, OWN - HALO : OWN, :].astype(jnp.float32)
-    low[20] = label[:, 0:HALO, :].astype(jnp.float32)
-    high[20] = label[:, OWN - HALO : OWN, :].astype(jnp.float32)
-    low[21] = target[:, 0:HALO, :]
-    high[21] = target[:, OWN - HALO : OWN, :]
+def edges_kernel(pops, fluid, label, target, low, high, whole, sems):
+    copies = []
+
+    def copy(source, goal):
+        one = pltpu.make_async_copy(source, goal, sems.at[len(copies)])
+        one.start()
+        copies.append(one)
+
+    for side, goal in ((0, low), (1, high)):
+        rows = pl.ds(0, HALO) if side == 0 else pl.ds(OWN - HALO, HALO)
+        copy(fluid.at[:, rows, :], whole.at[side, 0])
+        copy(label.at[:, rows, :], whole.at[side, 1])
+        copy(target.at[:, rows, :], goal.at[21])
+        copy(pops.at[:, :, rows, :], goal.at[pl.ds(0, 19)])
+    for one in copies:
+        one.wait()
+    for side, goal in ((0, low), (1, high)):
+        goal[19] = whole[side, 0].astype(jnp.float32)
+        goal[20] = whole[side, 1].astype(jnp.float32)
 
 
 def put_sends(send_left, send_right, t, lin, first, chosen, effective):
@@ -301,57 +314,68 @@
     send_right[9, flat(t), :] = effective[0]
 
 
-def start_kernel(
-    pops, fluid, label, target, wetting, below, above,
-    lin_out, flow_out, density_out, effective_out, share_out, target_out, send_left, send_right,
-    wide, label_wide,
-):
-    wide[:, :, HALO : HALO + OWN, :] = pops[...]
-    wide[:, :, 0:HALO, :] = below[0:19]
-    wide[:, :, HALO + OWN : ROWS, :] = above[0:19]
-    share_out[:, HALO : HALO + OWN, :] = fluid[...].astype(jnp.float32)
-    share_out[:, 0:HALO, :] = below[19]
-    share_out[:, HALO + OWN : ROWS, :] = above[19]
-    label_wide[:, HALO : HALO + OWN, :] = label[...]
-    label_wide[:, 0:HALO, :] = below[20].astype(jnp.int32)
-    label_wide[:, HALO + OWN : ROWS, :] = above[20].astype(jnp.int32)
-    target_out[:, HALO : HALO + OWN, :] = target[...]
-    target_out[:, 0:HALO, :] = below[21]
-    target_out[:, HALO + OWN : ROWS, :] = above[21]
-    half_low = jnp.broadcast_to(wetting[0:1, :], (8, DEPTH))
-    half_high = jnp.broadcast_to(wetting[1:2, :], (8, DEPTH))
+def start_rows(t, populations, shares, marks, table, outs):
+    lin_out, flow_out, density_out, effective_out, share_out, _, send_left, send_right = outs
+    half_low = jnp.broadcast_to(table[0:1, :], (8, DEPTH))
+    half_high = jnp.broadcast_to(table[1:2, :], (8, DEPTH))
+    lin, first, chosen, effective = [], [], [], []
+    for x in range(2):
+        share = shares[x]
+        spot = jnp.bitwise_and(marks[x], DEPTH - 1)
+        wall = jnp.where(
+            jnp.bitwise_and(marks[x], DEPTH) == 0,
+            jnp.take_along_axis(half_low, spot, axis=1),
+            jnp.take_along_axis(half_high, spot, axis=1),
+        )
+        total, momentum, linear = linear_part(populations[x], share, range(19))
+        eff = jnp.where(share > 0, 1.0 - jnp.exp(-total), wall)
+        for i in range(19):
+            lin_out[i, x, flat(t), :] = linear[i]
+        for a in range(3):
+            flow_out[a, x, flat(t), :] = momentum[a]
+        density_out[x, flat(t), :] = total
+        effective_out[x, flat(t), :] = eff
+        share_out[x, flat(t), :] = share
+        lin.append(linear)
+        first.append(momentum)
+        chosen.append(jnp.where(share > 0, total, wall))
+        effective.append(eff)
+    put_sends(send_left, send_right, t, lin, first, chosen, effective)
+    send_left[10, flat(t), :] = shares[0]
+    send_left[11, flat(t), :] = shares[1]
+    send_right[10, flat(t), :] = shares[1]
+    send_right[11, flat(t), :] = shares[0]
+
+
+def own_kernel(pops, fluid, label, target, table, *outs):
+    outs[5][:, HALO : HALO + OWN, :] = target[...]
 
     def body(t):
-        lin, first, chosen, effective = [], [], [], []
-        for x in range(2):
-            f = {i: wide[i, x, flat(t), :] for i in range(19)}
-            share = share_out[x, flat(t), :]
-            marks = label_wide[x, flat(t), :]
-            spot = jnp.bitwise_and(marks, DEPTH - 1)
-            wall = jnp.where(
-                jnp.bitwise_and(marks, DEPTH) == 0,
-                jnp.take_along_axis(half_low, spot, axis=1),
-                jnp.take_along_axis(half_high, spot, axis=1),
-            )
-            total, momentum, linear = linear_part(f, share, range(19))
-            eff = jnp.where(share > 0, 1.0 - jnp.exp(-total), wall)
-            for i in range(19):
-                lin_out[i, x, flat(t), :] = linear[i]
-            for a in range(3):
-                flow_out[a, x, flat(t), :] = momentum[a]
-            density_out[x, flat(t), :] = total
-            effective_out[x, flat(t), :] = eff
-            lin.append(linear)
-            first.append(momentum)
-            chosen.append(jnp.where(share > 0, total, wall))
-            effective.append(eff)
-        put_sends(send_left, send_right, t, lin, first, chosen, effective)
-        send_left[10, flat(t), :] = share_out[0, flat(t), :]
-        send_left[11, flat(t), :] = share_out[1, flat(t), :]
-        send_right[10, flat(t), :] = share_out[1, flat(t), :]
-        send_right[11, flat(t), :] = share_out[0, flat(t), :]
-
-    each_chunk(body)
+        rows = rows_at(t, 0, -HALO)
+        start_rows(
+            t,
+            [{i: pops[i, x, rows, :] for i in range(19)} for x in range(2)],
+            [fluid[x, rows, :].astype(jnp.float32) for x in range(2)],
+            [label[x, rows, :] for x in range(2)],
+            table,
+            outs,
+        )
+
+    each_chunk(body, HALO // 8, (HALO + OWN) // 8)
+
+
+def halo_kernel(table, below, above, *refs):
+    outs = refs[len(refs) // 2 :]
+    for t, edge in ((0, below), (CHUNKS - 1, above)):
+        outs[5][:, 8 * t : 8 * t + 8, :] = edge[21]
+        start_rows(
+            t,
+            [{i: edge[i, x] for i in range(19)} for x in range(2)],
+            [edge[19, x] for x in range(2)],
+            [edge[20, x].astype(jnp.int32) for x in range(2)],
+            table,
+            outs,
+        )
 
 
 def step_kernel(is_first, *refs):
@@ -570,47 +594,36 @@
     return jnp.where(mask_ahead(masks, i, 2 + x, t), there, adjoint[OPPOSITE[i], x, tall(t), :])
 
 
-def first_reverse_kernel(
-    adjoint, turned, wall, from_left, from_right, masks, field, speed, pull, chooser,
-    grad, label_part,
-    come, pulled, pulled_doubled, base,
+def place_sides(come, from_left, from_right, t):
+    for side, source, which in ((0, from_left, LEFTWARD), (1, from_right, RIGHTWARD)):
+        for k, i in enumerate(which):
+            come[side, k, tall(t), :] = rolled(source[k, flat(t), :], -VECTORS[i][2])
+
+
+def arrived(come, adjoint, masks, i, x, t):
+    which = LEFTWARD if x == 0 else RIGHTWARD
+    there = come[x, which.index(i), tall(t, VECTORS[i][1]), :]
+    return jnp.where(mask_ahead(masks, i, 2 + x, t), there, adjoint[OPPOSITE[i], x, tall(t), :])
+
+
+def wall_kernel(
+    adjoint, turned, wall, part_left, part_right, from_left, from_right, masks, field, speed, chooser,
+    more_out, label_part,
+    come, pulled, pulled_doubled, totals,
 ):
-    sides = ((0, from_left, LEFTWARD), (1, from_right, RIGHTWARD))
-
-    def place(t):
-        for side, source, which in sides:
-            for k, i in enumerate(which):
-                come[side, k, tall(t), :] = rolled(source[k, flat(t), :], -VECTORS[i][2])
-
-    each_chunk(place)
+    each_chunk(functools.partial(place_sides, come, from_left, from_right))
 
     def collide(t):
-        for x in range(2):
+        for x, part, which in ((0, part_left, LEFTWARD), (1, part_right, RIGHTWARD)):
             p = 2 + x
             s = masks[0, p, tall(t), :]
-            r = {}
-            for i in range(19):
-                cx, cy, cz = VECTORS[i]
-                if (x, cx) in ((0, -1), (1, 1)):
-                    side = x
-                    there = come[side, sides[side][2].index(i), tall(t, cy), :]
-                    value = jnp.where(
-                        mask_ahead(masks, i, p, t), there, adjoint[OPPOSITE[i], x, tall(t), :]
-                    )
-                else:
-                    value = adjoint_ahead(adjoint, turned, masks, i, x, t)
-                r[i] = s * value
-            psi = field[p, tall(t), :]
+            r = {i: arrived(come, adjoint, masks, i, x, t) for i in which}
             u = [speed[a, p - 1, flat(t), :] for a in range(3)]
-            rest, by_density, q = collide_adjoint(r, u)
-            along = add(*[q[a] * pull[a, x, flat(t), :] for a in range(3)])
-            const = by_density + along * ((PULL / SHEAR) * (1.0 - psi))
-            for i in range(19):
-                base[i, x, flat(t), :] = rest[i] + const
-            put_pulled(pulled, pulled_doubled, p - 1, t, psi, q)
-        for side, source, which in sides:
-            p = 1 if side == 0 else 4
-            x = 0 if side == 0 else 1
+            rest = flow_adjoint(*dual(r), u)
+            q = [part[5 + a, flat(t), :] + s * rest[a] for a in range(3)]
+            put_pulled(pulled, pulled_doubled, p - 1, t, field[p, tall(t), :], q)
+        for x, source, which in ((0, from_left, LEFTWARD), (1, from_right, RIGHTWARD)):
+            p = 1 if x == 0 else 4
             s = masks[0, p, tall(t), :]
             r = {}
             for i in [OPPOSITE[j] for j in which]:
@@ -622,8 +635,8 @@
                 here = source[which.index(OPPOSITE[i]), flat(t), :]
                 r[i] = jnp.where(mask_ahead(masks, i, p, t), there, here)
             u = [speed[a, p - 1, flat(t), :] for a in range(3)]
-            more = flow_adjoint(*dual(r), u)
-            q = [source[5 + a, flat(t), :] + s * more[a] for a in range(3)]
+            rest = flow_adjoint(*dual(r), u)
+            q = [source[5 + a, flat(t), :] + s * rest[a] for a in range(3)]
             put_pulled(pulled, pulled_doubled, p - 1, t, field[p, tall(t), :], q)
 
     each_chunk(collide)
@@ -634,24 +647,49 @@
             s = masks[0, 2 + x, tall(t), :]
             spread = spread_of(pulled, pulled_doubled, 1 + x, t)
             total = add(total, (1.0 - s) * spread + wall[x, flat(t), :])
-            more = s * spread * (1.0 - field[2 + x, tall(t), :])
-            for i in range(19):
-                grad[i, x, rows_at(t, 0, -HALO), :] = base[i, x, flat(t), :] + more
-        base[0, 0, flat(t), :] = total
+            more_out[x, rows_at(t, 0, -HALO), :] = s * spread * (1.0 - field[2 + x, tall(t), :])
+        totals[rows_at(t, 0, -HALO), :] = total
 
     each_chunk(finish, HALO // 8, (HALO + OWN) // 8)
 
-    totals = base[0, 0, HALO : HALO + OWN, :]
     blocks = (OWN // 2) * (DEPTH // 4)
     column = lax.broadcasted_iota(jnp.int32, (DEPTH, blocks), 1)
     quad = lax.broadcasted_iota(jnp.int32, (DEPTH, blocks), 0) // 4
     gather = (jnp.bitwise_and(column, DEPTH // 4 - 1) == quad).astype(jnp.bfloat16)
-    by_block = exact_dot(totals, gather)
+    by_block = exact_dot(totals[...], gather)
     pair = lax.broadcasted_iota(jnp.int32, (OWN, blocks), 0) // 2
     wanted = lax.broadcasted_iota(jnp.int32, (OWN, blocks), 1) // (DEPTH // 4)
     by_block = jnp.where(pair == wanted, by_block, 0.0)
     by_label = exact_dot(by_block, chooser[...])
     label_part[...] = jnp.sum(by_label, axis=0, keepdims=True)
+
+
+def grad_kernel(
+    adjoint, turned, more, from_left, from_right, masks, field, speed, pull,
+    grad,
+    come,
+):
+    each_chunk(functools.partial(place_sides, come, from_left, from_right))
+
+    def collide(t):
+        for x in range(2):
+            p = 2 + x
+            s = masks[0, p, tall(t), :]
+            r = {}
+            for i in range(19):
+                if VECTORS[i][0] == 2 * x - 1:
+                    r[i] = s * arrived(come, adjoint, masks, i, x, t)
+                else:
+                    r[i] = s * adjoint_ahead(adjoint, turned, masks, i, x, t)
+            u = [speed[a, p - 1, flat(t), :] for a in range(3)]
+            rest, by_density, q = collide_adjoint(r, u)
+            along = add(*[q[a] * pull[a, x, flat(t), :] for a in range(3)])
+            const = by_density + along * ((PULL / SHEAR) * (1.0 - field[p, tall(t), :]))
+            const = const + more[x, rows_at(t, 0, -HALO), :]
+            for i in range(19):
+                grad[i, x, rows_at(t, 0, -HALO), :] = rest[i] + const
+
+    each_chunk(collide, HALO // 8, (HALO + OWN) // 8)
 
 
 def exact_dot(values, zero_one):
@@ -663,15 +701,19 @@
     return dot(high) + (dot(middle) + dot(low))
 
 
-def call(kernel, args, outs, scratch):
+def call(kernel, args, outs, scratch, anywhere=0, grant=12, filled=0):
     whole = pl.BlockSpec(memory_space=pltpu.VMEM)
+    there = pl.BlockSpec(memory_space=pl.ANY)
+    size = 4 * sum(int(np.prod(s)) for s in outs) + sum(a.size * a.dtype.itemsize for a in args)
     return pl.pallas_call(
         kernel,
         out_shape=[jax.ShapeDtypeStruct(s, jnp.float32) for s in outs],
-        in_specs=[whole] * len(args),
+        in_specs=[there] * anywhere + [whole] * (len(args) - anywhere),
         out_specs=[whole] * len(outs),
-        scratch_shapes=[pltpu.VMEM(s, d) for s, d in scratch],
-        compiler_params=pltpu.CompilerParams(vmem_limit_bytes=40 * 1024 * 1024),
+        scratch_shapes=scratch,
+        input_output_aliases={len(args) - filled + k: k for k in range(filled)},
+        compiler_params=pltpu.CompilerParams(vmem_limit_bytes=grant * 1024 * 1024),
+        cost_estimate=pl.CostEstimate(flops=0, bytes_accessed=size, transcendentals=0),
     )(*args)
 
 
@@ -689,23 +731,30 @@
 
 
 def per_device(populations, fluid, label, wall_wetting, target):
-    f32 = jnp.float32
+    vmem = lambda *shape: pltpu.VMEM(shape, jnp.float32)
     plane = (ROWS, DEPTH)
     two = (2, *plane)
     edge = (22, 2, HALO, DEPTH)
-    low, high = call(edges_kernel, (populations, fluid, label, target), (edge, edge), ())
+    low, high = call(
+        edges_kernel,
+        (populations, fluid, label, target),
+        (edge, edge),
+        (pltpu.VMEM((2, 2, 2, HALO, DEPTH), jnp.int32), pltpu.SemaphoreType.DMA((8,))),
+        anywhere=4,
+        grant=56,
+    )
     below, above = both_ways(low, high, "gy")
     marks = jnp.bitwise_and(label[0, ::2, ::4], LABELS - 1).reshape(-1)
     chooser = (marks[:, None] == jnp.arange(LABELS, dtype=jnp.int32)[None, :]).astype(jnp.bfloat16)
+    table = wall_wetting.reshape(2, DEPTH)
+    started = ((19, *two), (3, *two), two, two, two, two, (12, *plane), (12, *plane))
+    own = call(own_kernel, (populations, fluid, label, target, table), started, ())
     lin, flow, density, effective, share, target_wide, to_left, to_right = call(
-        start_kernel,
-        (populations, fluid, label, target, wall_wetting.reshape(2, DEPTH), below, above),
-        ((19, *two), (3, *two), two, two, two, two, (12, *plane), (12, *plane)),
-        (((19, *two), f32), (two, jnp.int32)),
+        halo_kernel, (table, below, above, *own), started, (), filled=len(started)
     )
     from_left, from_right = both_ways(to_left, to_right, "gx")
     wide6 = (6, TALL, DEPTH)
-    work = ((wide6, f32), ((19, 4, TALL, DEPTH), f32), ((10, 4, TALL, DEPTH), f32))
+    work = (vmem(*wide6), vmem(19, 4, TALL, DEPTH), vmem(10, 4, TALL, DEPTH))
     masks, field0, speed0, pull0, lin, flow, density, effective, to_left, to_right = call(
         functools.partial(step_kernel, True),
         (lin, flow, density, effective, share, from_left, from_right),
@@ -723,19 +772,20 @@
         work,
     )
     from_left, from_right = both_ways(misfit, misfit, "gx")
-    pulled = (((3, 4, TALL, DEPTH), f32), ((2, 4, TALL, DEPTH), f32), ((19, *two), f32))
+    pulled = (vmem(3, 4, TALL, DEPTH), vmem(2, 4, TALL, DEPTH))
     adjoint, turned, wall, to_left, to_right = call(
         last_reverse_kernel,
         (misfit, from_left, from_right, masks, field1, speed1, pull1, speed0),
         ((19, 2, TALL, DEPTH), (10, 2, TALL, DEPTH), two, (8, *plane), (8, *plane)),
-        (((3, *wide6), f32), *pulled),
+        (vmem(3, *wide6), *pulled, vmem(19, *two)),
     )
     from_left, from_right = both_ways(to_left, to_right, "gx")
-    grad, label_part = call(
-        first_reverse_kernel,
-        (adjoint, turned, wall, from_left, from_right, masks, field0, speed0, pull0, chooser),
-        (populations.shape, (1, LABELS)),
-        (((2, 5, TALL, DEPTH), f32), *pulled),
+    come = vmem(2, 5, TALL, DEPTH)
+    more, label_part = call(
+        wall_kernel,
+        (adjoint, turned, wall, to_left, to_right, from_left, from_right, masks, field0, speed0, chooser),
+        ((2, OWN, DEPTH), (1, LABELS)),
+        (come, *pulled, vmem(OWN, DEPTH)),
     )
     count = lax.axis_size("gy")
     wetting_grad = label_part
@@ -743,6 +793,12 @@
         wetting_grad = wetting_grad + lax.ppermute(
             label_part, "gy", [(i, (i + step) % count) for i in range(count)]
         )
+    (grad,) = call(
+        grad_kernel,
+        (adjoint, turned, more, from_left, from_right, masks, field0, speed0, pull0),
+        (populations.shape,),
+        (come,),
+    )
     return (grad, wetting_grad.reshape(-1))
 
 

time: 85 us -> 83.4 us (0.981)
  waiting for transfers between devices: 26.4 us -> 21.5 us
  Pallas kernels: 12.2 us -> 16.2 us
    pallas_call x6 -> x8, Pallas kernels: 12.2 us -> 16.2 us  [call(): pl.pallas_call(kernel, out_shape=[jax.ShapeDtypeStruct(s, jnp.float32) fo...]
    ppermute x5, waiting for transfers between devices: 18.1 us -> 16.3 us  [both_ways(): from_lower = lax.ppermute(to_upper, axis, up)]
    ppermute x5, waiting for transfers between devices: 4.17 us -> 2.45 us  [both_ways(): from_upper = lax.ppermute(to_lower, axis, down)]
    ppermute x3, waiting for transfers between devices: 4.14 us -> 2.7 us  [per_device(): lax.ppermute(label_part, 'gy', [(i, (i + step) % count) for i in range(co...]
    unnamed x22 -> x18, local copies, waits for them, and re-layouts: 7.65 us -> 6.85 us
  transfers between devices with their start and end apart: 13 -> 13, of which waited for: 9 -> 7; matrix products, arithmetic and copies ran while one was open for 1% -> 1% of each run, Pallas kernels for 0% -> 3%
where the time goes in v1:
time: 83.4 us; the launch traced here: 82.8 us
  starting transfers between devices  35.9 us (43%)
  waiting for transfers between devices  21.5 us (26%)
  Pallas kernels  16.2 us (19%)
  local copies, waits for them, and re-layouts  7.77 us (9%)
    ppermute x5, starting transfers between devices, both_ways(): from_upper = lax.ppermute(to_lower, axis, down)  24.2 us
    ppermute x5, waiting for transfers between devices, both_ways(): from_lower = lax.ppermute(to_upper, axis, up)  16.3 us
    pallas_call x8, Pallas kernels, call(): pl.pallas_call(kernel, out_shape=[jax.ShapeDtypeStruct(s, jnp.float32) fo...  16.2 us
    unnamed x18, local copies, waits for them, and re-layouts  6.85 us
    ppermute x3, starting transfers between devices, per_device(): lax.ppermute(label_part, 'gy', [(i, (i + step) % count) for i in range(co...  6.08 us
    ppermute x5, starting transfers between devices, both_ways(): from_lower = lax.ppermute(to_upper, axis, up)  5.58 us
    ppermute x3, waiting for transfers between devices, per_device(): lax.ppermute(label_part, 'gy', [(i, (i + step) % count) for i in range(co...  2.7 us
    ppermute x5, waiting for transfers between devices, both_ways(): from_upper = lax.ppermute(to_lower, axis, down)  2.45 us
  transfers between devices with their start and end apart: 13, of which 7 were waited for; matrix products, arithmetic and copies ran while one was open for 1% of the time, Pallas kernels for 3%

profile of v1, /device:TPU:1, one launch (start us, length us, event | category | flops | bytes accessed | tf_op | source)
XLA Modules:
  0.0 82.8 jit_solution(2126681307964517645)
XLA Ops:
  0.6 1.9 %shard_map.68 = (f32[22,2,8,128]{3,2,1,0:T(8,128)}, f32[22,2,8,128]{3,2,1,0:T(8,128)}) custom-call(f32[19,2,32,128]{3,2,1,0:T(8,128)} %pops.3, s32[2,32,128]{2,1,0:T(8,128)} %fluid.3, s32[2,32,128]{2,1,0:T(8,128)} %label.3, f32[2,32,128]{2,1,0:T(8,128)} %target.3), custom_call_target="tpu_custom_call" | custom-call | bytes 1081344 | tf_op jit(solution)/shard_map/pallas_call | solution.py:708
  2.5 4.4 %collective-permute-start = (f32[22,2,8,128]{3,2,1,0:T(8,128)}, f32[22,2,8,128]{3,2,1,0:T(8,128)S(1)}, u32[]{:S(2)}, u32[]{:S(2)}) collective-permute-start(f32[22,2,8,128]{3,2,1,0:T(8,128)} %get-tuple-element.41), channel_id=1, source_target_pairs={{0,1},{1,2},{2,3},{3,0},{4,5},{5,6},{6,7},{7,4},{8,9},{9,10},{10,1... | collective-permute-start | bytes 540680 | tf_op jit(solution)/shard_map/ppermute | solution.py:728
  6.9 0.0 collective-permute-start.1
  6.9 0.0 copy-start
  6.9 1.1 %copy-done = f32[19,2,32,128]{3,2,1,0:T(8,128)S(1)} copy-done((f32[19,2,32,128]{3,2,1,0:T(8,128)S(1)}, f32[19,2,32,128]{3,2,1,0:T(8,128)}, u32[]{:S(2)}) %copy-start) | copy-done | bytes 622616
  8.0 0.8 copy-done.1
  8.8 0.8 copy-done.2
  9.5 0.8 copy-done.3
  10.3 0.7 copy-done.8
  11.0 0.3 shard_map.69
  11.3 0.0 collective-permute-done.below
  11.3 2.4 %collective-permute-done.1.above = f32[22,2,8,128]{3,2,1,0:T(8,128)S(1)} collective-permute-done((f32[22,2,8,128]{3,2,1,0:T(8,128)}, f32[22,2,8,128]{3,2,1,0:T(8,128)S(1)}, u32[]{:S(2)}, u32[]{:S(2)}) %collective-permute-start.1) | collective-permute-done | bytes 180256 | tf_op jit(solution)/shard_map/ppermute | solution.py:729
  13.7 0.1 shard_map.70
  13.9 1.1 %collective-permute-start.2 = (f32[12,48,128]{2,1,0:T(8,128)S(1)}, f32[12,48,128]{2,1,0:T(8,128)S(1)}, u32[]{:S(2)}, u32[]{:S(2)}) collective-permute-start(f32[12,48,128]{2,1,0:T(8,128)S(1)} %get-tuple-element.56), channel_id=1, source_target_pairs={{0,4},{4,8},{8,12},{12,16},{16,20},{20,24},{24,28},{28,32},{32,36}... | collective-permute-start | bytes 884744 | tf_op jit(solution)/shard_map/ppermute | solution.py:728
  15.0 6.8 %collective-permute-start.3 = (f32[12,48,128]{2,1,0:T(8,128)S(1)}, f32[12,48,128]{2,1,0:T(8,128)S(1)}, u32[]{:S(2)}, u32[]{:S(2)}) collective-permute-start(f32[12,48,128]{2,1,0:T(8,128)S(1)} %get-tuple-element.57), channel_id=1, source_target_pairs={{4,0},{8,4},{12,8},{16,12},{20,16},{24,20},{28,24},{32,28},{36,32}... | collective-permute-start | bytes 884744 | tf_op jit(solution)/shard_map/ppermute | solution.py:729
  21.7 6.5 %collective-permute-done.2.refs_5_ = f32[12,48,128]{2,1,0:T(8,128)S(1)} collective-permute-done((f32[12,48,128]{2,1,0:T(8,128)S(1)}, f32[12,48,128]{2,1,0:T(8,128)S(1)}, u32[]{:S(2)}, u32[]{:S(2)}) %collective-permute-start.2) | collective-permute-done | bytes 294944 | tf_op jit(solution)/shard_map/ppermute | solution.py:728
  28.2 0.0 collective-permute-done.3.refs_6_
  28.2 3.1 %shard_map.71 = (f32[3,6,64,128]{3,2,1,0:T(8,128)S(1)}, f32[6,64,128]{2,1,0:T(8,128)S(1)}, f32[3,4,48,128]{3,2,1,0:T(8,128)S(1)}, f32[3,2,48,128]{3,2,1,0:T(8,12...) custom-call(f32[19,2,48,128]{3,2,1,0:T(8,128)S(1)} %get-tuple-elemen, ...), custom_call_target="tpu_custom_call" | custom-call | bytes 4718592 | tf_op jit(solution)/shard_map/pallas_call | solution.py:708
  31.4 0.6 copy-done.4
  32.0 0.6 copy-done.6
  32.6 0.0 collective-permute-start.4
  32.6 6.0 %collective-permute-start.5 = (f32[10,48,128]{2,1,0:T(8,128)S(1)}, f32[10,48,128]{2,1,0:T(8,128)S(1)}, u32[]{:S(2)}, u32[]{:S(2)}) collective-permute-start(f32[10,48,128]{2,1,0:T(8,128)S(1)} %get-tuple-element.65), channel_id=1, source_target_pairs={{4,0},{8,4},{12,8},{16,12},{20,16},{24,20},{28,24},{32,28},{36,32}... | collective-permute-start | bytes 737288 | tf_op jit(solution)/shard_map/ppermute | solution.py:729
  38.6 0.8 %slice.3 = s32[1,16,32]{2,1,0:T(8,128)S(1)} slice(s32[2,32,128]{2,1,0:T(8,128)} %label.3), slice={[0:1:1], [0:32:2], [0:128:4]} | slice | bytes 4096 | tf_op jit(solution)/shard_map/slice | solution.py:747
  39.5 5.4 %collective-permute-done.4.refs_7_ = f32[10,48,128]{2,1,0:T(8,128)S(1)} collective-permute-done((f32[10,48,128]{2,1,0:T(8,128)}, f32[10,48,128]{2,1,0:T(8,128)S(1)}, u32[]{:S(2)}, u32[]{:S(2)}) %collective-permute-start.4) | collective-permute-done | bytes 245792 | tf_op jit(solution)/shard_map/ppermute | solution.py:728
  44.9 0.0 collective-permute-done.5.refs_8_
  44.9 0.8 copy-done.5
  45.7 0.8 copy-done.7
  46.5 2.7 %shard_map.72 = (f32[6,64,128]{2,1,0:T(8,128)S(1)}, f32[3,4,48,128]{3,2,1,0:T(8,128)S(1)}, f32[3,2,48,128]{3,2,1,0:T(8,128)S(1)}, f32[2,48,128]{2,1,0:T(8,128)}) custom-call(f32[19,2,48,128]{3,2,1,0:T(8,128)S(1)} %get-tuple-element.58.refs_0_, f32[3,2,48,128]{3,2,1,0:T(8,128)S(1)} %get-tuple-element.59.refs_1_, f32[2,48,128]{2,1,0:T(8,128)S(1)} %copy-done.5, ...), custom_call_target="tpu_custom_call" | custom-call | bytes 3047424 | tf_op jit(solution)/shard_map/pallas_call | solution.py:708
  49.2 0.0 collective-permute-start.6
  49.2 5.7 %collective-permute-start.7 = (f32[2,48,128]{2,1,0:T(8,128)}, f32[2,48,128]{2,1,0:T(8,128)S(1)}, u32[]{:S(2)}, u32[]{:S(2)}) collective-permute-start(f32[2,48,128]{2,1,0:T(8,128)} %get-tuple-element.66.misfit), channel_id=1, source_target_pairs={{4,0},{8,4},{12,8},{16,12},{20,16},{24,20},{28,24},{32,28},{36,32}... | collective-permute-start | bytes 147464 | tf_op jit(solution)/shard_map/ppermute | solution.py:729
  54.9 0.1 and.15
  55.0 1.6 %collective-permute-done.6.from_left = f32[2,48,128]{2,1,0:T(8,128)S(1)} collective-permute-done((f32[2,48,128]{2,1,0:T(8,128)}, f32[2,48,128]{2,1,0:T(8,128)S(1)}, u32[]{:S(2)}, u32[]{:S(2)}) %collective-permute-start.6) | collective-permute-done | bytes 49184 | tf_op jit(solution)/shard_map/ppermute | solution.py:728
  56.6 0.0 collective-permute-done.7.from_right
  56.6 4.3 %shard_map.73 = (f32[19,2,64,128]{3,2,1,0:T(8,128)S(1)}, f32[10,2,64,128]{3,2,1,0:T(8,128)S(1)}, f32[2,48,128]{2,1,0:T(8,128)S(1)}, f32[8,48,128]{2,1,0:T(8,128)S(1)}, f32[8,48,128]{2,1,0:T(8,128)S(1)}) custom-call(f32[2,48,128]{2,1,0:T(8,128)} %get-tuple-element.66.misfit, f32[2,48,128]{2,1,0:T(8,128)S(1)} %collective-permute-done.6.from_left, ...), custom_call_target="tpu_custom_call" | custom-call | bytes 4014080 | tf_op jit(solution)/shard_map/pallas_call | solution.py:708
  60.8 0.1 collective-permute-start.8
  60.9 5.8 %collective-permute-start.9 = (f32[8,48,128]{2,1,0:T(8,128)S(1)}, f32[8,48,128]{2,1,0:T(8,128)S(1)}, u32[]{:S(2)}, u32[]{:S(2)}) collective-permute-start(f32[8,48,128]{2,1,0:T(8,128)S(1)} %get-tuple-element.74.part_left), channel_id=1, source_target_pairs={{4,0},{8,4},{12,8},{16,12},{20,16},{24,20},{28,24},{32,28},{36,32}... | collective-permute-start | bytes 589832 | tf_op jit(solution)/shard_map/ppermute | solution.py:729
  66.7 0.1 fusion.chooser
  66.8 2.8 %collective-permute-done.8.from_left = f32[8,48,128]{2,1,0:T(8,128)S(1)} collective-permute-done((f32[8,48,128]{2,1,0:T(8,128)S(1)}, f32[8,48,128]{2,1,0:T(8,128)S(1)}, u32[]{:S(2)}, u32[]{:S(2)}) %collective-permute-start.8) | collective-permute-done | bytes 196640 | tf_op jit(solution)/shard_map/ppermute | solution.py:728
  69.7 0.0 collective-permute-done.9.from_right
  69.7 2.0 %shard_map.74 = (f32[2,32,128]{2,1,0:T(8,128)S(1)}, f32[1,256]{1,0:T(1,128)S(1)}) custom-call(f32[19,2,64,128]{3,2,1,0:T(8,128)S(1)} %get-tuple-element.71.adjoint, f32[10,2,64,128]{3,2,1,0:T(8,128)S(1)} %get-tuple-element.72.turned, f32[2,48,128]{2,1,0:T(8,128)S(1)} %get-tuple-element.73.wall, f32[8,48,128]{2,1,0:T(8,128)S(1)} %get-tuple-element.74.part_left, ...), custom_call_target="tpu_custom_call" | custom-call | bytes 4113408 | tf_op jit(solution)/shard_map/pallas_call | solution.py:708
  71.6 5.6 %collective-permute-start.10 = (f32[1,256]{1,0:T(1,128)S(1)}, f32[1,256]{1,0:T(1,128)S(1)}, u32[]{:S(2)}, u32[]{:S(2)}) collective-permute-start(f32[1,256]{1,0:T(1,128)S(1)} %get-tuple-element.79), channel_id=1, source_target_pairs={{0,1},{1,2},{2,3},{3,0},{4,5},{5,6},{6,7},{7,4},{8,9},{9,10},{10,1... | collective-permute-start | bytes 3080 | tf_op jit(solution)/shard_map/ppermute | solution.py:793
  77.2 0.5 collective-permute-start.11
  77.7 0.0 collective-permute-start.12
  77.7 1.8 %shard_map.75 = f32[19,2,32,128]{3,2,1,0:T(8,128)} custom-call(f32[19,2,64,128]{3,2,1,0:T(8,128)S(1)} %get-tuple-element.71.adjoint, f32[10,2,64,128]{3,2,1,0:T(8,128)S(1)} %get-tuple-element.72.turned, f32[2,32,128]{2,1,0:T(8,128)S(1)} %get-tuple-element.77.more, f32[8,48,128]{2,1,0:T(8,128)S(1)} %collective-permute-done.8.from_left, ...), custom_call_target="tpu_custom_call" | custom-call | bytes 4177920 | tf_op jit(solution)/shard_map/pallas_call | solution.py:708
  79.5 0.0 collective-permute-done.10
  79.5 1.6 %collective-permute-done.11 = f32[1,256]{1,0:T(1,128)S(1)} collective-permute-done((f32[1,256]{1,0:T(1,128)S(1)}, f32[1,256]{1,0:T(1,128)S(1)}, u32[]{:S(2)}, u32[]{:S(2)}) %collective-permute-start.11) | collective-permute-done | bytes 1056 | tf_op jit(solution)/shard_map/ppermute | solution.py:793
  81.2 1.1 %collective-permute-done.12 = f32[1,256]{1,0:T(1,128)S(1)} collective-permute-done((f32[1,256]{1,0:T(1,128)S(1)}, f32[1,256]{1,0:T(1,128)S(1)}, u32[]{:S(2)}, u32[]{:S(2)}) %collective-permute-start.12) | collective-permute-done | bytes 1056 | tf_op jit(solution)/shard_map/ppermute | solution.py:793
  82.2 0.6 add_add_fusion
  (9 shorter events, 0.0 us)
Async XLA Ops:
  2.5 8.7 %collective-permute-start = (f32[22,2,8,128]{3,2,1,0:T(8,128)}, f32[22,2,8,128]{3,2,1,0:T(8,128)S(1)}, u32[]{:S(2)}, u32[]{:S(2)}) collective-permute-start(f32[22,2,8,128]{3,2,1,0:T(8,128)} %get-tuple-element.41), channel_id=1, source_target_pairs={{0,1},{1,2},{2,3},{3,0},{4,5},{5,6},{6,7},{7,4},{8,9},{9,10},{10,1... | collective-permute-start | bytes 540680 | tf_op jit(solution)/shard_map/ppermute | solution.py:728
  6.9 6.8 %collective-permute-start.1 = (f32[22,2,8,128]{3,2,1,0:T(8,128)}, f32[22,2,8,128]{3,2,1,0:T(8,128)S(1)}, u32[]{:S(2)}, u32[]{:S(2)}) collective-permute-start(f32[22,2,8,128]{3,2,1,0:T(8,128)} %get-tuple-element.42), channel_id=1, source_target_pairs={{1,0},{2,1},{3,2},{0,3},{5,4},{6,5},{7,6},{4,7},{9,8},{10,9},{11,1... | collective-permute-start | bytes 540680 | tf_op jit(solution)/shard_map/ppermute | solution.py:729
  6.9 1.1 %copy-start = (f32[19,2,32,128]{3,2,1,0:T(8,128)S(1)}, f32[19,2,32,128]{3,2,1,0:T(8,128)}, u32[]{:S(2)}) copy-start(f32[19,2,32,128]{3,2,1,0:T(8,128)} %pops.3) | copy-start | bytes 1867780
  8.0 0.8 copy-start.1
  8.8 0.8 copy-start.2
  9.5 0.8 copy-start.3
  10.3 0.7 copy-start.8
  13.9 14.3 %collective-permute-start.2 = (f32[12,48,128]{2,1,0:T(8,128)S(1)}, f32[12,48,128]{2,1,0:T(8,128)S(1)}, u32[]{:S(2)}, u32[]{:S(2)}) collective-permute-start(f32[12,48,128]{2,1,0:T(8,128)S(1)} %get-tuple-element.56), channel_id=1, source_target_pairs={{0,4},{4,8},{8,12},{12,16},{16,20},{20,24},{24,28},{28,32},{32,36}... | collective-permute-start | bytes 884744 | tf_op jit(solution)/shard_map/ppermute | solution.py:728
  15.0 13.2 %collective-permute-start.3 = (f32[12,48,128]{2,1,0:T(8,128)S(1)}, f32[12,48,128]{2,1,0:T(8,128)S(1)}, u32[]{:S(2)}, u32[]{:S(2)}) collective-permute-start(f32[12,48,128]{2,1,0:T(8,128)S(1)} %get-tuple-element.57), channel_id=1, source_target_pairs={{4,0},{8,4},{12,8},{16,12},{20,16},{24,20},{28,24},{32,28},{36,32}... | collective-permute-start | bytes 884744 | tf_op jit(solution)/shard_map/ppermute | solution.py:729
  31.4 0.6 copy-start.4
  32.0 0.6 copy-start.6
  32.6 12.3 %collective-permute-start.4 = (f32[10,48,128]{2,1,0:T(8,128)}, f32[10,48,128]{2,1,0:T(8,128)S(1)}, u32[]{:S(2)}, u32[]{:S(2)}) collective-permute-start(f32[10,48,128]{2,1,0:T(8,128)} %get-tuple-element.64), channel_id=1, source_target_pairs={{0,4},{4,8},{8,12},{12,16},{16,20},{20,24},{24,28},{28,32},{32,36}... | collective-permute-start | bytes 737288 | tf_op jit(solution)/shard_map/ppermute | solution.py:728
  32.6 12.3 %collective-permute-start.5 = (f32[10,48,128]{2,1,0:T(8,128)S(1)}, f32[10,48,128]{2,1,0:T(8,128)S(1)}, u32[]{:S(2)}, u32[]{:S(2)}) collective-permute-start(f32[10,48,128]{2,1,0:T(8,128)S(1)} %get-tuple-element.65), channel_id=1, source_target_pairs={{4,0},{8,4},{12,8},{16,12},{20,16},{24,20},{28,24},{32,28},{36,32}... | collective-permute-start | bytes 737288 | tf_op jit(solution)/shard_map/ppermute | solution.py:729
  44.9 0.8 copy-start.5
  45.7 0.8 copy-start.7
  49.2 7.4 %collective-permute-start.6 = (f32[2,48,128]{2,1,0:T(8,128)}, f32[2,48,128]{2,1,0:T(8,128)S(1)}, u32[]{:S(2)}, u32[]{:S(2)}) collective-permute-start(f32[2,48,128]{2,1,0:T(8,128)} %get-tuple-element.66.misfit), channel_id=1, source_target_pairs={{0,4},{4,8},{8,12},{12,16},{16,20},{20,24},{24,28},{28,32},{32,36}... | collective-permute-start | bytes 147464 | tf_op jit(solution)/shard_map/ppermute | solution.py:728
  49.2 7.4 %collective-permute-start.7 = (f32[2,48,128]{2,1,0:T(8,128)}, f32[2,48,128]{2,1,0:T(8,128)S(1)}, u32[]{:S(2)}, u32[]{:S(2)}) collective-permute-start(f32[2,48,128]{2,1,0:T(8,128)} %get-tuple-element.66.misfit), channel_id=1, source_target_pairs={{4,0},{8,4},{12,8},{16,12},{20,16},{24,20},{28,24},{32,28},{36,32}... | collective-permute-start | bytes 147464 | tf_op jit(solution)/shard_map/ppermute | solution.py:729
  60.8 8.8 %collective-permute-start.8 = (f32[8,48,128]{2,1,0:T(8,128)S(1)}, f32[8,48,128]{2,1,0:T(8,128)S(1)}, u32[]{:S(2)}, u32[]{:S(2)}) collective-permute-start(f32[8,48,128]{2,1,0:T(8,128)S(1)} %get-tuple-element.75.part_right), channel_id=1, source_target_pairs={{0,4},{4,8},{8,12},{12,16},{16,20},{20,24},{24,28},{28,32},{32,36}... | collective-permute-start | bytes 589832 | tf_op jit(solution)/shard_map/ppermute | solution.py:728
  60.9 8.7 %collective-permute-start.9 = (f32[8,48,128]{2,1,0:T(8,128)S(1)}, f32[8,48,128]{2,1,0:T(8,128)S(1)}, u32[]{:S(2)}, u32[]{:S(2)}) collective-permute-start(f32[8,48,128]{2,1,0:T(8,128)S(1)} %get-tuple-element.74.part_left), channel_id=1, source_target_pairs={{4,0},{8,4},{12,8},{16,12},{20,16},{24,20},{28,24},{32,28},{36,32}... | collective-permute-start | bytes 589832 | tf_op jit(solution)/shard_map/ppermute | solution.py:729
  71.6 7.9 %collective-permute-start.10 = (f32[1,256]{1,0:T(1,128)S(1)}, f32[1,256]{1,0:T(1,128)S(1)}, u32[]{:S(2)}, u32[]{:S(2)}) collective-permute-start(f32[1,256]{1,0:T(1,128)S(1)} %get-tuple-element.79), channel_id=1, source_target_pairs={{0,1},{1,2},{2,3},{3,0},{4,5},{5,6},{6,7},{7,4},{8,9},{9,10},{10,1... | collective-permute-start | bytes 3080 | tf_op jit(solution)/shard_map/ppermute | solution.py:793
  77.2 3.9 %collective-permute-start.11 = (f32[1,256]{1,0:T(1,128)S(1)}, f32[1,256]{1,0:T(1,128)S(1)}, u32[]{:S(2)}, u32[]{:S(2)}) collective-permute-start(f32[1,256]{1,0:T(1,128)S(1)} %get-tuple-element.79), channel_id=1, source_target_pairs={{0,2},{1,3},{2,0},{3,1},{4,6},{5,7},{6,4},{7,5},{8,10},{9,11},{10,... | collective-permute-start | bytes 3080 | tf_op jit(solution)/shard_map/ppermute | solution.py:793
  77.7 4.5 %collective-permute-start.12 = (f32[1,256]{1,0:T(1,128)S(1)}, f32[1,256]{1,0:T(1,128)S(1)}, u32[]{:S(2)}, u32[]{:S(2)}) collective-permute-start(f32[1,256]{1,0:T(1,128)S(1)} %get-tuple-element.79), channel_id=1, source_target_pairs={{0,3},{1,0},{2,1},{3,2},{4,7},{5,4},{6,5},{7,6},{8,11},{9,8},{10,9... | collective-permute-start | bytes 3080 | tf_op jit(solution)/shard_map/ppermute | solution.py:793

commit v2 on v1

--- a/solution.py
+++ b/solution.py
@@ -2,7 +2,6 @@
 
 import jax
 import jax.numpy as jnp
-import numpy as np
 from jax import lax
 from jax.experimental import pallas as pl
 from jax.experimental.pallas import tpu as pltpu
@@ -13,6 +12,7 @@
 OWN = 32
 ROWS = OWN + 2 * HALO
 TALL = ROWS + 2 * PAD
+MID = OWN + HALO
 DEPTH = 128
 CHUNKS = ROWS // 8
 LABELS = 256
@@ -95,57 +95,56 @@
 
 def from_moments(first, diagonal, mixed, third, fourth, which):
     out = {}
-    for i in which:
-        v = VECTORS[i]
-        axes = [a for a in range(3) if v[a] != 0]
-        if not axes:
-            out[i] = (fourth[0, 1] + fourth[1, 2] + fourth[0, 2]) - (diagonal[0] + diagonal[1] + diagonal[2])
-        elif len(axes) == 1:
-            a = axes[0]
-            b, c = [k for k in range(3) if k != a]
-            even = diagonal[a] - fourth[tuple(sorted((a, b)))] - fourth[tuple(sorted((a, c)))]
-            odd = first[a] - third[a, b] - third[a, c]
-            out[i] = 0.5 * (even + odd if v[a] > 0 else even - odd)
-        else:
-            a, b = axes
-            value = fourth[a, b] + mixed[a, b] if v[a] * v[b] > 0 else fourth[a, b] - mixed[a, b]
-            value = value + third[a, b] if v[a] > 0 else value - third[a, b]
-            value = value + third[b, a] if v[b] > 0 else value - third[b, a]
-            out[i] = 0.25 * value
-    return out
-
-
-def rated(first, diagonal, mixed, third, fourth):
-    trace = TRACE * (diagonal[0] + diagonal[1] + diagonal[2])
-    return (
-        [SHEAR * m for m in first],
-        [SHEAR * m + trace for m in diagonal],
-        {k: SHEAR * m for k, m in mixed.items()},
-        {k: THIRD * m for k, m in third.items()},
-        {k: FOURTH * m for k, m in fourth.items()},
-    )
+    for a, b in PLANES:
+        even, cross = fourth[a, b] + mixed[a, b], fourth[a, b] - mixed[a, b]
+        odd, skew = third[a, b] + third[b, a], third[a, b] - third[b, a]
+        out[edge_index_of(a, b, 1, 1)] = even + odd
+        out[edge_index_of(a, b, -1, -1)] = even - odd
+        out[edge_index_of(a, b, 1, -1)] = cross + skew
+        out[edge_index_of(a, b, -1, 1)] = cross - skew
+    for a in range(3):
+        b, c = [k for k in range(3) if k != a]
+        even = diagonal[a] - 2.0 * (fourth[tuple(sorted((a, b)))] + fourth[tuple(sorted((a, c)))])
+        odd = first[a] - 2.0 * (third[a, b] + third[a, c])
+        out[axis_index_of(a, 1)] = even + odd
+        out[axis_index_of(a, -1)] = even - odd
+    out[0] = 4.0 * (fourth[0, 1] + fourth[1, 2] + fourth[0, 2]) - 2.0 * (diagonal[0] + diagonal[1] + diagonal[2])
+    return {i: out[i] for i in which}
 
 
 def linear_part(f, share, which):
     total, first, diagonal, mixed, third, fourth = moments(f)
-    change = from_moments(*rated(first, diagonal, mixed, third, fourth), which)
-    return total, first, {i: f[i] - share * change[i] for i in which}
+    half, quarter = (0.5 * SHEAR) * share, (0.25 * SHEAR) * share
+    trace = (0.5 * TRACE) * share * (diagonal[0] + diagonal[1] + diagonal[2])
+    by_third, by_fourth = (0.25 * THIRD) * share, (0.25 * FOURTH) * share
+    change = from_moments(
+        [half * m for m in first],
+        [half * m + trace for m in diagonal],
+        {k: quarter * m for k, m in mixed.items()},
+        {k: by_third * m for k, m in third.items()},
+        {k: by_fourth * m for k, m in fourth.items()},
+        which,
+    )
+    return total, first, {i: f[i] - change[i] for i in which}
 
 
 def balance_part(density, flow, velocity, share, which):
     d = density * share
     m = [flow[a] * share for a in range(3)]
     square = [m[a] * velocity[a] for a in range(3)]
-    diagonal = [d * (1.0 / 3.0) + square[a] for a in range(3)]
-    mixed = {(a, b): m[a] * velocity[b] for a, b in PLANES}
+    whole = square[0] + square[1] + square[2]
+    level = d * (SHEAR / 6.0 + 0.5 * TRACE) + whole * (0.5 * TRACE)
+    diagonal = [(0.5 * SHEAR) * square[a] + level for a in range(3)]
+    scaled = [(0.25 * SHEAR) * velocity[a] for a in range(3)]
+    mixed = {(a, b): m[a] * scaled[b] for a, b in PLANES}
+    part = [(THIRD / 12.0) * m[a] for a in range(3)]
     third = {}
     fourth = {}
+    level = d * (FOURTH / 36.0) + whole * (FOURTH / 12.0)
     for a, b in PLANES:
-        c = 3 - a - b
-        third[a, b] = m[a] * (1.0 / 3.0)
-        third[b, a] = m[b] * (1.0 / 3.0)
-        fourth[a, b] = d * (1.0 / 9.0) + (square[a] + square[b]) * (1.0 / 3.0) - square[c] * (1.0 / 6.0)
-    return from_moments(*rated(m, diagonal, mixed, third, fourth), which)
+        third[a, b], third[b, a] = part[a], part[b]
+        fourth[a, b] = level - (FOURTH / 8.0) * square[3 - a - b]
+    return from_moments([(0.5 * SHEAR) * m[a] for a in range(3)], diagonal, mixed, third, fourth, which)
 
 
 def dual(r):
@@ -258,6 +257,14 @@
     return rows_at(t, shift, PAD)
 
 
+def mid(t):
+    return pl.ds(t * 8 + (ROWS - MID) // 2, 8)
+
+
+def mid_tall(t, shift=0):
+    return pl.ds(t * 8 + ((ROWS - MID) // 2 + PAD + shift), 8)
+
+
 def each_chunk(body, first=0, last=CHUNKS):
     def step(t, carry):
         body(t)
@@ -279,7 +286,31 @@
     return 2.0 * x + rolled(x, 1) + rolled(x, -1)
 
 
-def edges_kernel(pops, fluid, label, target, low, high, whole, sems):
+def inner_gradient(field, doubled, here, inner, t):
+    at = lambda x, dy: field[x, tall(t, dy), :]
+    up, down = at(inner, 1), at(inner, -1)
+    along_x = doubled[inner, tall(t), :] + (up + down)
+    along_y = doubled[here, tall(t, 1), :] - doubled[here, tall(t, -1), :] + (up - down)
+    star = 2.0 * at(here, 0) + at(inner, 0) + at(here, 1) + at(here, -1)
+    return [along_x if inner > here else -along_x, along_y, rolled(star, -1) - rolled(star, 1)]
+
+
+def outer_gradient(field, doubled, p, inner, t):
+    at = lambda dy: field[inner, tall(t, dy), :]
+    up, down, here = at(1), at(-1), at(0)
+    along_x = doubled[inner, tall(t), :] + (up + down)
+    return [along_x if inner > p else -along_x, up - down, rolled(here, -1) - rolled(here, 1)]
+
+
+def send_flow(send_left, send_right, flow, field, doubled, t):
+    for send, here, inner in ((send_left, 0, 1), (send_right, 1, 0)):
+        push = field[here, tall(t), :] * (PULL / SHEAR)
+        pull = inner_gradient(field, doubled, here, inner, t)
+        for a in range(3):
+            send[5 + a, flat(t), :] = flow[a, here, flat(t), :] + push * pull[a]
+
+
+def edges_kernel(pops, fluid, label, target, table, low, high, small, whole, values, sems):
     copies = []
 
     def copy(source, goal):
@@ -287,38 +318,35 @@
         one.start()
         copies.append(one)
 
-    for side, goal in ((0, low), (1, high)):
-        rows = pl.ds(0, HALO) if side == 0 else pl.ds(OWN - HALO, HALO)
-        copy(fluid.at[:, rows, :], whole.at[side, 0])
-        copy(label.at[:, rows, :], whole.at[side, 1])
-        copy(target.at[:, rows, :], goal.at[21])
-        copy(pops.at[:, :, rows, :], goal.at[pl.ds(0, 19)])
+    copy(fluid, whole.at[0])
+    copy(label, whole.at[1])
+    copy(target, small.at[2])
+    copy(table, values)
+    copy(pops.at[:, :, pl.ds(0, HALO), :], low.at[pl.ds(0, 19)])
+    copy(pops.at[:, :, pl.ds(OWN - HALO, HALO), :], high.at[pl.ds(0, 19)])
     for one in copies:
         one.wait()
-    for side, goal in ((0, low), (1, high)):
-        goal[19] = whole[side, 0].astype(jnp.float32)
-        goal[20] = whole[side, 1].astype(jnp.float32)
-
-
-def put_sends(send_left, send_right, t, lin, first, chosen, effective):
+    small[0] = whole[0].astype(jnp.float32)
+    small[1] = whole[1].astype(jnp.float32)
+    small[3, 0, 0:2, :] = values[...]
+    low[19:22] = small[0:3, :, 0:HALO, :]
+    high[19:22] = small[0:3, :, OWN - HALO : OWN, :]
+
+
+def put_sends(send_left, send_right, t, lin, chosen):
     for k, i in enumerate(LEFTWARD):
         send_left[k, flat(t), :] = lin[0][i]
     for k, i in enumerate(RIGHTWARD):
         send_right[k, flat(t), :] = lin[1][i]
-    for a in range(3):
-        send_left[5 + a, flat(t), :] = first[0][a]
-        send_right[5 + a, flat(t), :] = first[1][a]
     send_left[8, flat(t), :] = chosen[0]
     send_right[8, flat(t), :] = chosen[1]
-    send_left[9, flat(t), :] = effective[1]
-    send_right[9, flat(t), :] = effective[0]
 
 
 def start_rows(t, populations, shares, marks, table, outs):
     lin_out, flow_out, density_out, effective_out, share_out, _, send_left, send_right = outs
     half_low = jnp.broadcast_to(table[0:1, :], (8, DEPTH))
     half_high = jnp.broadcast_to(table[1:2, :], (8, DEPTH))
-    lin, first, chosen, effective = [], [], [], []
+    lin, chosen = [], []
     for x in range(2):
         share = shares[x]
         spot = jnp.bitwise_and(marks[x], DEPTH - 1)
@@ -328,44 +356,49 @@
             jnp.take_along_axis(half_high, spot, axis=1),
         )
         total, momentum, linear = linear_part(populations[x], share, range(19))
-        eff = jnp.where(share > 0, 1.0 - jnp.exp(-total), wall)
         for i in range(19):
             lin_out[i, x, flat(t), :] = linear[i]
         for a in range(3):
             flow_out[a, x, flat(t), :] = momentum[a]
         density_out[x, flat(t), :] = total
-        effective_out[x, flat(t), :] = eff
+        effective_out[x, flat(t), :] = jnp.where(share > 0, 1.0 - jnp.exp(-total), wall)
         share_out[x, flat(t), :] = share
         lin.append(linear)
-        first.append(momentum)
         chosen.append(jnp.where(share > 0, total, wall))
-        effective.append(eff)
-    put_sends(send_left, send_right, t, lin, first, chosen, effective)
-    send_left[10, flat(t), :] = shares[0]
-    send_left[11, flat(t), :] = shares[1]
-    send_right[10, flat(t), :] = shares[1]
-    send_right[11, flat(t), :] = shares[0]
-
-
-def own_kernel(pops, fluid, label, target, table, *outs):
-    outs[5][:, HALO : HALO + OWN, :] = target[...]
+    put_sends(send_left, send_right, t, lin, chosen)
+    send_left[9, flat(t), :] = shares[0]
+    send_right[9, flat(t), :] = shares[1]
+
+
+def own_kernel(pops, small, *refs):
+    outs, chooser, turned_label = refs[:8], refs[8], refs[9]
+    outs[5][:, HALO : HALO + OWN, :] = small[2]
 
     def body(t):
         rows = rows_at(t, 0, -HALO)
         start_rows(
             t,
             [{i: pops[i, x, rows, :] for i in range(19)} for x in range(2)],
-            [fluid[x, rows, :].astype(jnp.float32) for x in range(2)],
-            [label[x, rows, :] for x in range(2)],
-            table,
+            [small[0, x, rows, :] for x in range(2)],
+            [small[1, x, rows, :].astype(jnp.int32) for x in range(2)],
+            small[3, 0, 0:2, :],
             outs,
         )
 
     each_chunk(body, HALO // 8, (HALO + OWN) // 8)
 
-
-def halo_kernel(table, below, above, *refs):
-    outs = refs[len(refs) // 2 :]
+    marks = jnp.bitwise_and(small[1, 0].astype(jnp.int32), LABELS - 1).astype(jnp.float32)
+    turned_label[...] = jnp.transpose(marks)
+    quads = DEPTH // 4
+    by_quad = turned_label[pl.ds(0, quads, stride=4), :]
+    names = lax.broadcasted_iota(jnp.int32, (quads, LABELS), 1).astype(jnp.float32)
+    for k in range(OWN // 2):
+        column = jnp.broadcast_to(by_quad[:, 2 * k : 2 * k + 1], (quads, LABELS))
+        chooser[quads * k : quads * (k + 1), :] = (column == names).astype(jnp.bfloat16)
+
+
+def halo_kernel(small, below, above, *refs):
+    outs, field, doubled = refs[8:16], refs[16], refs[17]
     for t, edge in ((0, below), (CHUNKS - 1, above)):
         outs[5][:, 8 * t : 8 * t + 8, :] = edge[21]
         start_rows(
@@ -373,21 +406,30 @@
             [{i: edge[i, x] for i in range(19)} for x in range(2)],
             [edge[19, x] for x in range(2)],
             [edge[20, x].astype(jnp.int32) for x in range(2)],
-            table,
+            small[3, 0, 0:2, :],
             outs,
         )
+    flow, effective, send_left, send_right = outs[1], outs[3], outs[6], outs[7]
+
+    def place(t):
+        for x in range(2):
+            value = effective[x, flat(t), :]
+            field[x, tall(t), :] = value
+            doubled[x, tall(t), :] = with_sides(value)
+
+    each_chunk(place)
+    each_chunk(functools.partial(send_flow, send_left, send_right, flow, field, doubled))
 
 
 def step_kernel(is_first, *refs):
     if is_first:
         (lin, flow, density, effective, share, from_left, from_right,
          masks, field, speed, pull_out, lin_out, flow_out, density_out, effective_out, send_left, send_right,
-         doubled, relaxed, turned) = refs
+         doubled, relaxed, turned, next_field, next_doubled) = refs
     else:
         (lin, flow, density, effective, share, target, masks, from_left, from_right,
-         field, speed, pull_out, misfit_out,
+         field, speed, pull_out, misfit_out, send_left, send_right,
          doubled, relaxed, turned) = refs
-    sides = ((1, from_left, 0), (4, from_right, 5))
 
     def place(t):
         def put(p, x, s):
@@ -400,24 +442,19 @@
 
         for x in range(2):
             put(2 + x, effective[x, flat(t), :], share[x, flat(t), :])
-        for near, come, far in sides:
-            if is_first:
-                s_near, s_far = come[10, flat(t), :], come[11, flat(t), :]
-            else:
-                s_near, s_far = masks[0, near, tall(t), :], None
+        for near, come in ((1, from_left), (4, from_right)):
+            s = come[9, flat(t), :] if is_first else masks[0, near, tall(t), :]
             chosen = come[8, flat(t), :]
-            put(near, jnp.where(s_near > 0, 1.0 - jnp.exp(-chosen), chosen), s_near)
-            put(far, come[9, flat(t), :], s_far)
+            put(near, jnp.where(s > 0, 1.0 - jnp.exp(-chosen), chosen), s)
 
     each_chunk(place)
 
     def collide(t):
         for p in range(1, 5):
-            own = p in (2, 3)
-            pull = gradient_of(field, doubled, p, t)
             psi = field[p, tall(t), :]
             s = masks[0, p, tall(t), :]
-            if own:
+            if p in (2, 3):
+                pull = gradient_of(field, doubled, p, t)
                 rho = density[p - 2, flat(t), :]
                 mom = [flow[a, p - 2, flat(t), :] for a in range(3)]
                 which = range(19)
@@ -425,6 +462,7 @@
                 for a in range(3):
                     pull_out[a, p - 2, flat(t), :] = pull[a]
             else:
+                pull = outer_gradient(field, doubled, p, 2 if p == 1 else 3, t)
                 come = from_left if p == 1 else from_right
                 rho = come[8, flat(t), :]
                 mom = [come[5 + a, flat(t), :] for a in range(3)]
@@ -445,48 +483,57 @@
 
     each_chunk(collide)
 
+    def streamed(x, rows):
+        f = {0: relaxed[0, 1 + x, rows(0), :]}
+        for i in range(1, 19):
+            cx, cy, cz = VECTORS[i]
+            if cz:
+                source = turned[TURNED.index(i), 1 + x - cx, rows(-cy), :]
+            else:
+                source = relaxed[i, 1 + x - cx, rows(-cy), :]
+            open_ = masks[cz % 3, 2 + x - cx, rows(-cy), :] > 0
+            f[i] = jnp.where(open_, source, relaxed[OPPOSITE[i], 1 + x, rows(0), :])
+        return f
+
     def stream(t):
-        lin_sent, first_sent, chosen_sent, effective_sent = [], [], [], []
+        lin_sent, chosen_sent = [], []
         for x in range(2):
-            f = {}
+            s = share[x, flat(t), :]
+            total, momentum, linear = linear_part(streamed(x, lambda dy: tall(t, dy)), s, range(19))
+            held = effective[x, flat(t), :]
+            eff = jnp.where(s > 0, 1.0 - jnp.exp(-total), held)
             for i in range(19):
-                cx, cy, cz = VECTORS[i]
-                if i == 0:
-                    f[i] = relaxed[0, 1 + x, tall(t), :]
-                    continue
-                if cz:
-                    source = turned[TURNED.index(i), 1 + x - cx, tall(t, -cy), :]
-                else:
-                    source = relaxed[i, 1 + x - cx, tall(t, -cy), :]
-                open_ = masks[cz % 3, 2 + x - cx, tall(t, -cy), :] > 0
-                f[i] = jnp.where(open_, source, relaxed[OPPOSITE[i], 1 + x, tall(t), :])
-            s = share[x, flat(t), :]
-            if is_first:
-                total, momentum, linear = linear_part(f, s, range(19))
-                held = effective[x, flat(t), :]
-                eff = jnp.where(s > 0, 1.0 - jnp.exp(-total), held)
-                for i in range(19):
-                    lin_out[i, x, flat(t), :] = linear[i]
-                for a in range(3):
-                    flow_out[a, x, flat(t), :] = momentum[a]
-                density_out[x, flat(t), :] = total
-                effective_out[x, flat(t), :] = eff
-                lin_sent.append(linear)
-                first_sent.append(momentum)
-                chosen_sent.append(jnp.where(s > 0, total, held))
-                effective_sent.append(eff)
-            else:
-                total = add(*[f[i] for i in range(19)])
-                misfit_out[x, flat(t), :] = s * (total - target[x, flat(t), :])
-        if is_first:
-            put_sends(send_left, send_right, t, lin_sent, first_sent, chosen_sent, effective_sent)
-
-    each_chunk(stream)
-
-
-def spread_of(pulled, pulled_doubled, p, t):
-    at = lambda a, dp, dy: pulled[a, p + dp, tall(t, dy), :]
-    two = lambda a, dp, dy: pulled_doubled[a, p + dp, tall(t, dy), :]
+                lin_out[i, x, flat(t), :] = linear[i]
+            for a in range(3):
+                flow_out[a, x, flat(t), :] = momentum[a]
+            density_out[x, flat(t), :] = total
+            effective_out[x, flat(t), :] = eff
+            next_field[x, tall(t), :] = eff
+            next_doubled[x, tall(t), :] = with_sides(eff)
+            lin_sent.append(linear)
+            chosen_sent.append(jnp.where(s > 0, total, held))
+        put_sends(send_left, send_right, t, lin_sent, chosen_sent)
+
+    def compare(t):
+        for x, near, far in ((0, send_left, send_right), (1, send_right, send_left)):
+            f = streamed(x, lambda dy: mid_tall(t, dy))
+            s = share[x, mid(t), :]
+            misfit = s * (add(*[f[i] for i in range(19)]) - target[x, mid(t), :])
+            misfit_out[x, flat(t), :] = misfit
+            near[0, flat(t), :] = misfit
+            far[1, flat(t), :] = misfit
+            far[2, flat(t), :] = s
+
+    if is_first:
+        each_chunk(stream)
+        each_chunk(functools.partial(send_flow, send_left, send_right, flow_out, next_field, next_doubled))
+    else:
+        each_chunk(compare, 0, MID // 8)
+
+
+def spread_of(pulled, pulled_doubled, p, rows):
+    at = lambda a, dp, dy: pulled[a, p + dp, rows(dy), :]
+    two = lambda a, dp, dy: pulled_doubled[a, p + dp, rows(dy), :]
     along_x = two(0, 1, 0) - two(0, -1, 0) + (at(0, 1, 1) + at(0, 1, -1)) - (at(0, -1, 1) + at(0, -1, -1))
     along_y = two(1, 0, 1) - two(1, 0, -1) + (at(1, 1, 1) + at(1, -1, 1)) - (at(1, 1, -1) + at(1, -1, -1))
     star = 2.0 * at(2, 0, 0) + at(2, 1, 0) + at(2, -1, 0) + at(2, 0, 1) + at(2, 0, -1)
@@ -494,116 +541,131 @@
     return (along_x + along_y + along_z) * (-1.0 / 36.0)
 
 
-def put_pulled(pulled, pulled_doubled, p, t, psi, q):
+def put_pulled(pulled, pulled_doubled, p, rows, psi, q):
     for a in range(3):
         s = (COUPLING / SHEAR) * psi * q[a]
-        pulled[a, p, tall(t), :] = s
+        pulled[a, p, rows(0), :] = s
         if a < 2:
-            pulled_doubled[a, p, tall(t), :] = with_sides(s)
-
-
-def mask_ahead(masks, i, p, t):
+            pulled_doubled[a, p, rows(0), :] = with_sides(s)
+
+
+def mask_ahead(masks, i, p, rows):
     cx, cy, cz = VECTORS[i]
-    return masks[(-cz) % 3, p + cx, tall(t, cy), :] > 0
+    return masks[(-cz) % 3, p + cx, rows(cy), :] > 0
+
+
+def middle(t):
+    return lambda dy: mid_tall(t, dy)
 
 
 def last_reverse_kernel(
     misfit, from_left, from_right, masks, field, speed, pull, early_speed,
     adjoint, turned, wall_out, send_left, send_right,
-    ahead, pulled, pulled_doubled, base,
+    ahead, far_masks, pulled, pulled_doubled, base,
 ):
     def place(t):
+        rows = middle(t)
         for p in range(6):
             if p < 2:
-                d = from_left[p, flat(t), :]
+                d = from_left[1 - p, flat(t), :]
             elif p < 4:
                 d = misfit[p - 2, flat(t), :]
             else:
                 d = from_right[p - 4, flat(t), :]
-            ahead[0, p, tall(t), :] = d
-            ahead[1, p, tall(t), :] = rolled(d, 1)
-            ahead[2, p, tall(t), :] = rolled(d, -1)
-
-    each_chunk(place)
+            ahead[0, p, rows(0), :] = d
+            ahead[1, p, rows(0), :] = rolled(d, 1)
+            ahead[2, p, rows(0), :] = rolled(d, -1)
+        for k, source in enumerate((from_left, from_right)):
+            s = source[2, flat(t), :]
+            far_masks[0, k, rows(0), :] = s
+            far_masks[1, k, rows(0), :] = rolled(s, 1)
+            far_masks[2, k, rows(0), :] = rolled(s, -1)
+
+    each_chunk(place, 0, MID // 8)
 
     def collide(t):
+        rows = middle(t)
         for p in range(1, 5):
-            s = masks[0, p, tall(t), :]
-            here = ahead[0, p, tall(t), :]
+            s = masks[0, p, rows(0), :]
+            here = ahead[0, p, rows(0), :]
             r = {0: here}
             for i in range(1, 19):
                 cx, cy, cz = VECTORS[i]
-                there = ahead[(-cz) % 3, p + cx, tall(t, cy), :]
-                r[i] = s * jnp.where(mask_ahead(masks, i, p, t), there, here)
-            psi = field[p, tall(t), :]
-            u = [speed[a, p - 1, flat(t), :] for a in range(3)]
+                there = ahead[(-cz) % 3, p + cx, rows(cy), :]
+                if p + cx in (0, 5):
+                    open_ = far_masks[(-cz) % 3, (p + cx) // 5, rows(cy), :] > 0
+                else:
+                    open_ = mask_ahead(masks, i, p, rows)
+                r[i] = s * jnp.where(open_, there, here)
+            psi = field[p, rows(0), :]
+            u = [speed[a, p - 1, mid(t), :] for a in range(3)]
             if p in (2, 3):
                 rest, by_density, q = collide_adjoint(r, u)
-                along = add(*[q[a] * pull[a, p - 2, flat(t), :] for a in range(3)])
+                along = add(*[q[a] * pull[a, p - 2, mid(t), :] for a in range(3)])
                 const = by_density + along * ((PULL / SHEAR) * (1.0 - psi))
                 for i in range(19):
                     base[i, p - 2, flat(t), :] = rest[i] + const
             else:
                 q = flow_adjoint(*dual(r), u)
-            put_pulled(pulled, pulled_doubled, p - 1, t, psi, q)
-
-    each_chunk(collide)
+            put_pulled(pulled, pulled_doubled, p - 1, rows, psi, q)
+
+    each_chunk(collide, 0, MID // 8)
 
     def finish(t):
+        rows = middle(t)
         for x in range(2):
-            s = masks[0, 2 + x, tall(t), :]
-            spread = spread_of(pulled, pulled_doubled, 1 + x, t)
+            s = masks[0, 2 + x, rows(0), :]
+            spread = spread_of(pulled, pulled_doubled, 1 + x, rows)
             wall_out[x, flat(t), :] = (1.0 - s) * spread
-            more = s * spread * (1.0 - field[2 + x, tall(t), :])
+            more = s * spread * (1.0 - field[2 + x, rows(0), :])
             for i in range(19):
                 value = base[i, x, flat(t), :] + more
-                adjoint[i, x, tall(t), :] = value
+                adjoint[i, x, rows(0), :] = value
                 if i in TURNED:
-                    turned[TURNED.index(i), x, tall(t), :] = rolled(value, -VECTORS[i][2])
-
-    each_chunk(finish)
+                    turned[TURNED.index(i), x, rows(0), :] = rolled(value, -VECTORS[i][2])
+
+    each_chunk(finish, 0, MID // 8)
 
     def part(t):
+        rows = middle(t)
         for x, send, sent, skipped in ((0, send_left, RIGHTWARD, -1), (1, send_right, LEFTWARD, 1)):
             p = 2 + x
-            s = masks[0, p, tall(t), :]
+            s = masks[0, p, rows(0), :]
             r = {}
             for i in range(19):
-                cx, cy, cz = VECTORS[i]
-                if cx == skipped:
-                    continue
-                r[i] = adjoint_ahead(adjoint, turned, masks, i, x, t)
-            u = [early_speed[a, p - 1, flat(t), :] for a in range(3)]
+                if VECTORS[i][0] != skipped:
+                    r[i] = adjoint_ahead(adjoint, turned, masks, i, x, rows)
+            u = [early_speed[a, p - 1, mid(t), :] for a in range(3)]
             q = flow_adjoint(*dual(r), u)
             for a in range(3):
                 send[5 + a, flat(t), :] = s * q[a]
             for k, i in enumerate(sent):
-                send[k, flat(t), :] = adjoint[i, x, tall(t), :]
-
-    each_chunk(part)
-
-
-def adjoint_ahead(adjoint, turned, masks, i, x, t):
+                send[k, flat(t), :] = adjoint[i, x, rows(0), :]
+
+    each_chunk(part, 0, MID // 8)
+
+
+def adjoint_ahead(adjoint, turned, masks, i, x, rows):
     cx, cy, cz = VECTORS[i]
     if i == 0:
-        return adjoint[0, x, tall(t), :]
+        return adjoint[0, x, rows(0), :]
     if cz:
-        there = turned[TURNED.index(i), x + cx, tall(t, cy), :]
+        there = turned[TURNED.index(i), x + cx, rows(cy), :]
     else:
-        there = adjoint[i, x + cx, tall(t, cy), :]
-    return jnp.where(mask_ahead(masks, i, 2 + x, t), there, adjoint[OPPOSITE[i], x, tall(t), :])
+        there = adjoint[i, x + cx, rows(cy), :]
+    return jnp.where(mask_ahead(masks, i, 2 + x, rows), there, adjoint[OPPOSITE[i], x, rows(0), :])
 
 
 def place_sides(come, from_left, from_right, t):
     for side, source, which in ((0, from_left, LEFTWARD), (1, from_right, RIGHTWARD)):
         for k, i in enumerate(which):
-            come[side, k, tall(t), :] = rolled(source[k, flat(t), :], -VECTORS[i][2])
-
-
-def arrived(come, adjoint, masks, i, x, t):
+            come[side, k, mid_tall(t), :] = rolled(source[k, flat(t), :], -VECTORS[i][2])
+
+
+def arrived(come, adjoint, masks, i, x, rows):
     which = LEFTWARD if x == 0 else RIGHTWARD
-    there = come[x, which.index(i), tall(t, VECTORS[i][1]), :]
-    return jnp.where(mask_ahead(masks, i, 2 + x, t), there, adjoint[OPPOSITE[i], x, tall(t), :])
+    there = come[x, which.index(i), rows(VECTORS[i][1]), :]
+    return jnp.where(mask_ahead(masks, i, 2 + x, rows), there, adjoint[OPPOSITE[i], x, rows(0), :])
 
 
 def wall_kernel(
@@ -611,42 +673,44 @@
     more_out, label_part,
     come, pulled, pulled_doubled, totals,
 ):
-    each_chunk(functools.partial(place_sides, come, from_left, from_right))
+    each_chunk(functools.partial(place_sides, come, from_left, from_right), 0, MID // 8)
 
     def collide(t):
+        rows = middle(t)
         for x, part, which in ((0, part_left, LEFTWARD), (1, part_right, RIGHTWARD)):
             p = 2 + x
-            s = masks[0, p, tall(t), :]
-            r = {i: arrived(come, adjoint, masks, i, x, t) for i in which}
-            u = [speed[a, p - 1, flat(t), :] for a in range(3)]
+            s = masks[0, p, rows(0), :]
+            r = {i: arrived(come, adjoint, masks, i, x, rows) for i in which}
+            u = [speed[a, p - 1, mid(t), :] for a in range(3)]
             rest = flow_adjoint(*dual(r), u)
             q = [part[5 + a, flat(t), :] + s * rest[a] for a in range(3)]
-            put_pulled(pulled, pulled_doubled, p - 1, t, field[p, tall(t), :], q)
+            put_pulled(pulled, pulled_doubled, p - 1, rows, field[p, rows(0), :], q)
         for x, source, which in ((0, from_left, LEFTWARD), (1, from_right, RIGHTWARD)):
             p = 1 if x == 0 else 4
-            s = masks[0, p, tall(t), :]
+            s = masks[0, p, rows(0), :]
             r = {}
             for i in [OPPOSITE[j] for j in which]:
                 cx, cy, cz = VECTORS[i]
                 if cz:
-                    there = turned[TURNED.index(i), x, tall(t, cy), :]
+                    there = turned[TURNED.index(i), x, rows(cy), :]
                 else:
-                    there = adjoint[i, x, tall(t, cy), :]
+                    there = adjoint[i, x, rows(cy), :]
                 here = source[which.index(OPPOSITE[i]), flat(t), :]
-                r[i] = jnp.where(mask_ahead(masks, i, p, t), there, here)
-            u = [speed[a, p - 1, flat(t), :] for a in range(3)]
+                r[i] = jnp.where(mask_ahead(masks, i, p, rows), there, here)
+            u = [speed[a, p - 1, mid(t), :] for a in range(3)]
             rest = flow_adjoint(*dual(r), u)
             q = [source[5 + a, flat(t), :] + s * rest[a] for a in range(3)]
-            put_pulled(pulled, pulled_doubled, p - 1, t, field[p, tall(t), :], q)
-
-    each_chunk(collide)
+            put_pulled(pulled, pulled_doubled, p - 1, rows, field[p, rows(0), :], q)
+
+    each_chunk(collide, 0, MID // 8)
 
     def finish(t):
         total = None
         for x in range(2):
             s = masks[0, 2 + x, tall(t), :]
-            spread = spread_of(pulled, pulled_doubled, 1 + x, t)
-            total = add(total, (1.0 - s) * spread + wall[x, flat(t), :])
+            spread = spread_of(pulled, pulled_doubled, 1 + x, lambda dy: tall(t, dy))
+            step_wall = wall[x, pl.ds(t * 8 - (ROWS - MID) // 2, 8), :]
+            total = add(total, (1.0 - s) * spread + step_wall)
             more_out[x, rows_at(t, 0, -HALO), :] = s * spread * (1.0 - field[2 + x, tall(t), :])
         totals[rows_at(t, 0, -HALO), :] = total
 
@@ -669,18 +733,19 @@
     grad,
     come,
 ):
-    each_chunk(functools.partial(place_sides, come, from_left, from_right))
+    each_chunk(functools.partial(place_sides, come, from_left, from_right), 0, MID // 8)
 
     def collide(t):
+        rows = lambda dy: tall(t, dy)
         for x in range(2):
             p = 2 + x
             s = masks[0, p, tall(t), :]
             r = {}
             for i in range(19):
                 if VECTORS[i][0] == 2 * x - 1:
-                    r[i] = s * arrived(come, adjoint, masks, i, x, t)
+                    r[i] = s * arrived(come, adjoint, masks, i, x, rows)
                 else:
-                    r[i] = s * adjoint_ahead(adjoint, turned, masks, i, x, t)
+                    r[i] = s * adjoint_ahead(adjoint, turned, masks, i, x, rows)
             u = [speed[a, p - 1, flat(t), :] for a in range(3)]
             rest, by_density, q = collide_adjoint(r, u)
             along = add(*[q[a] * pull[a, x, flat(t), :] for a in range(3)])
@@ -704,10 +769,10 @@
 def call(kernel, args, outs, scratch, anywhere=0, grant=12, filled=0):
     whole = pl.BlockSpec(memory_space=pltpu.VMEM)
     there = pl.BlockSpec(memory_space=pl.ANY)
-    size = 4 * sum(int(np.prod(s)) for s in outs) + sum(a.size * a.dtype.itemsize for a in args)
+    size = sum(a.size * a.dtype.itemsize for a in args)
     return pl.pallas_call(
         kernel,
-        out_shape=[jax.ShapeDtypeStruct(s, jnp.float32) for s in outs],
+        out_shape=[s if hasattr(s, "dtype") else jax.ShapeDtypeStruct(s, jnp.float32) for s in outs],
         in_specs=[there] * anywhere + [whole] * (len(args) - anywhere),
         out_specs=[whole] * len(outs),
         scratch_shapes=scratch,
@@ -735,22 +800,30 @@
     plane = (ROWS, DEPTH)
     two = (2, *plane)
     edge = (22, 2, HALO, DEPTH)
-    low, high = call(
+    low, high, small = call(
         edges_kernel,
-        (populations, fluid, label, target),
-        (edge, edge),
-        (pltpu.VMEM((2, 2, 2, HALO, DEPTH), jnp.int32), pltpu.SemaphoreType.DMA((8,))),
-        anywhere=4,
+        (populations, fluid, label, target, wall_wetting.reshape(2, DEPTH)),
+        (edge, edge, (4, 2, OWN, DEPTH)),
+        (
+            pltpu.VMEM((2, 2, OWN, DEPTH), jnp.int32),
+            vmem(2, DEPTH),
+            pltpu.SemaphoreType.DMA((6,)),
+        ),
+        anywhere=5,
         grant=56,
     )
     below, above = both_ways(low, high, "gy")
-    marks = jnp.bitwise_and(label[0, ::2, ::4], LABELS - 1).reshape(-1)
-    chooser = (marks[:, None] == jnp.arange(LABELS, dtype=jnp.int32)[None, :]).astype(jnp.bfloat16)
-    table = wall_wetting.reshape(2, DEPTH)
-    started = ((19, *two), (3, *two), two, two, two, two, (12, *plane), (12, *plane))
-    own = call(own_kernel, (populations, fluid, label, target, table), started, ())
+    blocks = (OWN // 2) * (DEPTH // 4)
+    started = ((19, *two), (3, *two), two, two, two, two, (10, *plane), (10, *plane))
+    *own, chooser = call(
+        own_kernel,
+        (populations, small),
+        (*started, jax.ShapeDtypeStruct((blocks, LABELS), jnp.bfloat16)),
+        (vmem(DEPTH, OWN),),
+    )
+    beside = (vmem(2, TALL, DEPTH), vmem(2, TALL, DEPTH))
     lin, flow, density, effective, share, target_wide, to_left, to_right = call(
-        halo_kernel, (table, below, above, *own), started, (), filled=len(started)
+        halo_kernel, (small, below, above, *own), started, beside, filled=len(started)
     )
     from_left, from_right = both_ways(to_left, to_right, "gx")
     wide6 = (6, TALL, DEPTH)
@@ -760,24 +833,25 @@
         (lin, flow, density, effective, share, from_left, from_right),
         (
             (3, *wide6), wide6, (3, 4, *plane), (3, *two),
-            (19, *two), (3, *two), two, two, (10, *plane), (10, *plane),
+            (19, *two), (3, *two), two, two, (9, *plane), (9, *plane),
         ),
-        work,
+        (*work, *beside),
     )
     from_left, from_right = both_ways(to_left, to_right, "gx")
-    field1, speed1, pull1, misfit = call(
+    less = (MID, DEPTH)
+    field1, speed1, pull1, misfit, to_left, to_right = call(
         functools.partial(step_kernel, False),
         (lin, flow, density, effective, share, target_wide, masks, from_left, from_right),
-        (wide6, (3, 4, *plane), (3, *two), two),
+        (wide6, (3, 4, *plane), (3, *two), (2, *less), (3, *less), (3, *less)),
         work,
     )
-    from_left, from_right = both_ways(misfit, misfit, "gx")
+    from_left, from_right = both_ways(to_left, to_right, "gx")
     pulled = (vmem(3, 4, TALL, DEPTH), vmem(2, 4, TALL, DEPTH))
     adjoint, turned, wall, to_left, to_right = call(
         last_reverse_kernel,
         (misfit, from_left, from_right, masks, field1, speed1, pull1, speed0),
-        ((19, 2, TALL, DEPTH), (10, 2, TALL, DEPTH), two, (8, *plane), (8, *plane)),
-        (vmem(3, *wide6), *pulled, vmem(19, *two)),
+        ((19, 2, TALL, DEPTH), (10, 2, TALL, DEPTH), (2, *less), (8, *less), (8, *less)),
+        (vmem(3, *wide6), vmem(3, 2, TALL, DEPTH), *pulled, vmem(19, 2, *less)),
     )
     from_left, from_right = both_ways(to_left, to_right, "gx")
     come = vmem(2, 5, TALL, DEPTH)

time: 83.4 us -> 79.4 us (0.952)
  local copies, waits for them, and re-layouts: 7.77 us -> 1.98 us
  waiting for transfers between devices: 21.5 us -> 24.7 us
  Pallas kernels: 16.2 us -> 14.7 us
    unnamed x18 -> x4, local copies, waits for them, and re-layouts: 6.85 us -> 1.98 us
    ppermute x5, waiting for transfers between devices: 2.45 us -> 6.32 us  [both_ways(): from_upper = lax.ppermute(to_lower, axis, down)]
    ppermute x3, waiting for transfers between devices: 2.7 us -> 0.01 us  [per_device(): lax.ppermute(label_part, 'gy', [(i, (i + step) % count) for i in range(co...]
    ppermute x5, waiting for transfers between devices: 16.3 us -> 18.4 us  [both_ways(): from_lower = lax.ppermute(to_upper, axis, up)]
    pallas_call x8, Pallas kernels: 16.2 us -> 14.7 us  [call(): pl.pallas_call(kernel, out_shape=[s if hasattr(s, 'dtype') else jax.Shape...]
    slice x1 -> x0, local copies, waits for them, and re-layouts: 0.84 us -> none  [per_device(): marks = jnp.bitwise_and(label[0, ::2, ::4], LABELS - 1).reshape(-1)]
  transfers between devices with their start and end apart: 13 -> 13, of which waited for: 7 -> 7; matrix products, arithmetic and copies ran while one was open for 1% -> 0% of each run, Pallas kernels for 3% -> 3%
where the time goes in v2:
time: 79.4 us; the launch traced here: 79.2 us
  starting transfers between devices  36.5 us (46%)
  waiting for transfers between devices  24.7 us (31%)
  Pallas kernels  14.7 us (19%)
  local copies, waits for them, and re-layouts  1.98 us (2%)
    ppermute x5, starting transfers between devices, both_ways(): from_upper = lax.ppermute(to_lower, axis, down)  24.6 us
    ppermute x5, waiting for transfers between devices, both_ways(): from_lower = lax.ppermute(to_upper, axis, up)  18.4 us
    pallas_call x8, Pallas kernels, call(): pl.pallas_call(kernel, out_shape=[s if hasattr(s, 'dtype') else jax.Shape...  14.7 us
    ppermute x3, starting transfers between devices, per_device(): lax.ppermute(label_part, 'gy', [(i, (i + step) % count) for i in range(co...  6.33 us
    ppermute x5, waiting for transfers between devices, both_ways(): from_upper = lax.ppermute(to_lower, axis, down)  6.32 us
    ppermute x5, starting transfers between devices, both_ways(): from_lower = lax.ppermute(to_upper, axis, up)  5.56 us
    unnamed x4, local copies, waits for them, and re-layouts  1.98 us
  transfers between devices with their start and end apart: 13, of which 7 were waited for; matrix products, arithmetic and copies ran while one was open for 0% of the time, Pallas kernels for 3%

profile of v2, /device:TPU:1, one launch (start us, length us, event | category | flops | bytes accessed | tf_op | source)
XLA Modules:
  0.0 79.2 jit_solution(12895778015649034060)
XLA Ops:
  0.6 1.9 %shard_map.68 = (f32[22,2,8,128]{3,2,1,0:T(8,128)}, f32[22,2,8,128]{3,2,1,0:T(8,128)}, f32[4,2,32,128]{3,2,1,0:T(8,128)}) custom-call(f32[19,2,32,128]{3,2,1,0:T(8,128)} %pops.3, s32[2,32,128]{2,1,0:T(8,128)} %fluid.1, s32[2,32,128]{2,1,0:T(8,128)} %label.1, f32[2,32,128]{2,1,0:T(8,128)} %target.1, f32[2,128]{1,0:T(2,128)} %bitcast.2), custom_call_target="tpu_custom_call" | custom-call | bytes 721920 | tf_op jit(solution)/shard_map/pallas_call | solution.py:773
  2.5 4.4 %collective-permute-start = (f32[22,2,8,128]{3,2,1,0:T(8,128)}, f32[22,2,8,128]{3,2,1,0:T(8,128)S(1)}, u32[]{:S(2)}, u32[]{:S(2)}) collective-permute-start(f32[22,2,8,128]{3,2,1,0:T(8,128)} %get-tuple-element.46), channel_id=1, source_target_pairs={{0,1},{1,2},{2,3},{3,0},{4,5},{5,6},{6,7},{7,4},{8,9},{9,10},{10,1... | collective-permute-start | bytes 540680 | tf_op jit(solution)/shard_map/ppermute | solution.py:793
  6.9 0.0 collective-permute-start.1
  6.9 0.0 copy-start
  6.9 1.1 %copy-done = f32[19,2,32,128]{3,2,1,0:T(8,128)S(1)} copy-done((f32[19,2,32,128]{3,2,1,0:T(8,128)S(1)}, f32[19,2,32,128]{3,2,1,0:T(8,128)}, u32[]{:S(2)}) %copy-start) | copy-done | bytes 622616
  8.0 0.0 copy-start.1
  8.0 0.9 %copy-done.1 = f32[4,2,32,128]{3,2,1,0:T(8,128)S(1)} copy-done((f32[4,2,32,128]{3,2,1,0:T(8,128)S(1)}, f32[4,2,32,128]{3,2,1,0:T(8,128)}, u32[]{:S(2)}) %copy-start.1) | copy-done | bytes 131096
  8.9 0.6 shard_map.69
  9.5 0.2 collective-permute-done.below
  9.7 4.1 %collective-permute-done.1.above = f32[22,2,8,128]{3,2,1,0:T(8,128)S(1)} collective-permute-done((f32[22,2,8,128]{3,2,1,0:T(8,128)}, f32[22,2,8,128]{3,2,1,0:T(8,128)S(1)}, u32[]{:S(2)}, u32[]{:S(2)}) %collective-permute-start.1) | collective-permute-done | bytes 180256 | tf_op jit(solution)/shard_map/ppermute | solution.py:794
  13.7 1.0 %shard_map.70 = (f32[19,2,48,128]{3,2,1,0:T(8,128)S(1)}, f32[3,2,48,128]{3,2,1,0:T(8,128)S(1)}, f32[2,48,128]{2,1,0:T(8,128)S(1)}, f32[2,48,128]{2,1,0:T(8,128)S...) custom-call(f32[4,2,32,128]{3,2,1,0:T(8,128)S(1)} %copy-done.1, ...), custom_call_target="tpu_custom_call", output_to_operand_aliasing={{0}: (3, {}), {1}: (4, {}), {2}: (5, {}), {3}: (6, {}), {4}... | custom-call | bytes 2260992 | tf_op jit(solution)/shard_map/pallas_call | solution.py:773
  14.7 1.1 %collective-permute-start.2 = (f32[10,48,128]{2,1,0:T(8,128)S(1)}, f32[10,48,128]{2,1,0:T(8,128)S(1)}, u32[]{:S(2)}, u32[]{:S(2)}) collective-permute-start(f32[10,48,128]{2,1,0:T(8,128)S(1)} %get-tuple-element.61), channel_id=1, source_target_pairs={{0,4},{4,8},{8,12},{12,16},{16,20},{20,24},{24,28},{28,32},{32,36}... | collective-permute-start | bytes 737288 | tf_op jit(solution)/shard_map/ppermute | solution.py:793
  15.8 6.8 %collective-permute-start.3 = (f32[10,48,128]{2,1,0:T(8,128)S(1)}, f32[10,48,128]{2,1,0:T(8,128)S(1)}, u32[]{:S(2)}, u32[]{:S(2)}) collective-permute-start(f32[10,48,128]{2,1,0:T(8,128)S(1)} %get-tuple-element.62), channel_id=1, source_target_pairs={{4,0},{8,4},{12,8},{16,12},{20,16},{24,20},{28,24},{32,28},{36,32}... | collective-permute-start | bytes 737288 | tf_op jit(solution)/shard_map/ppermute | solution.py:794
  22.6 4.8 %collective-permute-done.2.refs_5_ = f32[10,48,128]{2,1,0:T(8,128)S(1)} collective-permute-done((f32[10,48,128]{2,1,0:T(8,128)S(1)}, f32[10,48,128]{2,1,0:T(8,128)S(1)}, u32[]{:S(2)}, u32[]{:S(2)}) %collective-permute-start.2) | collective-permute-done | bytes 245792 | tf_op jit(solution)/shard_map/ppermute | solution.py:793
  27.3 0.0 collective-permute-done.3.refs_6_
  27.3 3.0 %shard_map.71 = (f32[3,6,64,128]{3,2,1,0:T(8,128)S(1)}, f32[6,64,128]{2,1,0:T(8,128)S(1)}, f32[3,4,48,128]{3,2,1,0:T(8,128)S(1)}, f32[3,2,48,128]{3,2,1,0:T(8,12...) custom-call(f32[19,2,48,128]{3,2,1,0:T(8,128)S(1)} %get-tuple-elemen, ...), custom_call_target="tpu_custom_call" | custom-call | bytes 1720320 | tf_op jit(solution)/shard_map/pallas_call | solution.py:773
  30.3 0.0 collective-permute-start.4
  30.3 6.1 %collective-permute-start.5 = (f32[9,48,128]{2,1,0:T(8,128)S(1)}, f32[9,48,128]{2,1,0:T(8,128)S(1)}, u32[]{:S(2)}, u32[]{:S(2)}) collective-permute-start(f32[9,48,128]{2,1,0:T(8,128)S(1)} %get-tuple-element.70), channel_id=1, source_target_pairs={{4,0},{8,4},{12,8},{16,12},{20,16},{24,20},{28,24},{32,28},{36,32}... | collective-permute-start | bytes 663560 | tf_op jit(solution)/shard_map/ppermute | solution.py:794
  36.4 5.4 %collective-permute-done.4.refs_7_ = f32[9,48,128]{2,1,0:T(8,128)S(1)} collective-permute-done((f32[9,48,128]{2,1,0:T(8,128)S(1)}, f32[9,48,128]{2,1,0:T(8,128)S(1)}, u32[]{:S(2)}, u32[]{:S(2)}) %collective-permute-start.4) | collective-permute-done | bytes 221216 | tf_op jit(solution)/shard_map/ppermute | solution.py:793
  41.9 0.0 collective-permute-done.5.refs_8_
  41.9 1.9 %shard_map.72 = (f32[6,64,128]{2,1,0:T(8,128)S(1)}, f32[3,4,48,128]{3,2,1,0:T(8,128)S(1)}, f32[3,2,48,128]{3,2,1,0:T(8,128)S(1)}, f32[2,40,128]{2,1,0:T(8,128)S(...) custom-call(f32[19,2,48,128]{3,2,1,0:T(8,128)S(1)} %get-tuple-element.63.refs_0_, ...), custom_call_target="tpu_custom_call" | custom-call | bytes 2310144 | tf_op jit(solution)/shard_map/pallas_call | solution.py:773
  43.8 0.1 collective-permute-start.6
  43.9 6.3 %collective-permute-start.7 = (f32[3,40,128]{2,1,0:T(8,128)S(1)}, f32[3,40,128]{2,1,0:T(8,128)S(1)}, u32[]{:S(2)}, u32[]{:S(2)}) collective-permute-start(f32[3,40,128]{2,1,0:T(8,128)S(1)} %get-tuple-element.73), channel_id=1, source_target_pairs={{4,0},{8,4},{12,8},{16,12},{20,16},{24,20},{28,24},{32,28},{36,32}... | collective-permute-start | bytes 184328 | tf_op jit(solution)/shard_map/ppermute | solution.py:794
  50.2 1.9 %collective-permute-done.6.from_left = f32[3,40,128]{2,1,0:T(8,128)S(1)} collective-permute-done((f32[3,40,128]{2,1,0:T(8,128)S(1)}, f32[3,40,128]{2,1,0:T(8,128)S(1)}, u32[]{:S(2)}, u32[]{:S(2)}) %collective-permute-start.6) | collective-permute-done | bytes 61472 | tf_op jit(solution)/shard_map/ppermute | solution.py:793
  52.1 0.0 collective-permute-done.7.from_right
  52.1 2.9 %shard_map.73 = (f32[19,2,64,128]{3,2,1,0:T(8,128)S(1)}, f32[10,2,64,128]{3,2,1,0:T(8,128)S(1)}, f32[2,40,128]{2,1,0:T(8,128)S(1)}, f32[8,40,128]{2,1,0:T(8,128)S(1)}, f32[8,40,128]{2,1,0:T(8,128)S(1)}) custom-call(f32[2,40,128]{2,1,0:T(8,128)S(1)} %get-tuple-element.71.misfit, f32[3,40,128]{2,1,0:T(8,128)S(1)} %collective-permute-done.6.from_left, ...), custom_call_target="tpu_custom_call" | custom-call | bytes 1687552 | tf_op jit(solution)/shard_map/pallas_call | solution.py:773
  55.0 5.5 %collective-permute-start.9 = (f32[8,40,128]{2,1,0:T(8,128)S(1)}, f32[8,40,128]{2,1,0:T(8,128)S(1)}, u32[]{:S(2)}, u32[]{:S(2)}) collective-permute-start(f32[8,40,128]{2,1,0:T(8,128)S(1)} %get-tuple-element.81.part_left), channel_id=1, source_target_pairs={{4,0},{8,4},{12,8},{16,12},{20,16},{24,20},{28,24},{32,28},{36,32}... | collective-permute-start | bytes 491528 | tf_op jit(solution)/shard_map/ppermute | solution.py:794
  60.4 0.0 collective-permute-start.8
  60.4 2.3 %collective-permute-done.9.from_right = f32[8,40,128]{2,1,0:T(8,128)S(1)} collective-permute-done((f32[8,40,128]{2,1,0:T(8,128)S(1)}, f32[8,40,128]{2,1,0:T(8,128)S(1)}, u32[]{:S(2)}, u32[]{:S(2)}) %collective-permute-start.9) | collective-permute-done | bytes 163872 | tf_op jit(solution)/shard_map/ppermute | solution.py:794
  62.7 6.1 %collective-permute-done.8.from_left = f32[8,40,128]{2,1,0:T(8,128)S(1)} collective-permute-done((f32[8,40,128]{2,1,0:T(8,128)S(1)}, f32[8,40,128]{2,1,0:T(8,128)S(1)}, u32[]{:S(2)}, u32[]{:S(2)}) %collective-permute-start.8) | collective-permute-done | bytes 163872 | tf_op jit(solution)/shard_map/ppermute | solution.py:793
  68.8 1.8 %shard_map.74 = (f32[2,32,128]{2,1,0:T(8,128)S(1)}, f32[1,256]{1,0:T(1,128)S(1)}) custom-call(f32[19,2,64,128]{3,2,1,0:T(8,128)S(1)} %get-tuple-element.78.adjoint, f32[10,2,64,128]{3,2,1,0:T(8,128)S(1)} %get-tuple-element.79.turned, f32[2,40,128]{2,1,0:T(8,128)S(1)} %get-tuple-element.80.wall, f32[8,40,128]{2,1,0:T(8,128)S(1)} %get-tuple-element.81.part_left, ...), custom_call_target="tpu_custom_call" | custom-call | bytes 3940352 | tf_op jit(solution)/shard_map/pallas_call | solution.py:773
  70.6 3.1 %collective-permute-start.12 = (f32[1,256]{1,0:T(1,128)S(1)}, f32[1,256]{1,0:T(1,128)S(1)}, u32[]{:S(2)}, u32[]{:S(2)}) collective-permute-start(f32[1,256]{1,0:T(1,128)S(1)} %get-tuple-element.87), channel_id=1, source_target_pairs={{0,3},{1,0},{2,1},{3,2},{4,7},{5,4},{6,5},{7,6},{8,11},{9,8},{10,9... | collective-permute-start | bytes 3080 | tf_op jit(solution)/shard_map/ppermute | solution.py:867
  73.7 2.7 %collective-permute-start.11 = (f32[1,256]{1,0:T(1,128)S(1)}, f32[1,256]{1,0:T(1,128)S(1)}, u32[]{:S(2)}, u32[]{:S(2)}) collective-permute-start(f32[1,256]{1,0:T(1,128)S(1)} %get-tuple-element.87), channel_id=1, source_target_pairs={{0,2},{1,3},{2,0},{3,1},{4,6},{5,7},{6,4},{7,5},{8,10},{9,11},{10,... | collective-permute-start | bytes 3080 | tf_op jit(solution)/shard_map/ppermute | solution.py:867
  76.4 0.5 collective-permute-start.10
  76.9 1.7 %shard_map.75 = f32[19,2,32,128]{3,2,1,0:T(8,128)} custom-call(f32[19,2,64,128]{3,2,1,0:T(8,128)S(1)} %get-tuple-element.78.adjoint, f32[10,2,64,128]{3,2,1,0:T(8,128)S(1)} %get-tuple-element.79.turned, f32[2,32,128]{2,1,0:T(8,128)S(1)} %get-tuple-element.85.more, f32[8,40,128]{2,1,0:T(8,128)S(1)} %collective-permute-done.8.from_left, ...), custom_call_target="tpu_custom_call" | custom-call | bytes 3489792 | tf_op jit(solution)/shard_map/pallas_call | solution.py:773
  78.6 0.0 collective-permute-done.12
  78.6 0.0 collective-permute-done.11
  78.6 0.0 collective-permute-done.10
  78.6 0.6 add_add_fusion
Async XLA Ops:
  2.5 7.1 %collective-permute-start = (f32[22,2,8,128]{3,2,1,0:T(8,128)}, f32[22,2,8,128]{3,2,1,0:T(8,128)S(1)}, u32[]{:S(2)}, u32[]{:S(2)}) collective-permute-start(f32[22,2,8,128]{3,2,1,0:T(8,128)} %get-tuple-element.46), channel_id=1, source_target_pairs={{0,1},{1,2},{2,3},{3,0},{4,5},{5,6},{6,7},{7,4},{8,9},{9,10},{10,1... | collective-permute-start | bytes 540680 | tf_op jit(solution)/shard_map/ppermute | solution.py:793
  6.9 6.8 %collective-permute-start.1 = (f32[22,2,8,128]{3,2,1,0:T(8,128)}, f32[22,2,8,128]{3,2,1,0:T(8,128)S(1)}, u32[]{:S(2)}, u32[]{:S(2)}) collective-permute-start(f32[22,2,8,128]{3,2,1,0:T(8,128)} %get-tuple-element.47), channel_id=1, source_target_pairs={{1,0},{2,1},{3,2},{0,3},{5,4},{6,5},{7,6},{4,7},{9,8},{10,9},{11,1... | collective-permute-start | bytes 540680 | tf_op jit(solution)/shard_map/ppermute | solution.py:794
  6.9 1.1 %copy-start = (f32[19,2,32,128]{3,2,1,0:T(8,128)S(1)}, f32[19,2,32,128]{3,2,1,0:T(8,128)}, u32[]{:S(2)}) copy-start(f32[19,2,32,128]{3,2,1,0:T(8,128)} %pops.3) | copy-start | bytes 1867780
  8.0 0.9 %copy-start.1 = (f32[4,2,32,128]{3,2,1,0:T(8,128)S(1)}, f32[4,2,32,128]{3,2,1,0:T(8,128)}, u32[]{:S(2)}) copy-start(f32[4,2,32,128]{3,2,1,0:T(8,128)} %get-tuple-element.45.small) | copy-start | bytes 393220
  14.7 12.6 %collective-permute-start.2 = (f32[10,48,128]{2,1,0:T(8,128)S(1)}, f32[10,48,128]{2,1,0:T(8,128)S(1)}, u32[]{:S(2)}, u32[]{:S(2)}) collective-permute-start(f32[10,48,128]{2,1,0:T(8,128)S(1)} %get-tuple-element.61), channel_id=1, source_target_pairs={{0,4},{4,8},{8,12},{12,16},{16,20},{20,24},{24,28},{28,32},{32,36}... | collective-permute-start | bytes 737288 | tf_op jit(solution)/shard_map/ppermute | solution.py:793
  15.8 11.5 %collective-permute-start.3 = (f32[10,48,128]{2,1,0:T(8,128)S(1)}, f32[10,48,128]{2,1,0:T(8,128)S(1)}, u32[]{:S(2)}, u32[]{:S(2)}) collective-permute-start(f32[10,48,128]{2,1,0:T(8,128)S(1)} %get-tuple-element.62), channel_id=1, source_target_pairs={{4,0},{8,4},{12,8},{16,12},{20,16},{24,20},{28,24},{32,28},{36,32}... | collective-permute-start | bytes 737288 | tf_op jit(solution)/shard_map/ppermute | solution.py:794
  30.3 11.6 %collective-permute-start.4 = (f32[9,48,128]{2,1,0:T(8,128)S(1)}, f32[9,48,128]{2,1,0:T(8,128)S(1)}, u32[]{:S(2)}, u32[]{:S(2)}) collective-permute-start(f32[9,48,128]{2,1,0:T(8,128)S(1)} %get-tuple-element.69), channel_id=1, source_target_pairs={{0,4},{4,8},{8,12},{12,16},{16,20},{20,24},{24,28},{28,32},{32,36}... | collective-permute-start | bytes 663560 | tf_op jit(solution)/shard_map/ppermute | solution.py:793
  30.3 11.5 %collective-permute-start.5 = (f32[9,48,128]{2,1,0:T(8,128)S(1)}, f32[9,48,128]{2,1,0:T(8,128)S(1)}, u32[]{:S(2)}, u32[]{:S(2)}) collective-permute-start(f32[9,48,128]{2,1,0:T(8,128)S(1)} %get-tuple-element.70), channel_id=1, source_target_pairs={{4,0},{8,4},{12,8},{16,12},{20,16},{24,20},{28,24},{32,28},{36,32}... | collective-permute-start | bytes 663560 | tf_op jit(solution)/shard_map/ppermute | solution.py:794
  43.8 8.3 %collective-permute-start.6 = (f32[3,40,128]{2,1,0:T(8,128)S(1)}, f32[3,40,128]{2,1,0:T(8,128)S(1)}, u32[]{:S(2)}, u32[]{:S(2)}) collective-permute-start(f32[3,40,128]{2,1,0:T(8,128)S(1)} %get-tuple-element.72), channel_id=1, source_target_pairs={{0,4},{4,8},{8,12},{12,16},{16,20},{20,24},{24,28},{28,32},{32,36}... | collective-permute-start | bytes 184328 | tf_op jit(solution)/shard_map/ppermute | solution.py:793
  43.9 8.2 %collective-permute-start.7 = (f32[3,40,128]{2,1,0:T(8,128)S(1)}, f32[3,40,128]{2,1,0:T(8,128)S(1)}, u32[]{:S(2)}, u32[]{:S(2)}) collective-permute-start(f32[3,40,128]{2,1,0:T(8,128)S(1)} %get-tuple-element.73), channel_id=1, source_target_pairs={{4,0},{8,4},{12,8},{16,12},{20,16},{24,20},{28,24},{32,28},{36,32}... | collective-permute-start | bytes 184328 | tf_op jit(solution)/shard_map/ppermute | solution.py:794
  55.0 7.7 %collective-permute-start.9 = (f32[8,40,128]{2,1,0:T(8,128)S(1)}, f32[8,40,128]{2,1,0:T(8,128)S(1)}, u32[]{:S(2)}, u32[]{:S(2)}) collective-permute-start(f32[8,40,128]{2,1,0:T(8,128)S(1)} %get-tuple-element.81.part_left), channel_id=1, source_target_pairs={{4,0},{8,4},{12,8},{16,12},{20,16},{24,20},{28,24},{32,28},{36,32}... | collective-permute-start | bytes 491528 | tf_op jit(solution)/shard_map/ppermute | solution.py:794
  60.4 8.4 %collective-permute-start.8 = (f32[8,40,128]{2,1,0:T(8,128)S(1)}, f32[8,40,128]{2,1,0:T(8,128)S(1)}, u32[]{:S(2)}, u32[]{:S(2)}) collective-permute-start(f32[8,40,128]{2,1,0:T(8,128)S(1)} %get-tuple-element.82.part_right), channel_id=1, source_target_pairs={{0,4},{4,8},{8,12},{12,16},{16,20},{20,24},{24,28},{28,32},{32,36}... | collective-permute-start | bytes 491528 | tf_op jit(solution)/shard_map/ppermute | solution.py:793
  70.6 8.0 %collective-permute-start.12 = (f32[1,256]{1,0:T(1,128)S(1)}, f32[1,256]{1,0:T(1,128)S(1)}, u32[]{:S(2)}, u32[]{:S(2)}) collective-permute-start(f32[1,256]{1,0:T(1,128)S(1)} %get-tuple-element.87), channel_id=1, source_target_pairs={{0,3},{1,0},{2,1},{3,2},{4,7},{5,4},{6,5},{7,6},{8,11},{9,8},{10,9... | collective-permute-start | bytes 3080 | tf_op jit(solution)/shard_map/ppermute | solution.py:867
  73.7 5.0 %collective-permute-start.11 = (f32[1,256]{1,0:T(1,128)S(1)}, f32[1,256]{1,0:T(1,128)S(1)}, u32[]{:S(2)}, u32[]{:S(2)}) collective-permute-start(f32[1,256]{1,0:T(1,128)S(1)} %get-tuple-element.87), channel_id=1, source_target_pairs={{0,2},{1,3},{2,0},{3,1},{4,6},{5,7},{6,4},{7,5},{8,10},{9,11},{10,... | collective-permute-start | bytes 3080 | tf_op jit(solution)/shard_map/ppermute | solution.py:867
  76.4 2.2 %collective-permute-start.10 = (f32[1,256]{1,0:T(1,128)S(1)}, f32[1,256]{1,0:T(1,128)S(1)}, u32[]{:S(2)}, u32[]{:S(2)}) collective-permute-start(f32[1,256]{1,0:T(1,128)S(1)} %get-tuple-element.87), channel_id=1, source_target_pairs={{0,1},{1,2},{2,3},{3,0},{4,5},{5,6},{6,7},{7,4},{8,9},{9,10},{10,1... | collective-permute-start | bytes 3080 | tf_op jit(solution)/shard_map/ppermute | solution.py:867

commit v3 on v2

--- a/solution.py
+++ b/solution.py
@@ -266,11 +266,8 @@
 
 
 def each_chunk(body, first=0, last=CHUNKS):
-    def step(t, carry):
+    for t in range(first, last):
         body(t)
-        return carry
-
-    lax.fori_loop(first, last, step, 0)
 
 
 def gradient_of(field, doubled, p, t):
@@ -560,7 +557,7 @@
 
 def last_reverse_kernel(
     misfit, from_left, from_right, masks, field, speed, pull, early_speed,
-    adjoint, turned, wall_out, send_left, send_right,
+    adjoint, turned, wall_out, send_left, send_right, part_left, part_right,
     ahead, far_masks, pulled, pulled_doubled, base,
 ):
     def place(t):
@@ -628,7 +625,7 @@
 
     def part(t):
         rows = middle(t)
-        for x, send, sent, skipped in ((0, send_left, RIGHTWARD, -1), (1, send_right, LEFTWARD, 1)):
+        for x, send, kept, sent, skipped in ((0, send_left, part_left, RIGHTWARD, -1), (1, send_right, part_right, LEFTWARD, 1)):
             p = 2 + x
             s = masks[0, p, rows(0), :]
             r = {}
@@ -639,6 +636,7 @@
             q = flow_adjoint(*dual(r), u)
             for a in range(3):
                 send[5 + a, flat(t), :] = s * q[a]
+                kept[a, flat(t), :] = s * q[a]
             for k, i in enumerate(sent):
                 send[k, flat(t), :] = adjoint[i, x, rows(0), :]
 
@@ -683,7 +681,7 @@
             r = {i: arrived(come, adjoint, masks, i, x, rows) for i in which}
             u = [speed[a, p - 1, mid(t), :] for a in range(3)]
             rest = flow_adjoint(*dual(r), u)
-            q = [part[5 + a, flat(t), :] + s * rest[a] for a in range(3)]
+            q = [part[a, flat(t), :] + s * rest[a] for a in range(3)]
             put_pulled(pulled, pulled_doubled, p - 1, rows, field[p, rows(0), :], q)
         for x, source, which in ((0, from_left, LEFTWARD), (1, from_right, RIGHTWARD)):
             p = 1 if x == 0 else 4
@@ -847,17 +845,17 @@
     )
     from_left, from_right = both_ways(to_left, to_right, "gx")
     pulled = (vmem(3, 4, TALL, DEPTH), vmem(2, 4, TALL, DEPTH))
-    adjoint, turned, wall, to_left, to_right = call(
+    adjoint, turned, wall, to_left, to_right, part_left, part_right = call(
         last_reverse_kernel,
         (misfit, from_left, from_right, masks, field1, speed1, pull1, speed0),
-        ((19, 2, TALL, DEPTH), (10, 2, TALL, DEPTH), (2, *less), (8, *less), (8, *less)),
+        ((19, 2, TALL, DEPTH), (10, 2, TALL, DEPTH), (2, *less), (8, *less), (8, *less), (3, *less), (3, *less)),
         (vmem(3, *wide6), vmem(3, 2, TALL, DEPTH), *pulled, vmem(19, 2, *less)),
     )
     from_left, from_right = both_ways(to_left, to_right, "gx")
     come = vmem(2, 5, TALL, DEPTH)
     more, label_part = call(
         wall_kernel,
-        (adjoint, turned, wall, to_left, to_right, from_left, from_right, masks, field0, speed0, chooser),
+        (adjoint, turned, wall, part_left, part_right, from_left, from_right, masks, field0, speed0, chooser),
         ((2, OWN, DEPTH), (1, LABELS)),
         (come, *pulled, vmem(OWN, DEPTH)),
     )

time: 79.4 us -> 67.9 us (0.86)
  Pallas kernels: 14.7 us -> 8.74 us
  waiting for transfers between devices: 24.7 us -> 19.8 us
    pallas_call x8, Pallas kernels: 14.7 us -> 8.74 us  [call(): pl.pallas_call(kernel, out_shape=[s if hasattr(s, 'dtype') else jax.Shape...]
    ppermute x5, waiting for transfers between devices: 18.4 us -> 15.7 us  [both_ways(): from_lower = lax.ppermute(to_upper, axis, up)]
    ppermute x5, waiting for transfers between devices: 6.32 us -> 4.07 us  [both_ways(): from_upper = lax.ppermute(to_lower, axis, down)]
    ppermute x3, starting transfers between devices: 6.33 us -> 5.23 us  [per_device(): lax.ppermute(label_part, 'gy', [(i, (i + step) % count) for i in range(co...]
  transfers between devices with their start and end apart: 13 -> 13, of which waited for: 7 -> 6; matrix products, arithmetic and copies ran while one was open for 0% -> 0% of each run, Pallas kernels for 3% -> 3%
where the time goes in v3:
time: 67.9 us; the launch traced here: 67.6 us
  starting transfers between devices  35.8 us (53%)
  waiting for transfers between devices  19.8 us (29%)
  Pallas kernels  8.74 us (13%)
  local copies, waits for them, and re-layouts  1.98 us (3%)
  between operations  0.72 us (1%)
    ppermute x5, starting transfers between devices, both_ways(): from_upper = lax.ppermute(to_lower, axis, down)  24.8 us
    ppermute x5, waiting for transfers between devices, both_ways(): from_lower = lax.ppermute(to_upper, axis, up)  15.7 us
    pallas_call x8, Pallas kernels, call(): pl.pallas_call(kernel, out_shape=[s if hasattr(s, 'dtype') else jax.Shape...  8.74 us
    ppermute x5, starting transfers between devices, both_ways(): from_lower = lax.ppermute(to_upper, axis, up)  5.74 us
    ppermute x3, starting transfers between devices, per_device(): lax.ppermute(label_part, 'gy', [(i, (i + step) % count) for i in range(co...  5.23 us
    ppermute x5, waiting for transfers between devices, both_ways(): from_upper = lax.ppermute(to_lower, axis, down)  4.07 us
    unnamed x4, local copies, waits for them, and re-layouts  1.98 us
  transfers between devices with their start and end apart: 13, of which 6 were waited for; matrix products, arithmetic and copies ran while one was open for 0% of the time, Pallas kernels for 3%

profile of v3, /device:TPU:1, one launch (start us, length us, event | category | flops | bytes accessed | tf_op | source)
XLA Modules:
  0.0 67.6 jit_solution(16176940393166032563)
XLA Ops:
  0.6 1.9 %shard_map.68 = (f32[22,2,8,128]{3,2,1,0:T(8,128)}, f32[22,2,8,128]{3,2,1,0:T(8,128)}, f32[4,2,32,128]{3,2,1,0:T(8,128)}) custom-call(f32[19,2,32,128]{3,2,1,0:T(8,128)} %pops.3, s32[2,32,128]{2,1,0:T(8,128)} %fluid.1, s32[2,32,128]{2,1,0:T(8,128)} %label.1, f32[2,32,128]{2,1,0:T(8,128)} %target.1, f32[2,128]{1,0:T(2,128)} %bitcast.2), custom_call_target="tpu_custom_call" | custom-call | bytes 721920 | tf_op jit(solution)/shard_map/pallas_call | solution.py:771
  2.5 4.4 %collective-permute-start = (f32[22,2,8,128]{3,2,1,0:T(8,128)}, f32[22,2,8,128]{3,2,1,0:T(8,128)S(1)}, u32[]{:S(2)}, u32[]{:S(2)}) collective-permute-start(f32[22,2,8,128]{3,2,1,0:T(8,128)} %get-tuple-element.48), channel_id=1, source_target_pairs={{0,1},{1,2},{2,3},{3,0},{4,5},{5,6},{6,7},{7,4},{8,9},{9,10},{10,1... | collective-permute-start | bytes 540680 | tf_op jit(solution)/shard_map/ppermute | solution.py:791
  6.9 0.0 collective-permute-start.1
  6.9 0.0 copy-start
  6.9 1.1 %copy-done = f32[19,2,32,128]{3,2,1,0:T(8,128)S(1)} copy-done((f32[19,2,32,128]{3,2,1,0:T(8,128)S(1)}, f32[19,2,32,128]{3,2,1,0:T(8,128)}, u32[]{:S(2)}) %copy-start) | copy-done | bytes 622616
  8.0 0.0 copy-start.1
  8.0 0.9 %copy-done.1 = f32[4,2,32,128]{3,2,1,0:T(8,128)S(1)} copy-done((f32[4,2,32,128]{3,2,1,0:T(8,128)S(1)}, f32[4,2,32,128]{3,2,1,0:T(8,128)}, u32[]{:S(2)}) %copy-start.1) | copy-done | bytes 131096
  8.9 0.4 shard_map.69
  9.3 0.4 collective-permute-done.below
  9.7 4.1 %collective-permute-done.1.above = f32[22,2,8,128]{3,2,1,0:T(8,128)S(1)} collective-permute-done((f32[22,2,8,128]{3,2,1,0:T(8,128)}, f32[22,2,8,128]{3,2,1,0:T(8,128)S(1)}, u32[]{:S(2)}, u32[]{:S(2)}) %collective-permute-start.1) | collective-permute-done | bytes 180256 | tf_op jit(solution)/shard_map/ppermute | solution.py:792
  13.7 0.2 shard_map.70
  13.9 1.1 %collective-permute-start.2 = (f32[10,48,128]{2,1,0:T(8,128)S(1)}, f32[10,48,128]{2,1,0:T(8,128)S(1)}, u32[]{:S(2)}, u32[]{:S(2)}) collective-permute-start(f32[10,48,128]{2,1,0:T(8,128)S(1)} %get-tuple-element.63), channel_id=1, source_target_pairs={{0,4},{4,8},{8,12},{12,16},{16,20},{20,24},{24,28},{28,32},{32,36}... | collective-permute-start | bytes 737288 | tf_op jit(solution)/shard_map/ppermute | solution.py:791
  15.1 6.8 %collective-permute-start.3 = (f32[10,48,128]{2,1,0:T(8,128)S(1)}, f32[10,48,128]{2,1,0:T(8,128)S(1)}, u32[]{:S(2)}, u32[]{:S(2)}) collective-permute-start(f32[10,48,128]{2,1,0:T(8,128)S(1)} %get-tuple-element.64), channel_id=1, source_target_pairs={{4,0},{8,4},{12,8},{16,12},{20,16},{24,20},{28,24},{32,28},{36,32}... | collective-permute-start | bytes 737288 | tf_op jit(solution)/shard_map/ppermute | solution.py:792
  21.8 4.8 %collective-permute-done.2.refs_5_ = f32[10,48,128]{2,1,0:T(8,128)S(1)} collective-permute-done((f32[10,48,128]{2,1,0:T(8,128)S(1)}, f32[10,48,128]{2,1,0:T(8,128)S(1)}, u32[]{:S(2)}, u32[]{:S(2)}) %collective-permute-start.2) | collective-permute-done | bytes 245792 | tf_op jit(solution)/shard_map/ppermute | solution.py:791
  26.6 0.0 collective-permute-done.3.refs_6_
  26.6 1.9 %shard_map.71 = (f32[3,6,64,128]{3,2,1,0:T(8,128)S(1)}, f32[6,64,128]{2,1,0:T(8,128)S(1)}, f32[3,4,48,128]{3,2,1,0:T(8,128)S(1)}, f32[3,2,48,128]{3,2,1,0:T(8,12...) custom-call(f32[19,2,48,128]{3,2,1,0:T(8,128)S(1)} %get-tuple-elemen, ...), custom_call_target="tpu_custom_call" | custom-call | bytes 1720320 | tf_op jit(solution)/shard_map/pallas_call | solution.py:771
  28.5 0.1 collective-permute-start.4
  28.6 6.1 %collective-permute-start.5 = (f32[9,48,128]{2,1,0:T(8,128)S(1)}, f32[9,48,128]{2,1,0:T(8,128)S(1)}, u32[]{:S(2)}, u32[]{:S(2)}) collective-permute-start(f32[9,48,128]{2,1,0:T(8,128)S(1)} %get-tuple-element.72), channel_id=1, source_target_pairs={{4,0},{8,4},{12,8},{16,12},{20,16},{24,20},{28,24},{32,28},{36,32}... | collective-permute-start | bytes 663560 | tf_op jit(solution)/shard_map/ppermute | solution.py:792
  34.7 5.4 %collective-permute-done.4.refs_7_ = f32[9,48,128]{2,1,0:T(8,128)S(1)} collective-permute-done((f32[9,48,128]{2,1,0:T(8,128)S(1)}, f32[9,48,128]{2,1,0:T(8,128)S(1)}, u32[]{:S(2)}, u32[]{:S(2)}) %collective-permute-start.4) | collective-permute-done | bytes 221216 | tf_op jit(solution)/shard_map/ppermute | solution.py:791
  40.1 0.0 collective-permute-done.5.refs_8_
  40.1 0.9 %shard_map.72 = (f32[6,64,128]{2,1,0:T(8,128)S(1)}, f32[3,4,48,128]{3,2,1,0:T(8,128)S(1)}, f32[3,2,48,128]{3,2,1,0:T(8,128)S(1)}, f32[2,40,128]{2,1,0:T(8,128)S(...) custom-call(f32[19,2,48,128]{3,2,1,0:T(8,128)S(1)} %get-tuple-element.65.refs_0_, ...), custom_call_target="tpu_custom_call" | custom-call | bytes 2310144 | tf_op jit(solution)/shard_map/pallas_call | solution.py:771
  41.0 0.1 collective-permute-start.6
  41.1 6.3 %collective-permute-start.7 = (f32[3,40,128]{2,1,0:T(8,128)S(1)}, f32[3,40,128]{2,1,0:T(8,128)S(1)}, u32[]{:S(2)}, u32[]{:S(2)}) collective-permute-start(f32[3,40,128]{2,1,0:T(8,128)S(1)} %get-tuple-element.75), channel_id=1, source_target_pairs={{4,0},{8,4},{12,8},{16,12},{20,16},{24,20},{28,24},{32,28},{36,32}... | collective-permute-start | bytes 184328 | tf_op jit(solution)/shard_map/ppermute | solution.py:792
  47.4 1.9 %collective-permute-done.6.from_left = f32[3,40,128]{2,1,0:T(8,128)S(1)} collective-permute-done((f32[3,40,128]{2,1,0:T(8,128)S(1)}, f32[3,40,128]{2,1,0:T(8,128)S(1)}, u32[]{:S(2)}, u32[]{:S(2)}) %collective-permute-start.6) | collective-permute-done | bytes 61472 | tf_op jit(solution)/shard_map/ppermute | solution.py:791
  49.3 0.0 collective-permute-done.7.from_right
  49.3 1.4 %shard_map.73 = (f32[19,2,64,128]{3,2,1,0:T(8,128)S(1)}, f32[10,2,64,128]{3,2,1,0:T(8,128)S(1)}, f32[2,40,128]{2,1,0:T(8,128)S(1)}, f32[8,40,128]{2,1,0:T(8,128)...) custom-call(f32[2,40,128]{2,1,0:T(8,128)S(1)} %get-tuple-element.73.misfit, ...), custom_call_target="tpu_custom_call" | custom-call | bytes 1687552 | tf_op jit(solution)/shard_map/pallas_call | solution.py:771
  50.7 0.1 collective-permute-start.8
  50.8 5.7 %collective-permute-start.9 = (f32[8,40,128]{2,1,0:T(8,128)S(1)}, f32[8,40,128]{2,1,0:T(8,128)S(1)}, u32[]{:S(2)}, u32[]{:S(2)}) collective-permute-start(f32[8,40,128]{2,1,0:T(8,128)S(1)} %get-tuple-element.86), channel_id=1, source_target_pairs={{4,0},{8,4},{12,8},{16,12},{20,16},{24,20},{28,24},{32,28},{36,32}... | collective-permute-start | bytes 491528 | tf_op jit(solution)/shard_map/ppermute | solution.py:792
  56.5 3.2 %collective-permute-done.8.from_left = f32[8,40,128]{2,1,0:T(8,128)S(1)} collective-permute-done((f32[8,40,128]{2,1,0:T(8,128)S(1)}, f32[8,40,128]{2,1,0:T(8,128)S(1)}, u32[]{:S(2)}, u32[]{:S(2)}) %collective-permute-start.8) | collective-permute-done | bytes 163872 | tf_op jit(solution)/shard_map/ppermute | solution.py:791
  59.7 0.0 collective-permute-done.9.from_right
  59.7 0.7 %shard_map.74 = (f32[2,32,128]{2,1,0:T(8,128)S(1)}, f32[1,256]{1,0:T(1,128)S(1)}) custom-call(f32[19,2,64,128]{3,2,1,0:T(8,128)S(1)} %get-tuple-element.80.adjoint, f32[10,2,64,128]{3,2,1,0:T(8,128)S(1)} %get-tuple-element.81.turned, f32[2,40,128]{2,1,0:T(8,128)S(1)} %get-tuple-element.82.wall, f32[3,40,128]{2,1,0:T(8,128)S(1)} %get-tuple-element.83.part_left, ...), custom_call_target="tpu_custom_call" | custom-call | bytes 3735552 | tf_op jit(solution)/shard_map/pallas_call | solution.py:771
  60.5 2.0 %collective-permute-start.12 = (f32[1,256]{1,0:T(1,128)S(1)}, f32[1,256]{1,0:T(1,128)S(1)}, u32[]{:S(2)}, u32[]{:S(2)}) collective-permute-start(f32[1,256]{1,0:T(1,128)S(1)} %get-tuple-element.91), channel_id=1, source_target_pairs={{0,3},{1,0},{2,1},{3,2},{4,7},{5,4},{6,5},{7,6},{8,11},{9,8},{10,9... | collective-permute-start | bytes 3080 | tf_op jit(solution)/shard_map/ppermute | solution.py:865
  62.5 2.5 %collective-permute-start.11 = (f32[1,256]{1,0:T(1,128)S(1)}, f32[1,256]{1,0:T(1,128)S(1)}, u32[]{:S(2)}, u32[]{:S(2)}) collective-permute-start(f32[1,256]{1,0:T(1,128)S(1)} %get-tuple-element.91), channel_id=1, source_target_pairs={{0,2},{1,3},{2,0},{3,1},{4,6},{5,7},{6,4},{7,5},{8,10},{9,11},{10,... | collective-permute-start | bytes 3080 | tf_op jit(solution)/shard_map/ppermute | solution.py:865
  64.9 0.8 %collective-permute-start.10 = (f32[1,256]{1,0:T(1,128)S(1)}, f32[1,256]{1,0:T(1,128)S(1)}, u32[]{:S(2)}, u32[]{:S(2)}) collective-permute-start(f32[1,256]{1,0:T(1,128)S(1)} %get-tuple-element.91), channel_id=1, source_target_pairs={{0,1},{1,2},{2,3},{3,0},{4,5},{5,6},{6,7},{7,4},{8,9},{9,10},{10,1... | collective-permute-start | bytes 3080 | tf_op jit(solution)/shard_map/ppermute | solution.py:865
  65.7 1.3 %shard_map.75 = f32[19,2,32,128]{3,2,1,0:T(8,128)} custom-call(f32[19,2,64,128]{3,2,1,0:T(8,128)S(1)} %get-tuple-element.80.adjoint, f32[10,2,64,128]{3,2,1,0:T(8,128)S(1)} %get-tuple-element.81.turned, f32[2,32,128]{2,1,0:T(8,128)S(1)} %get-tuple-element.89.more, f32[8,40,128]{2,1,0:T(8,128)S(1)} %collective-permute-done.8.from_left, ...), custom_call_target="tpu_custom_call" | custom-call | bytes 3489792 | tf_op jit(solution)/shard_map/pallas_call | solution.py:771
  67.0 0.0 collective-permute-done.12
  67.0 0.0 collective-permute-done.11
  67.0 0.0 collective-permute-done.10
  67.0 0.6 add_add_fusion
Async XLA Ops:
  2.5 7.1 %collective-permute-start = (f32[22,2,8,128]{3,2,1,0:T(8,128)}, f32[22,2,8,128]{3,2,1,0:T(8,128)S(1)}, u32[]{:S(2)}, u32[]{:S(2)}) collective-permute-start(f32[22,2,8,128]{3,2,1,0:T(8,128)} %get-tuple-element.48), channel_id=1, source_target_pairs={{0,1},{1,2},{2,3},{3,0},{4,5},{5,6},{6,7},{7,4},{8,9},{9,10},{10,1... | collective-permute-start | bytes 540680 | tf_op jit(solution)/shard_map/ppermute | solution.py:791
  6.9 6.8 %collective-permute-start.1 = (f32[22,2,8,128]{3,2,1,0:T(8,128)}, f32[22,2,8,128]{3,2,1,0:T(8,128)S(1)}, u32[]{:S(2)}, u32[]{:S(2)}) collective-permute-start(f32[22,2,8,128]{3,2,1,0:T(8,128)} %get-tuple-element.49), channel_id=1, source_target_pairs={{1,0},{2,1},{3,2},{0,3},{5,4},{6,5},{7,6},{4,7},{9,8},{10,9},{11,1... | collective-permute-start | bytes 540680 | tf_op jit(solution)/shard_map/ppermute | solution.py:792
  6.9 1.1 %copy-start = (f32[19,2,32,128]{3,2,1,0:T(8,128)S(1)}, f32[19,2,32,128]{3,2,1,0:T(8,128)}, u32[]{:S(2)}) copy-start(f32[19,2,32,128]{3,2,1,0:T(8,128)} %pops.3) | copy-start | bytes 1867780
  8.0 0.9 %copy-start.1 = (f32[4,2,32,128]{3,2,1,0:T(8,128)S(1)}, f32[4,2,32,128]{3,2,1,0:T(8,128)}, u32[]{:S(2)}) copy-start(f32[4,2,32,128]{3,2,1,0:T(8,128)} %get-tuple-element.47.small) | copy-start | bytes 393220
  13.9 12.6 %collective-permute-start.2 = (f32[10,48,128]{2,1,0:T(8,128)S(1)}, f32[10,48,128]{2,1,0:T(8,128)S(1)}, u32[]{:S(2)}, u32[]{:S(2)}) collective-permute-start(f32[10,48,128]{2,1,0:T(8,128)S(1)} %get-tuple-element.63), channel_id=1, source_target_pairs={{0,4},{4,8},{8,12},{12,16},{16,20},{20,24},{24,28},{28,32},{32,36}... | collective-permute-start | bytes 737288 | tf_op jit(solution)/shard_map/ppermute | solution.py:791
  15.1 11.5 %collective-permute-start.3 = (f32[10,48,128]{2,1,0:T(8,128)S(1)}, f32[10,48,128]{2,1,0:T(8,128)S(1)}, u32[]{:S(2)}, u32[]{:S(2)}) collective-permute-start(f32[10,48,128]{2,1,0:T(8,128)S(1)} %get-tuple-element.64), channel_id=1, source_target_pairs={{4,0},{8,4},{12,8},{16,12},{20,16},{24,20},{28,24},{32,28},{36,32}... | collective-permute-start | bytes 737288 | tf_op jit(solution)/shard_map/ppermute | solution.py:792
  28.5 11.6 %collective-permute-start.4 = (f32[9,48,128]{2,1,0:T(8,128)S(1)}, f32[9,48,128]{2,1,0:T(8,128)S(1)}, u32[]{:S(2)}, u32[]{:S(2)}) collective-permute-start(f32[9,48,128]{2,1,0:T(8,128)S(1)} %get-tuple-element.71), channel_id=1, source_target_pairs={{0,4},{4,8},{8,12},{12,16},{16,20},{20,24},{24,28},{28,32},{32,36}... | collective-permute-start | bytes 663560 | tf_op jit(solution)/shard_map/ppermute | solution.py:791
  28.6 11.5 %collective-permute-start.5 = (f32[9,48,128]{2,1,0:T(8,128)S(1)}, f32[9,48,128]{2,1,0:T(8,128)S(1)}, u32[]{:S(2)}, u32[]{:S(2)}) collective-permute-start(f32[9,48,128]{2,1,0:T(8,128)S(1)} %get-tuple-element.72), channel_id=1, source_target_pairs={{4,0},{8,4},{12,8},{16,12},{20,16},{24,20},{28,24},{32,28},{36,32}... | collective-permute-start | bytes 663560 | tf_op jit(solution)/shard_map/ppermute | solution.py:792
  41.0 8.3 %collective-permute-start.6 = (f32[3,40,128]{2,1,0:T(8,128)S(1)}, f32[3,40,128]{2,1,0:T(8,128)S(1)}, u32[]{:S(2)}, u32[]{:S(2)}) collective-permute-start(f32[3,40,128]{2,1,0:T(8,128)S(1)} %get-tuple-element.74), channel_id=1, source_target_pairs={{0,4},{4,8},{8,12},{12,16},{16,20},{20,24},{24,28},{28,32},{32,36}... | collective-permute-start | bytes 184328 | tf_op jit(solution)/shard_map/ppermute | solution.py:791
  41.1 8.2 %collective-permute-start.7 = (f32[3,40,128]{2,1,0:T(8,128)S(1)}, f32[3,40,128]{2,1,0:T(8,128)S(1)}, u32[]{:S(2)}, u32[]{:S(2)}) collective-permute-start(f32[3,40,128]{2,1,0:T(8,128)S(1)} %get-tuple-element.75), channel_id=1, source_target_pairs={{4,0},{8,4},{12,8},{16,12},{20,16},{24,20},{28,24},{32,28},{36,32}... | collective-permute-start | bytes 184328 | tf_op jit(solution)/shard_map/ppermute | solution.py:792
  50.7 9.0 %collective-permute-start.8 = (f32[8,40,128]{2,1,0:T(8,128)S(1)}, f32[8,40,128]{2,1,0:T(8,128)S(1)}, u32[]{:S(2)}, u32[]{:S(2)}) collective-permute-start(f32[8,40,128]{2,1,0:T(8,128)S(1)} %get-tuple-element.85), channel_id=1, source_target_pairs={{0,4},{4,8},{8,12},{12,16},{16,20},{20,24},{24,28},{28,32},{32,36}... | collective-permute-start | bytes 491528 | tf_op jit(solution)/shard_map/ppermute | solution.py:791
  50.8 8.9 %collective-permute-start.9 = (f32[8,40,128]{2,1,0:T(8,128)S(1)}, f32[8,40,128]{2,1,0:T(8,128)S(1)}, u32[]{:S(2)}, u32[]{:S(2)}) collective-permute-start(f32[8,40,128]{2,1,0:T(8,128)S(1)} %get-tuple-element.86), channel_id=1, source_target_pairs={{4,0},{8,4},{12,8},{16,12},{20,16},{24,20},{28,24},{32,28},{36,32}... | collective-permute-start | bytes 491528 | tf_op jit(solution)/shard_map/ppermute | solution.py:792
  60.5 6.5 %collective-permute-start.12 = (f32[1,256]{1,0:T(1,128)S(1)}, f32[1,256]{1,0:T(1,128)S(1)}, u32[]{:S(2)}, u32[]{:S(2)}) collective-permute-start(f32[1,256]{1,0:T(1,128)S(1)} %get-tuple-element.91), channel_id=1, source_target_pairs={{0,3},{1,0},{2,1},{3,2},{4,7},{5,4},{6,5},{7,6},{8,11},{9,8},{10,9... | collective-permute-start | bytes 3080 | tf_op jit(solution)/shard_map/ppermute | solution.py:865
  62.5 4.6 %collective-permute-start.11 = (f32[1,256]{1,0:T(1,128)S(1)}, f32[1,256]{1,0:T(1,128)S(1)}, u32[]{:S(2)}, u32[]{:S(2)}) collective-permute-start(f32[1,256]{1,0:T(1,128)S(1)} %get-tuple-element.91), channel_id=1, source_target_pairs={{0,2},{1,3},{2,0},{3,1},{4,6},{5,7},{6,4},{7,5},{8,10},{9,11},{10,... | collective-permute-start | bytes 3080 | tf_op jit(solution)/shard_map/ppermute | solution.py:865
  64.9 2.1 %collective-permute-start.10 = (f32[1,256]{1,0:T(1,128)S(1)}, f32[1,256]{1,0:T(1,128)S(1)}, u32[]{:S(2)}, u32[]{:S(2)}) collective-permute-start(f32[1,256]{1,0:T(1,128)S(1)} %get-tuple-element.91), channel_id=1, source_target_pairs={{0,1},{1,2},{2,3},{3,0},{4,5},{5,6},{6,7},{7,4},{8,9},{9,10},{10,1... | collective-permute-start | bytes 3080 | tf_op jit(solution)/shard_map/ppermute | solution.py:865

commit v4 on v3

--- a/solution.py
+++ b/solution.py
@@ -265,9 +265,53 @@
     return pl.ds(t * 8 + ((ROWS - MID) // 2 + PAD + shift), 8)
 
 
-def each_chunk(body, first=0, last=CHUNKS):
-    for t in range(first, last):
+class Packed:
+    def __init__(self, spans, limit):
+        self.spans, self.shift, at = spans, [], spans[0][0]
+        for low, high in spans:
+            self.shift.append(at - low)
+            at += high - low
+        self.shape = (-(-(max(self.shift) + limit) // 8) * 8, DEPTH)
+
+    def put(self, ref, k, t, value):
+        low, high = max(8 * t, self.spans[k][0]), min(8 * t + 8, self.spans[k][1])
+        if low < high:
+            ref[self.shift[k] + low : self.shift[k] + high, :] = value[low - 8 * t : high - 8 * t, :]
+
+    def get(self, ref, k, t):
+        return ref[pl.ds(8 * t + self.shift[k], 8), :]
+
+
+def step_spans(first, last, which, more):
+    return [(first - VECTORS[i][1], last - VECTORS[i][1]) for i in which] + [(first - 1, last + 1)] * 3 + more
+
+
+def adjoint_spans(which):
+    first, last = (MID - OWN) // 2 - 1, (MID + OWN) // 2 + 1
+    rows = [(first + min(VECTORS[i][1], 0), last + max(VECTORS[i][1], 0)) for i in which]
+    return rows + [(first, last)] * 3
+
+
+START = {
+    which: Packed(step_spans(2, ROWS - 2, which, [(0, ROWS)] * 2), ROWS) for which in (LEFTWARD, RIGHTWARD)
+}
+SECOND = {
+    which: Packed(step_spans(4, ROWS - 4, which, [(2, ROWS - 2)]), ROWS) for which in (LEFTWARD, RIGHTWARD)
+}
+BACK = {which: Packed(adjoint_spans(which), MID) for which in (LEFTWARD, RIGHTWARD)}
+
+
+def each_chunk(body, first=0, last=CHUNKS, unroll=0):
+    if unroll == 0:
+        for t in range(first, last):
+            body(t)
+        return
+
+    def step(t, carry):
         body(t)
+        return carry
+
+    lax.fori_loop(first, last, step, 0, unroll=unroll)
 
 
 def gradient_of(field, doubled, p, t):
@@ -299,12 +343,12 @@
     return [along_x if inner > p else -along_x, up - down, rolled(here, -1) - rolled(here, 1)]
 
 
-def send_flow(send_left, send_right, flow, field, doubled, t):
-    for send, here, inner in ((send_left, 0, 1), (send_right, 1, 0)):
+def send_flow(packed, send_left, send_right, flow, field, doubled, t):
+    for send, which, here, inner in ((send_left, LEFTWARD, 0, 1), (send_right, RIGHTWARD, 1, 0)):
         push = field[here, tall(t), :] * (PULL / SHEAR)
         pull = inner_gradient(field, doubled, here, inner, t)
         for a in range(3):
-            send[5 + a, flat(t), :] = flow[a, here, flat(t), :] + push * pull[a]
+            packed[which].put(send, 5 + a, t, flow[a, here, flat(t), :] + push * pull[a])
 
 
 def edges_kernel(pops, fluid, label, target, table, low, high, small, whole, values, sems):
@@ -330,13 +374,11 @@
     high[19:22] = small[0:3, :, OWN - HALO : OWN, :]
 
 
-def put_sends(send_left, send_right, t, lin, chosen):
-    for k, i in enumerate(LEFTWARD):
-        send_left[k, flat(t), :] = lin[0][i]
-    for k, i in enumerate(RIGHTWARD):
-        send_right[k, flat(t), :] = lin[1][i]
-    send_left[8, flat(t), :] = chosen[0]
-    send_right[8, flat(t), :] = chosen[1]
+def put_sends(packed, send_left, send_right, t, lin, chosen):
+    for x, send, which in ((0, send_left, LEFTWARD), (1, send_right, RIGHTWARD)):
+        for k, i in enumerate(which):
+            packed[which].put(send, k, t, lin[x][i])
+        packed[which].put(send, 8, t, chosen[x])
 
 
 def start_rows(t, populations, shares, marks, table, outs):
@@ -362,9 +404,9 @@
         share_out[x, flat(t), :] = share
         lin.append(linear)
         chosen.append(jnp.where(share > 0, total, wall))
-    put_sends(send_left, send_right, t, lin, chosen)
-    send_left[9, flat(t), :] = shares[0]
-    send_right[9, flat(t), :] = shares[1]
+    put_sends(START, send_left, send_right, t, lin, chosen)
+    START[LEFTWARD].put(send_left, 9, t, shares[0])
+    START[RIGHTWARD].put(send_right, 9, t, shares[1])
 
 
 def own_kernel(pops, small, *refs):
@@ -415,7 +457,7 @@
             doubled[x, tall(t), :] = with_sides(value)
 
     each_chunk(place)
-    each_chunk(functools.partial(send_flow, send_left, send_right, flow, field, doubled))
+    each_chunk(functools.partial(send_flow, START, send_left, send_right, flow, field, doubled))
 
 
 def step_kernel(is_first, *refs):
@@ -428,6 +470,8 @@
          field, speed, pull_out, misfit_out, send_left, send_right,
          doubled, relaxed, turned) = refs
 
+    packed = START if is_first else SECOND
+
     def place(t):
         def put(p, x, s):
             field[p, tall(t), :] = x
@@ -439,9 +483,9 @@
 
         for x in range(2):
             put(2 + x, effective[x, flat(t), :], share[x, flat(t), :])
-        for near, come in ((1, from_left), (4, from_right)):
-            s = come[9, flat(t), :] if is_first else masks[0, near, tall(t), :]
-            chosen = come[8, flat(t), :]
+        for near, come, which in ((1, from_left, RIGHTWARD), (4, from_right, LEFTWARD)):
+            s = packed[which].get(come, 9, t) if is_first else masks[0, near, tall(t), :]
+            chosen = packed[which].get(come, 8, t)
             put(near, jnp.where(s > 0, 1.0 - jnp.exp(-chosen), chosen), s)
 
     each_chunk(place)
@@ -461,10 +505,10 @@
             else:
                 pull = outer_gradient(field, doubled, p, 2 if p == 1 else 3, t)
                 come = from_left if p == 1 else from_right
-                rho = come[8, flat(t), :]
-                mom = [come[5 + a, flat(t), :] for a in range(3)]
                 which = RIGHTWARD if p == 1 else LEFTWARD
-                lin_at = {i: come[k, flat(t), :] for k, i in enumerate(which)}
+                rho = packed[which].get(come, 8, t)
+                mom = [packed[which].get(come, 5 + a, t) for a in range(3)]
+                lin_at = {i: packed[which].get(come, k, t) for k, i in enumerate(which)}
             push = psi * (PULL / SHEAR)
             full = [mom[a] + push * pull[a] for a in range(3)]
             inverse = 1.0 / rho
@@ -478,7 +522,7 @@
                 if i in TURNED:
                     turned[TURNED.index(i), p - 1, tall(t), :] = rolled(value, VECTORS[i][2])
 
-    each_chunk(collide)
+    each_chunk(collide, unroll=3)
 
     def streamed(x, rows):
         f = {0: relaxed[0, 1 + x, rows(0), :]}
@@ -509,7 +553,7 @@
             next_doubled[x, tall(t), :] = with_sides(eff)
             lin_sent.append(linear)
             chosen_sent.append(jnp.where(s > 0, total, held))
-        put_sends(send_left, send_right, t, lin_sent, chosen_sent)
+        put_sends(SECOND, send_left, send_right, t, lin_sent, chosen_sent)
 
     def compare(t):
         for x, near, far in ((0, send_left, send_right), (1, send_right, send_left)):
@@ -523,7 +567,7 @@
 
     if is_first:
         each_chunk(stream)
-        each_chunk(functools.partial(send_flow, send_left, send_right, flow_out, next_field, next_doubled))
+        each_chunk(functools.partial(send_flow, SECOND, send_left, send_right, flow_out, next_field, next_doubled))
     else:
         each_chunk(compare, 0, MID // 8)
 
@@ -635,10 +679,10 @@
             u = [early_speed[a, p - 1, mid(t), :] for a in range(3)]
             q = flow_adjoint(*dual(r), u)
             for a in range(3):
-                send[5 + a, flat(t), :] = s * q[a]
+                BACK[sent].put(send, 5 + a, t, s * q[a])
                 kept[a, flat(t), :] = s * q[a]
             for k, i in enumerate(sent):
-                send[k, flat(t), :] = adjoint[i, x, rows(0), :]
+                BACK[sent].put(send, k, t, adjoint[i, x, rows(0), :])
 
     each_chunk(part, 0, MID // 8)
 
@@ -657,7 +701,7 @@
 def place_sides(come, from_left, from_right, t):
     for side, source, which in ((0, from_left, LEFTWARD), (1, from_right, RIGHTWARD)):
         for k, i in enumerate(which):
-            come[side, k, mid_tall(t), :] = rolled(source[k, flat(t), :], -VECTORS[i][2])
+            come[side, k, mid_tall(t), :] = rolled(BACK[which].get(source, k, t), -VECTORS[i][2])
 
 
 def arrived(come, adjoint, masks, i, x, rows):
@@ -693,11 +737,11 @@
                     there = turned[TURNED.index(i), x, rows(cy), :]
                 else:
                     there = adjoint[i, x, rows(cy), :]
-                here = source[which.index(OPPOSITE[i]), flat(t), :]
+                here = BACK[which].get(source, which.index(OPPOSITE[i]), t)
                 r[i] = jnp.where(mask_ahead(masks, i, p, rows), there, here)
             u = [speed[a, p - 1, mid(t), :] for a in range(3)]
             rest = flow_adjoint(*dual(r), u)
-            q = [source[5 + a, flat(t), :] + s * rest[a] for a in range(3)]
+            q = [BACK[which].get(source, 5 + a, t) + s * rest[a] for a in range(3)]
             put_pulled(pulled, pulled_doubled, p - 1, rows, field[p, rows(0), :], q)
 
     each_chunk(collide, 0, MID // 8)
@@ -812,7 +856,7 @@
     )
     below, above = both_ways(low, high, "gy")
     blocks = (OWN // 2) * (DEPTH // 4)
-    started = ((19, *two), (3, *two), two, two, two, two, (10, *plane), (10, *plane))
+    started = ((19, *two), (3, *two), two, two, two, two, START[LEFTWARD].shape, START[RIGHTWARD].shape)
     *own, chooser = call(
         own_kernel,
         (populations, small),
@@ -831,7 +875,7 @@
         (lin, flow, density, effective, share, from_left, from_right),
         (
             (3, *wide6), wide6, (3, 4, *plane), (3, *two),
-            (19, *two), (3, *two), two, two, (9, *plane), (9, *plane),
+            (19, *two), (3, *two), two, two, SECOND[LEFTWARD].shape, SECOND[RIGHTWARD].shape,
         ),
         (*work, *beside),
     )
@@ -848,7 +892,7 @@
     adjoint, turned, wall, to_left, to_right, part_left, part_right = call(
         last_reverse_kernel,
         (misfit, from_left, from_right, masks, field1, speed1, pull1, speed0),
-        ((19, 2, TALL, DEPTH), (10, 2, TALL, DEPTH), (2, *less), (8, *less), (8, *less), (3, *less), (3, *less)),
+        ((19, 2, TALL, DEPTH), (10, 2, TALL, DEPTH), (2, *less), BACK[RIGHTWARD].shape, BACK[LEFTWARD].shape, (3, *less), (3, *less)),
         (vmem(3, *wide6), vmem(3, 2, TALL, DEPTH), *pulled, vmem(19, 2, *less)),
     )
     from_left, from_right = both_ways(to_left, to_right, "gx")

time: 67.9 us -> 66.3 us (0.976)
  waiting for transfers between devices: 19.8 us -> 18.4 us
    ppermute x5, waiting for transfers between devices: 15.7 us -> 14.4 us  [both_ways(): from_lower = lax.ppermute(to_upper, axis, up)]
where the time goes in v4:
time: 66.3 us; the launch traced here: 65.8 us
  starting transfers between devices  35.8 us (54%)
  waiting for transfers between devices  18.4 us (28%)
  Pallas kernels  8.23 us (12%)
  local copies, waits for them, and re-layouts  1.98 us (3%)
  between operations  0.72 us (1%)
    ppermute x5, starting transfers between devices, both_ways(): from_upper = lax.ppermute(to_lower, axis, down)  24.8 us
    ppermute x5, waiting for transfers between devices, both_ways(): from_lower = lax.ppermute(to_upper, axis, up)  14.4 us
    pallas_call x8, Pallas kernels, call(): pl.pallas_call(kernel, out_shape=[s if hasattr(s, 'dtype') else jax.Shape...  8.23 us
    ppermute x5, starting transfers between devices, both_ways(): from_lower = lax.ppermute(to_upper, axis, up)  5.74 us
    ppermute x3, starting transfers between devices, per_device(): lax.ppermute(label_part, 'gy', [(i, (i + step) % count) for i in range(co...  5.23 us
    ppermute x5, waiting for transfers between devices, both_ways(): from_upper = lax.ppermute(to_lower, axis, down)  4.07 us
    unnamed x4, local copies, waits for them, and re-layouts  1.98 us
  transfers between devices with their start and end apart: 13, of which 6 were waited for; matrix products, arithmetic and copies ran while one was open for 0% of the time, Pallas kernels for 3%

profile of v4, /device:TPU:1, one launch (start us, length us, event | category | flops | bytes accessed | tf_op | source)
XLA Modules:
  0.0 65.8 jit_solution(3760624235966864031)
XLA Ops:
  0.6 1.9 %shard_map.68 = (f32[22,2,8,128]{3,2,1,0:T(8,128)}, f32[22,2,8,128]{3,2,1,0:T(8,128)}, f32[4,2,32,128]{3,2,1,0:T(8,128)}) custom-call(f32[19,2,32,128]{3,2,1,0:T(8,128)} %pops.3, s32[2,32,128]{2,1,0:T(8,128)} %fluid.1, s32[2,32,128]{2,1,0:T(8,128)} %label.1, f32[2,32,128]{2,1,0:T(8,128)} %target.1, f32[2,128]{1,0:T(2,128)} %bitcast.2), custom_call_target="tpu_custom_call" | custom-call | bytes 721920 | tf_op jit(solution)/shard_map/pallas_call | solution.py:815
  2.5 4.4 %collective-permute-start = (f32[22,2,8,128]{3,2,1,0:T(8,128)}, f32[22,2,8,128]{3,2,1,0:T(8,128)S(1)}, u32[]{:S(2)}, u32[]{:S(2)}) collective-permute-start(f32[22,2,8,128]{3,2,1,0:T(8,128)} %get-tuple-element.48), channel_id=1, source_target_pairs={{0,1},{1,2},{2,3},{3,0},{4,5},{5,6},{6,7},{7,4},{8,9},{9,10},{10,1... | collective-permute-start | bytes 540680 | tf_op jit(solution)/shard_map/ppermute | solution.py:835
  6.9 0.0 collective-permute-start.1
  6.9 0.0 copy-start
  6.9 1.1 %copy-done = f32[19,2,32,128]{3,2,1,0:T(8,128)S(1)} copy-done((f32[19,2,32,128]{3,2,1,0:T(8,128)S(1)}, f32[19,2,32,128]{3,2,1,0:T(8,128)}, u32[]{:S(2)}) %copy-start) | copy-done | bytes 622616
  8.0 0.0 copy-start.1
  8.0 0.9 %copy-done.1 = f32[4,2,32,128]{3,2,1,0:T(8,128)S(1)} copy-done((f32[4,2,32,128]{3,2,1,0:T(8,128)S(1)}, f32[4,2,32,128]{3,2,1,0:T(8,128)}, u32[]{:S(2)}) %copy-start.1) | copy-done | bytes 131096
  8.9 0.4 shard_map.69
  9.3 0.4 collective-permute-done.below
  9.7 4.1 %collective-permute-done.1.above = f32[22,2,8,128]{3,2,1,0:T(8,128)S(1)} collective-permute-done((f32[22,2,8,128]{3,2,1,0:T(8,128)}, f32[22,2,8,128]{3,2,1,0:T(8,128)S(1)}, u32[]{:S(2)}, u32[]{:S(2)}) %collective-permute-start.1) | collective-permute-done | bytes 180256 | tf_op jit(solution)/shard_map/ppermute | solution.py:836
  13.7 0.2 shard_map.70
  13.9 1.1 %collective-permute-start.2 = (f32[456,128]{1,0:T(8,128)S(1)}, f32[456,128]{1,0:T(8,128)S(1)}, u32[]{:S(2)}, u32[]{:S(2)}) collective-permute-start(f32[456,128]{1,0:T(8,128)S(1)} %get-tuple-element.63), channel_id=1, source_target_pairs={{0,4},{4,8},{8,12},{12,16},{16,20},{20,24},{24,28},{28,32},{32,36}... | collective-permute-start | bytes 700424 | tf_op jit(solution)/shard_map/ppermute | solution.py:835
  15.1 6.8 %collective-permute-start.3 = (f32[456,128]{1,0:T(8,128)S(1)}, f32[456,128]{1,0:T(8,128)S(1)}, u32[]{:S(2)}, u32[]{:S(2)}) collective-permute-start(f32[456,128]{1,0:T(8,128)S(1)} %get-tuple-element.64), channel_id=1, source_target_pairs={{4,0},{8,4},{12,8},{16,12},{20,16},{24,20},{28,24},{32,28},{36,32}... | collective-permute-start | bytes 700424 | tf_op jit(solution)/shard_map/ppermute | solution.py:836
  21.8 4.5 %collective-permute-done.2.refs_5_ = f32[456,128]{1,0:T(8,128)S(1)} collective-permute-done((f32[456,128]{1,0:T(8,128)S(1)}, f32[456,128]{1,0:T(8,128)S(1)}, u32[]{:S(2)}, u32[]{:S(2)}) %collective-permute-start.2) | collective-permute-done | bytes 233504 | tf_op jit(solution)/shard_map/ppermute | solution.py:835
  26.3 0.0 collective-permute-done.3.refs_6_
  26.3 1.4 %shard_map.71 = (f32[3,6,64,128]{3,2,1,0:T(8,128)S(1)}, f32[6,64,128]{2,1,0:T(8,128)S(1)}, f32[3,4,48,128]{3,2,1,0:T(8,128)S(1)}, f32[3,2,48,128]{3,2,1,0:T(8,12...) custom-call(f32[19,2,48,128]{3,2,1,0:T(8,128)S(1)} %get-tuple-elemen, ...), custom_call_target="tpu_custom_call" | custom-call | bytes 1695744 | tf_op jit(solution)/shard_map/pallas_call | solution.py:815
  27.7 0.1 collective-permute-start.4
  27.8 6.1 %collective-permute-start.5 = (f32[376,128]{1,0:T(8,128)S(1)}, f32[376,128]{1,0:T(8,128)S(1)}, u32[]{:S(2)}, u32[]{:S(2)}) collective-permute-start(f32[376,128]{1,0:T(8,128)S(1)} %get-tuple-element.72), channel_id=1, source_target_pairs={{4,0},{8,4},{12,8},{16,12},{20,16},{24,20},{28,24},{32,28},{36,32}... | collective-permute-start | bytes 577544 | tf_op jit(solution)/shard_map/ppermute | solution.py:836
  34.0 4.8 %collective-permute-done.4.refs_7_ = f32[376,128]{1,0:T(8,128)S(1)} collective-permute-done((f32[376,128]{1,0:T(8,128)S(1)}, f32[376,128]{1,0:T(8,128)S(1)}, u32[]{:S(2)}, u32[]{:S(2)}) %collective-permute-start.4) | collective-permute-done | bytes 192544 | tf_op jit(solution)/shard_map/ppermute | solution.py:835
  38.8 0.0 collective-permute-done.5.refs_8_
  38.8 0.9 %shard_map.72 = (f32[6,64,128]{2,1,0:T(8,128)S(1)}, f32[3,4,48,128]{3,2,1,0:T(8,128)S(1)}, f32[3,2,48,128]{3,2,1,0:T(8,128)S(1)}, f32[2,40,128]{2,1,0:T(8,128)S(...) custom-call(f32[19,2,48,128]{3,2,1,0:T(8,128)S(1)} %get-tuple-element.65.refs_0_, ...), custom_call_target="tpu_custom_call" | custom-call | bytes 2252800 | tf_op jit(solution)/shard_map/pallas_call | solution.py:815
  39.6 0.1 collective-permute-start.6
  39.7 6.3 %collective-permute-start.7 = (f32[3,40,128]{2,1,0:T(8,128)S(1)}, f32[3,40,128]{2,1,0:T(8,128)S(1)}, u32[]{:S(2)}, u32[]{:S(2)}) collective-permute-start(f32[3,40,128]{2,1,0:T(8,128)S(1)} %get-tuple-element.75), channel_id=1, source_target_pairs={{4,0},{8,4},{12,8},{16,12},{20,16},{24,20},{28,24},{32,28},{36,32}... | collective-permute-start | bytes 184328 | tf_op jit(solution)/shard_map/ppermute | solution.py:836
  46.0 1.9 %collective-permute-done.6.from_left = f32[3,40,128]{2,1,0:T(8,128)S(1)} collective-permute-done((f32[3,40,128]{2,1,0:T(8,128)S(1)}, f32[3,40,128]{2,1,0:T(8,128)S(1)}, u32[]{:S(2)}, u32[]{:S(2)}) %collective-permute-start.6) | collective-permute-done | bytes 61472 | tf_op jit(solution)/shard_map/ppermute | solution.py:835
  47.9 0.0 collective-permute-done.7.from_right
  47.9 1.4 %shard_map.73 = (f32[19,2,64,128]{3,2,1,0:T(8,128)S(1)}, f32[10,2,64,128]{3,2,1,0:T(8,128)S(1)}, f32[2,40,128]{2,1,0:T(8,128)S(1)}, f32[280,128]{1,0:T(8,128)S(1...) custom-call(f32[2,40,128]{2,1,0:T(8,128)S(1)} %get-tuple-element.73.misfit, ...), custom_call_target="tpu_custom_call" | custom-call | bytes 1687552 | tf_op jit(solution)/shard_map/pallas_call | solution.py:815
  49.3 0.1 collective-permute-start.8
  49.4 5.7 %collective-permute-start.9 = (f32[280,128]{1,0:T(8,128)S(1)}, f32[280,128]{1,0:T(8,128)S(1)}, u32[]{:S(2)}, u32[]{:S(2)}) collective-permute-start(f32[280,128]{1,0:T(8,128)S(1)} %get-tuple-element.86), channel_id=1, source_target_pairs={{4,0},{8,4},{12,8},{16,12},{20,16},{24,20},{28,24},{32,28},{36,32}... | collective-permute-start | bytes 430088 | tf_op jit(solution)/shard_map/ppermute | solution.py:836
  55.1 2.8 %collective-permute-done.8.from_left = f32[280,128]{1,0:T(8,128)S(1)} collective-permute-done((f32[280,128]{1,0:T(8,128)S(1)}, f32[280,128]{1,0:T(8,128)S(1)}, u32[]{:S(2)}, u32[]{:S(2)}) %collective-permute-start.8) | collective-permute-done | bytes 143392 | tf_op jit(solution)/shard_map/ppermute | solution.py:835
  57.9 0.0 collective-permute-done.9.from_right
  57.9 0.7 %shard_map.74 = (f32[2,32,128]{2,1,0:T(8,128)S(1)}, f32[1,256]{1,0:T(1,128)S(1)}) custom-call(f32[19,2,64,128]{3,2,1,0:T(8,128)S(1)} %get-tuple-element.80.adjoint, f32[10,2,64,128]{3,2,1,0:T(8,128)S(1)} %get-tuple-element.81.turned, f32[2,40,128]{2,1,0:T(8,128)S(1)} %get-tuple-element.82.wall, f32[3,40,128]{2,1,0:T(8,128)S(1)} %get-tuple-element.83.part_left, ...), custom_call_target="tpu_custom_call" | custom-call | bytes 3694592 | tf_op jit(solution)/shard_map/pallas_call | solution.py:815
  58.6 2.0 %collective-permute-start.12 = (f32[1,256]{1,0:T(1,128)S(1)}, f32[1,256]{1,0:T(1,128)S(1)}, u32[]{:S(2)}, u32[]{:S(2)}) collective-permute-start(f32[1,256]{1,0:T(1,128)S(1)} %get-tuple-element.91), channel_id=1, source_target_pairs={{0,3},{1,0},{2,1},{3,2},{4,7},{5,4},{6,5},{7,6},{8,11},{9,8},{10,9... | collective-permute-start | bytes 3080 | tf_op jit(solution)/shard_map/ppermute | solution.py:909
  60.6 2.7 %collective-permute-start.11 = (f32[1,256]{1,0:T(1,128)S(1)}, f32[1,256]{1,0:T(1,128)S(1)}, u32[]{:S(2)}, u32[]{:S(2)}) collective-permute-start(f32[1,256]{1,0:T(1,128)S(1)} %get-tuple-element.91), channel_id=1, source_target_pairs={{0,2},{1,3},{2,0},{3,1},{4,6},{5,7},{6,4},{7,5},{8,10},{9,11},{10,... | collective-permute-start | bytes 3080 | tf_op jit(solution)/shard_map/ppermute | solution.py:909
  63.3 0.6 collective-permute-start.10
  63.9 1.3 %shard_map.75 = f32[19,2,32,128]{3,2,1,0:T(8,128)} custom-call(f32[19,2,64,128]{3,2,1,0:T(8,128)S(1)} %get-tuple-element.80.adjoint, f32[10,2,64,128]{3,2,1,0:T(8,128)S(1)} %get-tuple-element.81.turned, f32[2,32,128]{2,1,0:T(8,128)S(1)} %get-tuple-element.89.more, f32[280,128]{1,0:T(8,128)S(1)} %collective-permute-done.8.from_left, ...), custom_call_target="tpu_custom_call" | custom-call | bytes 3448832 | tf_op jit(solution)/shard_map/pallas_call | solution.py:815
  65.2 0.0 collective-permute-done.12
  65.2 0.0 collective-permute-done.11
  65.2 0.0 collective-permute-done.10
  65.2 0.6 add_add_fusion
Async XLA Ops:
  2.5 7.1 %collective-permute-start = (f32[22,2,8,128]{3,2,1,0:T(8,128)}, f32[22,2,8,128]{3,2,1,0:T(8,128)S(1)}, u32[]{:S(2)}, u32[]{:S(2)}) collective-permute-start(f32[22,2,8,128]{3,2,1,0:T(8,128)} %get-tuple-element.48), channel_id=1, source_target_pairs={{0,1},{1,2},{2,3},{3,0},{4,5},{5,6},{6,7},{7,4},{8,9},{9,10},{10,1... | collective-permute-start | bytes 540680 | tf_op jit(solution)/shard_map/ppermute | solution.py:835
  6.9 6.8 %collective-permute-start.1 = (f32[22,2,8,128]{3,2,1,0:T(8,128)}, f32[22,2,8,128]{3,2,1,0:T(8,128)S(1)}, u32[]{:S(2)}, u32[]{:S(2)}) collective-permute-start(f32[22,2,8,128]{3,2,1,0:T(8,128)} %get-tuple-element.49), channel_id=1, source_target_pairs={{1,0},{2,1},{3,2},{0,3},{5,4},{6,5},{7,6},{4,7},{9,8},{10,9},{11,1... | collective-permute-start | bytes 540680 | tf_op jit(solution)/shard_map/ppermute | solution.py:836
  6.9 1.1 %copy-start = (f32[19,2,32,128]{3,2,1,0:T(8,128)S(1)}, f32[19,2,32,128]{3,2,1,0:T(8,128)}, u32[]{:S(2)}) copy-start(f32[19,2,32,128]{3,2,1,0:T(8,128)} %pops.3) | copy-start | bytes 1867780
  8.0 0.9 %copy-start.1 = (f32[4,2,32,128]{3,2,1,0:T(8,128)S(1)}, f32[4,2,32,128]{3,2,1,0:T(8,128)}, u32[]{:S(2)}) copy-start(f32[4,2,32,128]{3,2,1,0:T(8,128)} %get-tuple-element.47.small) | copy-start | bytes 393220
  13.9 12.4 %collective-permute-start.2 = (f32[456,128]{1,0:T(8,128)S(1)}, f32[456,128]{1,0:T(8,128)S(1)}, u32[]{:S(2)}, u32[]{:S(2)}) collective-permute-start(f32[456,128]{1,0:T(8,128)S(1)} %get-tuple-element.63), channel_id=1, source_target_pairs={{0,4},{4,8},{8,12},{12,16},{16,20},{20,24},{24,28},{28,32},{32,36}... | collective-permute-start | bytes 700424 | tf_op jit(solution)/shard_map/ppermute | solution.py:835
  15.1 11.3 %collective-permute-start.3 = (f32[456,128]{1,0:T(8,128)S(1)}, f32[456,128]{1,0:T(8,128)S(1)}, u32[]{:S(2)}, u32[]{:S(2)}) collective-permute-start(f32[456,128]{1,0:T(8,128)S(1)} %get-tuple-element.64), channel_id=1, source_target_pairs={{4,0},{8,4},{12,8},{16,12},{20,16},{24,20},{28,24},{32,28},{36,32}... | collective-permute-start | bytes 700424 | tf_op jit(solution)/shard_map/ppermute | solution.py:836
  27.7 11.0 %collective-permute-start.4 = (f32[376,128]{1,0:T(8,128)S(1)}, f32[376,128]{1,0:T(8,128)S(1)}, u32[]{:S(2)}, u32[]{:S(2)}) collective-permute-start(f32[376,128]{1,0:T(8,128)S(1)} %get-tuple-element.71), channel_id=1, source_target_pairs={{0,4},{4,8},{8,12},{12,16},{16,20},{20,24},{24,28},{28,32},{32,36}... | collective-permute-start | bytes 577544 | tf_op jit(solution)/shard_map/ppermute | solution.py:835
  27.8 10.9 %collective-permute-start.5 = (f32[376,128]{1,0:T(8,128)S(1)}, f32[376,128]{1,0:T(8,128)S(1)}, u32[]{:S(2)}, u32[]{:S(2)}) collective-permute-start(f32[376,128]{1,0:T(8,128)S(1)} %get-tuple-element.72), channel_id=1, source_target_pairs={{4,0},{8,4},{12,8},{16,12},{20,16},{24,20},{28,24},{32,28},{36,32}... | collective-permute-start | bytes 577544 | tf_op jit(solution)/shard_map/ppermute | solution.py:836
  39.6 8.3 %collective-permute-start.6 = (f32[3,40,128]{2,1,0:T(8,128)S(1)}, f32[3,40,128]{2,1,0:T(8,128)S(1)}, u32[]{:S(2)}, u32[]{:S(2)}) collective-permute-start(f32[3,40,128]{2,1,0:T(8,128)S(1)} %get-tuple-element.74), channel_id=1, source_target_pairs={{0,4},{4,8},{8,12},{12,16},{16,20},{20,24},{24,28},{28,32},{32,36}... | collective-permute-start | bytes 184328 | tf_op jit(solution)/shard_map/ppermute | solution.py:835
  39.7 8.2 %collective-permute-start.7 = (f32[3,40,128]{2,1,0:T(8,128)S(1)}, f32[3,40,128]{2,1,0:T(8,128)S(1)}, u32[]{:S(2)}, u32[]{:S(2)}) collective-permute-start(f32[3,40,128]{2,1,0:T(8,128)S(1)} %get-tuple-element.75), channel_id=1, source_target_pairs={{4,0},{8,4},{12,8},{16,12},{20,16},{24,20},{28,24},{32,28},{36,32}... | collective-permute-start | bytes 184328 | tf_op jit(solution)/shard_map/ppermute | solution.py:836
  49.3 8.6 %collective-permute-start.8 = (f32[280,128]{1,0:T(8,128)S(1)}, f32[280,128]{1,0:T(8,128)S(1)}, u32[]{:S(2)}, u32[]{:S(2)}) collective-permute-start(f32[280,128]{1,0:T(8,128)S(1)} %get-tuple-element.85), channel_id=1, source_target_pairs={{0,4},{4,8},{8,12},{12,16},{16,20},{20,24},{24,28},{28,32},{32,36}... | collective-permute-start | bytes 430088 | tf_op jit(solution)/shard_map/ppermute | solution.py:835
  49.4 8.5 %collective-permute-start.9 = (f32[280,128]{1,0:T(8,128)S(1)}, f32[280,128]{1,0:T(8,128)S(1)}, u32[]{:S(2)}, u32[]{:S(2)}) collective-permute-start(f32[280,128]{1,0:T(8,128)S(1)} %get-tuple-element.86), channel_id=1, source_target_pairs={{4,0},{8,4},{12,8},{16,12},{20,16},{24,20},{28,24},{32,28},{36,32}... | collective-permute-start | bytes 430088 | tf_op jit(solution)/shard_map/ppermute | solution.py:836
  58.6 6.6 %collective-permute-start.12 = (f32[1,256]{1,0:T(1,128)S(1)}, f32[1,256]{1,0:T(1,128)S(1)}, u32[]{:S(2)}, u32[]{:S(2)}) collective-permute-start(f32[1,256]{1,0:T(1,128)S(1)} %get-tuple-element.91), channel_id=1, source_target_pairs={{0,3},{1,0},{2,1},{3,2},{4,7},{5,4},{6,5},{7,6},{8,11},{9,8},{10,9... | collective-permute-start | bytes 3080 | tf_op jit(solution)/shard_map/ppermute | solution.py:909
  60.6 4.6 %collective-permute-start.11 = (f32[1,256]{1,0:T(1,128)S(1)}, f32[1,256]{1,0:T(1,128)S(1)}, u32[]{:S(2)}, u32[]{:S(2)}) collective-permute-start(f32[1,256]{1,0:T(1,128)S(1)} %get-tuple-element.91), channel_id=1, source_target_pairs={{0,2},{1,3},{2,0},{3,1},{4,6},{5,7},{6,4},{7,5},{8,10},{9,11},{10,... | collective-permute-start | bytes 3080 | tf_op jit(solution)/shard_map/ppermute | solution.py:909
  63.3 1.9 %collective-permute-start.10 = (f32[1,256]{1,0:T(1,128)S(1)}, f32[1,256]{1,0:T(1,128)S(1)}, u32[]{:S(2)}, u32[]{:S(2)}) collective-permute-start(f32[1,256]{1,0:T(1,128)S(1)} %get-tuple-element.91), channel_id=1, source_target_pairs={{0,1},{1,2},{2,3},{3,0},{4,5},{5,6},{6,7},{7,4},{8,9},{9,10},{10,1... | collective-permute-start | bytes 3080 | tf_op jit(solution)/shard_map/ppermute | solution.py:909

commit v5 on v4

--- a/solution.py
+++ b/solution.py
@@ -460,33 +460,58 @@
     each_chunk(functools.partial(send_flow, START, send_left, send_right, flow, field, doubled))
 
 
+def put_field(field, doubled, p, t, value):
+    field[p, tall(t), :] = value
+    doubled[p, tall(t), :] = with_sides(value)
+
+
+def put_masks(masks, p, t, share):
+    masks[0, p, tall(t), :] = share
+    masks[1, p, tall(t), :] = rolled(share, 1)
+    masks[2, p, tall(t), :] = rolled(share, -1)
+
+
+def first_flight_kernel(effective, share, masks, field, doubled):
+    def body(t):
+        for x in range(2):
+            put_field(field, doubled, 2 + x, t, effective[x, flat(t), :])
+            put_masks(masks, 2 + x, t, share[x, flat(t), :])
+
+    each_chunk(body)
+
+
+def second_flight_kernel(state, effective, share, field, doubled, lin):
+    def body(t):
+        for x in range(2):
+            put_field(field, doubled, 2 + x, t, effective[x, flat(t), :])
+            f = {i: state[i, x, flat(t), :] for i in range(19)}
+            linear = linear_part(f, share[x, flat(t), :], range(19))[2]
+            for i in range(19):
+                lin[i, x, flat(t), :] = linear[i]
+
+    each_chunk(body)
+
+
 def step_kernel(is_first, *refs):
     if is_first:
-        (lin, flow, density, effective, share, from_left, from_right,
-         masks, field, speed, pull_out, lin_out, flow_out, density_out, effective_out, send_left, send_right,
-         doubled, relaxed, turned, next_field, next_doubled) = refs
+        (lin, flow, density, effective, share, from_left, from_right, _, _, _,
+         masks, field, doubled, speed, pull_out, state_out, flow_out, density_out, effective_out,
+         send_left, send_right,
+         relaxed, turned, next_field, next_doubled) = refs
     else:
-        (lin, flow, density, effective, share, target, masks, from_left, from_right,
-         field, speed, pull_out, misfit_out, send_left, send_right,
-         doubled, relaxed, turned) = refs
+        (lin, flow, density, share, target, masks, from_left, from_right, _, _,
+         field, doubled, speed, pull_out, misfit_out, send_left, send_right,
+         relaxed, turned) = refs
 
     packed = START if is_first else SECOND
 
     def place(t):
-        def put(p, x, s):
-            field[p, tall(t), :] = x
-            doubled[p, tall(t), :] = with_sides(x)
-            if is_first:
-                masks[0, p, tall(t), :] = s
-                masks[1, p, tall(t), :] = rolled(s, 1)
-                masks[2, p, tall(t), :] = rolled(s, -1)
-
-        for x in range(2):
-            put(2 + x, effective[x, flat(t), :], share[x, flat(t), :])
         for near, come, which in ((1, from_left, RIGHTWARD), (4, from_right, LEFTWARD)):
             s = packed[which].get(come, 9, t) if is_first else masks[0, near, tall(t), :]
             chosen = packed[which].get(come, 8, t)
-            put(near, jnp.where(s > 0, 1.0 - jnp.exp(-chosen), chosen), s)
+            put_field(field, doubled, near, t, jnp.where(s > 0, 1.0 - jnp.exp(-chosen), chosen))
+            if is_first:
+                put_masks(masks, near, t, s)
 
     each_chunk(place)
 
@@ -540,11 +565,12 @@
         lin_sent, chosen_sent = [], []
         for x in range(2):
             s = share[x, flat(t), :]
-            total, momentum, linear = linear_part(streamed(x, lambda dy: tall(t, dy)), s, range(19))
+            f = streamed(x, lambda dy: tall(t, dy))
+            total, momentum, linear = linear_part(f, s, (LEFTWARD, RIGHTWARD)[x])
             held = effective[x, flat(t), :]
             eff = jnp.where(s > 0, 1.0 - jnp.exp(-total), held)
             for i in range(19):
-                lin_out[i, x, flat(t), :] = linear[i]
+                state_out[i, x, flat(t), :] = f[i]
             for a in range(3):
                 flow_out[a, x, flat(t), :] = momentum[a]
             density_out[x, flat(t), :] = total
@@ -869,23 +895,29 @@
     )
     from_left, from_right = both_ways(to_left, to_right, "gx")
     wide6 = (6, TALL, DEPTH)
-    work = (vmem(*wide6), vmem(19, 4, TALL, DEPTH), vmem(10, 4, TALL, DEPTH))
-    masks, field0, speed0, pull0, lin, flow, density, effective, to_left, to_right = call(
+    work = (vmem(19, 4, TALL, DEPTH), vmem(10, 4, TALL, DEPTH))
+    begun = call(first_flight_kernel, (effective, share), ((3, *wide6), wide6, wide6), ())
+    masks, field0, _, speed0, pull0, state, flow, density, effective, to_left, to_right = call(
         functools.partial(step_kernel, True),
-        (lin, flow, density, effective, share, from_left, from_right),
+        (lin, flow, density, effective, share, from_left, from_right, *begun),
         (
-            (3, *wide6), wide6, (3, 4, *plane), (3, *two),
+            (3, *wide6), wide6, wide6, (3, 4, *plane), (3, *two),
             (19, *two), (3, *two), two, two, SECOND[LEFTWARD].shape, SECOND[RIGHTWARD].shape,
         ),
         (*work, *beside),
+        filled=3,
     )
     from_left, from_right = both_ways(to_left, to_right, "gx")
     less = (MID, DEPTH)
-    field1, speed1, pull1, misfit, to_left, to_right = call(
+    field1, doubled, lin = call(
+        second_flight_kernel, (state, effective, share), (wide6, wide6, (19, *two)), ()
+    )
+    field1, _, speed1, pull1, misfit, to_left, to_right = call(
         functools.partial(step_kernel, False),
-        (lin, flow, density, effective, share, target_wide, masks, from_left, from_right),
-        (wide6, (3, 4, *plane), (3, *two), (2, *less), (3, *less), (3, *less)),
+        (lin, flow, density, share, target_wide, masks, from_left, from_right, field1, doubled),
+        (wide6, wide6, (3, 4, *plane), (3, *two), (2, *less), (3, *less), (3, *less)),
         work,
+        filled=2,
     )
     from_left, from_right = both_ways(to_left, to_right, "gx")
     pulled = (vmem(3, 4, TALL, DEPTH), vmem(2, 4, TALL, DEPTH))

time: 66.3 us -> 66 us (level)
    pallas_call x8 -> x10, Pallas kernels: 8.23 us -> 8.35 us  [call(): pl.pallas_call(kernel, out_shape=[s if hasattr(s, 'dtype') else jax.Shape...]
where the time goes in v5:
time: 66 us; the launch traced here: 65.5 us
  starting transfers between devices  35.8 us (54%)
  waiting for transfers between devices  18 us (27%)
  Pallas kernels  8.35 us (13%)
  local copies, waits for them, and re-layouts  1.98 us (3%)
  between operations  0.73 us (1%)
    ppermute x5, starting transfers between devices, both_ways(): from_upper = lax.ppermute(to_lower, axis, down)  24.8 us
    ppermute x5, waiting for transfers between devices, both_ways(): from_lower = lax.ppermute(to_upper, axis, up)  13.9 us
    pallas_call x10, Pallas kernels, call(): pl.pallas_call(kernel, out_shape=[s if hasattr(s, 'dtype') else jax.Shape...  8.35 us
    ppermute x5, starting transfers between devices, both_ways(): from_lower = lax.ppermute(to_upper, axis, up)  5.74 us
    ppermute x3, starting transfers between devices, per_device(): lax.ppermute(label_part, 'gy', [(i, (i + step) % count) for i in range(co...  5.23 us
    ppermute x5, waiting for transfers between devices, both_ways(): from_upper = lax.ppermute(to_lower, axis, down)  4.07 us
    unnamed x4, local copies, waits for them, and re-layouts  1.98 us
  transfers between devices with their start and end apart: 13, of which 6 were waited for; matrix products, arithmetic and copies ran while one was open for 0% of the time, Pallas kernels for 3%

profile of v5, /device:TPU:1, one launch (start us, length us, event | category | flops | bytes accessed | tf_op | source)
XLA Modules:
  0.0 65.5 jit_solution(3600133065116319486)
XLA Ops:
  0.6 1.9 %shard_map.68 = (f32[22,2,8,128]{3,2,1,0:T(8,128)}, f32[22,2,8,128]{3,2,1,0:T(8,128)}, f32[4,2,32,128]{3,2,1,0:T(8,128)}) custom-call(f32[19,2,32,128]{3,2,1,0:T(8,128)} %pops.3, s32[2,32,128]{2,1,0:T(8,128)} %fluid.1, s32[2,32,128]{2,1,0:T(8,128)} %label.1, f32[2,32,128]{2,1,0:T(8,128)} %target.1, f32[2,128]{1,0:T(2,128)} %bitcast.2), custom_call_target="tpu_custom_call" | custom-call | bytes 721920 | tf_op jit(solution)/shard_map/pallas_call | solution.py:841
  2.5 4.4 %collective-permute-start = (f32[22,2,8,128]{3,2,1,0:T(8,128)}, f32[22,2,8,128]{3,2,1,0:T(8,128)S(1)}, u32[]{:S(2)}, u32[]{:S(2)}) collective-permute-start(f32[22,2,8,128]{3,2,1,0:T(8,128)} %get-tuple-element.54), channel_id=1, source_target_pairs={{0,1},{1,2},{2,3},{3,0},{4,5},{5,6},{6,7},{7,4},{8,9},{9,10},{10,1... | collective-permute-start | bytes 540680 | tf_op jit(solution)/shard_map/ppermute | solution.py:861
  6.9 0.0 collective-permute-start.1
  6.9 0.0 copy-start
  6.9 1.1 %copy-done = f32[19,2,32,128]{3,2,1,0:T(8,128)S(1)} copy-done((f32[19,2,32,128]{3,2,1,0:T(8,128)S(1)}, f32[19,2,32,128]{3,2,1,0:T(8,128)}, u32[]{:S(2)}) %copy-start) | copy-done | bytes 622616
  8.0 0.0 copy-start.1
  8.0 0.9 %copy-done.1 = f32[4,2,32,128]{3,2,1,0:T(8,128)S(1)} copy-done((f32[4,2,32,128]{3,2,1,0:T(8,128)S(1)}, f32[4,2,32,128]{3,2,1,0:T(8,128)}, u32[]{:S(2)}) %copy-start.1) | copy-done | bytes 131096
  8.9 0.4 shard_map.69
  9.3 0.4 collective-permute-done.below
  9.7 4.1 %collective-permute-done.1.above = f32[22,2,8,128]{3,2,1,0:T(8,128)S(1)} collective-permute-done((f32[22,2,8,128]{3,2,1,0:T(8,128)}, f32[22,2,8,128]{3,2,1,0:T(8,128)S(1)}, u32[]{:S(2)}, u32[]{:S(2)}) %collective-permute-start.1) | collective-permute-done | bytes 180256 | tf_op jit(solution)/shard_map/ppermute | solution.py:862
  13.7 0.2 shard_map.70
  13.9 1.1 %collective-permute-start.2 = (f32[456,128]{1,0:T(8,128)S(1)}, f32[456,128]{1,0:T(8,128)S(1)}, u32[]{:S(2)}, u32[]{:S(2)}) collective-permute-start(f32[456,128]{1,0:T(8,128)S(1)} %get-tuple-element.69), channel_id=1, source_target_pairs={{0,4},{4,8},{8,12},{12,16},{16,20},{20,24},{24,28},{28,32},{32,36}... | collective-permute-start | bytes 700424 | tf_op jit(solution)/shard_map/ppermute | solution.py:861
  15.1 6.8 %collective-permute-start.3 = (f32[456,128]{1,0:T(8,128)S(1)}, f32[456,128]{1,0:T(8,128)S(1)}, u32[]{:S(2)}, u32[]{:S(2)}) collective-permute-start(f32[456,128]{1,0:T(8,128)S(1)} %get-tuple-element.70), channel_id=1, source_target_pairs={{4,0},{8,4},{12,8},{16,12},{20,16},{24,20},{28,24},{32,28},{36,32}... | collective-permute-start | bytes 700424 | tf_op jit(solution)/shard_map/ppermute | solution.py:862
  21.8 0.1 shard_map.71
  21.9 4.4 %collective-permute-done.2.refs_5_ = f32[456,128]{1,0:T(8,128)S(1)} collective-permute-done((f32[456,128]{1,0:T(8,128)S(1)}, f32[456,128]{1,0:T(8,128)S(1)}, u32[]{:S(2)}, u32[]{:S(2)}) %collective-permute-start.2) | collective-permute-done | bytes 233504 | tf_op jit(solution)/shard_map/ppermute | solution.py:861
  26.3 0.0 collective-permute-done.3.refs_6_
  26.3 1.1 %shard_map.72 = (f32[3,6,64,128]{3,2,1,0:T(8,128)S(1)}, f32[6,64,128]{2,1,0:T(8,128)S(1)}, f32[6,64,128]{2,1,0:T(8,128)S(1)}, f32[3,4,48,128]{3,2,1,0:T(8,128)S(...) custom-call(f32[19,2,48,128]{3,2,1,0:T(8,128)S(1)} %get-tuple-elemen, ...), custom_call_target="tpu_custom_call", output_to_operand_aliasing={{0}: (7, {}), {1}: (8, {}), {2}: (9, {})} | custom-call | bytes 2678784 | tf_op jit(solution)/shard_map/pallas_call | solution.py:841
  27.5 0.1 collective-permute-start.4
  27.5 6.1 %collective-permute-start.5 = (f32[376,128]{1,0:T(8,128)S(1)}, f32[376,128]{1,0:T(8,128)S(1)}, u32[]{:S(2)}, u32[]{:S(2)}) collective-permute-start(f32[376,128]{1,0:T(8,128)S(1)} %get-tuple-element.82), channel_id=1, source_target_pairs={{4,0},{8,4},{12,8},{16,12},{20,16},{24,20},{28,24},{32,28},{36,32}... | collective-permute-start | bytes 577544 | tf_op jit(solution)/shard_map/ppermute | solution.py:862
  33.7 0.3 shard_map.73
  34.0 4.5 %collective-permute-done.4.refs_6_ = f32[376,128]{1,0:T(8,128)S(1)} collective-permute-done((f32[376,128]{1,0:T(8,128)S(1)}, f32[376,128]{1,0:T(8,128)S(1)}, u32[]{:S(2)}, u32[]{:S(2)}) %collective-permute-start.4) | collective-permute-done | bytes 192544 | tf_op jit(solution)/shard_map/ppermute | solution.py:861
  38.5 0.0 collective-permute-done.5.refs_7_
  38.5 0.9 %shard_map.74 = (f32[6,64,128]{2,1,0:T(8,128)S(1)}, f32[6,64,128]{2,1,0:T(8,128)S(1)}, f32[3,4,48,128]{3,2,1,0:T(8,128)S(1)}, f32[3,2,48,128]{3,2,1,0:T(8,128)S(...) custom-call(f32[19,2,48,128]{3,2,1,0:T(8,128)S(1)} %get-tuple-elemen, ...), custom_call_target="tpu_custom_call", output_to_operand_aliasing={{0}: (8, {}), {1}: (9, {})} | custom-call | bytes 2596864 | tf_op jit(solution)/shard_map/pallas_call | solution.py:841
  39.3 0.1 collective-permute-start.6
  39.4 6.3 %collective-permute-start.7 = (f32[3,40,128]{2,1,0:T(8,128)S(1)}, f32[3,40,128]{2,1,0:T(8,128)S(1)}, u32[]{:S(2)}, u32[]{:S(2)}) collective-permute-start(f32[3,40,128]{2,1,0:T(8,128)S(1)} %get-tuple-element.87), channel_id=1, source_target_pairs={{4,0},{8,4},{12,8},{16,12},{20,16},{24,20},{28,24},{32,28},{36,32}... | collective-permute-start | bytes 184328 | tf_op jit(solution)/shard_map/ppermute | solution.py:862
  45.7 1.9 %collective-permute-done.6.from_left = f32[3,40,128]{2,1,0:T(8,128)S(1)} collective-permute-done((f32[3,40,128]{2,1,0:T(8,128)S(1)}, f32[3,40,128]{2,1,0:T(8,128)S(1)}, u32[]{:S(2)}, u32[]{:S(2)}) %collective-permute-start.6) | collective-permute-done | bytes 61472 | tf_op jit(solution)/shard_map/ppermute | solution.py:861
  47.6 0.0 collective-permute-done.7.from_right
  47.6 1.4 %shard_map.75 = (f32[19,2,64,128]{3,2,1,0:T(8,128)S(1)}, f32[10,2,64,128]{3,2,1,0:T(8,128)S(1)}, f32[2,40,128]{2,1,0:T(8,128)S(1)}, f32[280,128]{1,0:T(8,128)S(1...) custom-call(f32[2,40,128]{2,1,0:T(8,128)S(1)} %get-tuple-element.85.misfit, ...), custom_call_target="tpu_custom_call" | custom-call | bytes 1687552 | tf_op jit(solution)/shard_map/pallas_call | solution.py:841
  49.0 0.1 collective-permute-start.8
  49.1 5.7 %collective-permute-start.9 = (f32[280,128]{1,0:T(8,128)S(1)}, f32[280,128]{1,0:T(8,128)S(1)}, u32[]{:S(2)}, u32[]{:S(2)}) collective-permute-start(f32[280,128]{1,0:T(8,128)S(1)} %get-tuple-element.98), channel_id=1, source_target_pairs={{4,0},{8,4},{12,8},{16,12},{20,16},{24,20},{28,24},{32,28},{36,32}... | collective-permute-start | bytes 430088 | tf_op jit(solution)/shard_map/ppermute | solution.py:862
  54.8 2.8 %collective-permute-done.8.from_left = f32[280,128]{1,0:T(8,128)S(1)} collective-permute-done((f32[280,128]{1,0:T(8,128)S(1)}, f32[280,128]{1,0:T(8,128)S(1)}, u32[]{:S(2)}, u32[]{:S(2)}) %collective-permute-start.8) | collective-permute-done | bytes 143392 | tf_op jit(solution)/shard_map/ppermute | solution.py:861
  57.6 0.0 collective-permute-done.9.from_right
  57.6 0.7 %shard_map.76 = (f32[2,32,128]{2,1,0:T(8,128)S(1)}, f32[1,256]{1,0:T(1,128)S(1)}) custom-call(f32[19,2,64,128]{3,2,1,0:T(8,128)S(1)} %get-tuple-element.92.adjoint, f32[10,2,64,128]{3,2,1,0:T(8,128)S(1)} %get-tuple-element.93.turned, f32[2,40,128]{2,1,0:T(8,128)S(1)} %get-tuple-element.94.wall, f32[3,40,128]{2,1,0:T(8,128)S(1)} %get-tuple-element.95.part_left, ...), custom_call_target="tpu_custom_call" | custom-call | bytes 3694592 | tf_op jit(solution)/shard_map/pallas_call | solution.py:841
  58.3 2.0 %collective-permute-start.12 = (f32[1,256]{1,0:T(1,128)S(1)}, f32[1,256]{1,0:T(1,128)S(1)}, u32[]{:S(2)}, u32[]{:S(2)}) collective-permute-start(f32[1,256]{1,0:T(1,128)S(1)} %get-tuple-element.103), channel_id=1, source_target_pairs={{0,3},{1,0},{2,1},{3,2},{4,7},{5,4},{6,5},{7,6},{8,11},{9,8},{10,9... | collective-permute-start | bytes 3080 | tf_op jit(solution)/shard_map/ppermute | solution.py:941
  60.3 2.7 %collective-permute-start.11 = (f32[1,256]{1,0:T(1,128)S(1)}, f32[1,256]{1,0:T(1,128)S(1)}, u32[]{:S(2)}, u32[]{:S(2)}) collective-permute-start(f32[1,256]{1,0:T(1,128)S(1)} %get-tuple-element.103), channel_id=1, source_target_pairs={{0,2},{1,3},{2,0},{3,1},{4,6},{5,7},{6,4},{7,5},{8,10},{9,11},{10,... | collective-permute-start | bytes 3080 | tf_op jit(solution)/shard_map/ppermute | solution.py:941
  63.0 0.6 collective-permute-start.10
  63.6 1.3 %shard_map.77 = f32[19,2,32,128]{3,2,1,0:T(8,128)} custom-call(f32[19,2,64,128]{3,2,1,0:T(8,128)S(1)} %get-tuple-element.92.adjoint, f32[10,2,64,128]{3,2,1,0:T(8,128)S(1)} %get-tuple-element.93.turned, f32[2,32,128]{2,1,0:T(8,128)S(1)} %get-tuple-element.101.more, f32[280,128]{1,0:T(8,128)S(1)} %collective-permute-done.8.from_left, ...), custom_call_target="tpu_custom_call" | custom-call | bytes 3448832 | tf_op jit(solution)/shard_map/pallas_call | solution.py:841
  64.9 0.0 collective-permute-done.12
  64.9 0.0 collective-permute-done.11
  64.9 0.0 collective-permute-done.10
  64.9 0.6 add_add_fusion
Async XLA Ops:
  2.5 7.1 %collective-permute-start = (f32[22,2,8,128]{3,2,1,0:T(8,128)}, f32[22,2,8,128]{3,2,1,0:T(8,128)S(1)}, u32[]{:S(2)}, u32[]{:S(2)}) collective-permute-start(f32[22,2,8,128]{3,2,1,0:T(8,128)} %get-tuple-element.54), channel_id=1, source_target_pairs={{0,1},{1,2},{2,3},{3,0},{4,5},{5,6},{6,7},{7,4},{8,9},{9,10},{10,1... | collective-permute-start | bytes 540680 | tf_op jit(solution)/shard_map/ppermute | solution.py:861
  6.9 6.8 %collective-permute-start.1 = (f32[22,2,8,128]{3,2,1,0:T(8,128)}, f32[22,2,8,128]{3,2,1,0:T(8,128)S(1)}, u32[]{:S(2)}, u32[]{:S(2)}) collective-permute-start(f32[22,2,8,128]{3,2,1,0:T(8,128)} %get-tuple-element.55), channel_id=1, source_target_pairs={{1,0},{2,1},{3,2},{0,3},{5,4},{6,5},{7,6},{4,7},{9,8},{10,9},{11,1... | collective-permute-start | bytes 540680 | tf_op jit(solution)/shard_map/ppermute | solution.py:862
  6.9 1.1 %copy-start = (f32[19,2,32,128]{3,2,1,0:T(8,128)S(1)}, f32[19,2,32,128]{3,2,1,0:T(8,128)}, u32[]{:S(2)}) copy-start(f32[19,2,32,128]{3,2,1,0:T(8,128)} %pops.3) | copy-start | bytes 1867780
  8.0 0.9 %copy-start.1 = (f32[4,2,32,128]{3,2,1,0:T(8,128)S(1)}, f32[4,2,32,128]{3,2,1,0:T(8,128)}, u32[]{:S(2)}) copy-start(f32[4,2,32,128]{3,2,1,0:T(8,128)} %get-tuple-element.53.small) | copy-start | bytes 393220
  13.9 12.4 %collective-permute-start.2 = (f32[456,128]{1,0:T(8,128)S(1)}, f32[456,128]{1,0:T(8,128)S(1)}, u32[]{:S(2)}, u32[]{:S(2)}) collective-permute-start(f32[456,128]{1,0:T(8,128)S(1)} %get-tuple-element.69), channel_id=1, source_target_pairs={{0,4},{4,8},{8,12},{12,16},{16,20},{20,24},{24,28},{28,32},{32,36}... | collective-permute-start | bytes 700424 | tf_op jit(solution)/shard_map/ppermute | solution.py:861
  15.1 11.3 %collective-permute-start.3 = (f32[456,128]{1,0:T(8,128)S(1)}, f32[456,128]{1,0:T(8,128)S(1)}, u32[]{:S(2)}, u32[]{:S(2)}) collective-permute-start(f32[456,128]{1,0:T(8,128)S(1)} %get-tuple-element.70), channel_id=1, source_target_pairs={{4,0},{8,4},{12,8},{16,12},{20,16},{24,20},{28,24},{32,28},{36,32}... | collective-permute-start | bytes 700424 | tf_op jit(solution)/shard_map/ppermute | solution.py:862
  27.5 11.0 %collective-permute-start.4 = (f32[376,128]{1,0:T(8,128)S(1)}, f32[376,128]{1,0:T(8,128)S(1)}, u32[]{:S(2)}, u32[]{:S(2)}) collective-permute-start(f32[376,128]{1,0:T(8,128)S(1)} %get-tuple-element.81), channel_id=1, source_target_pairs={{0,4},{4,8},{8,12},{12,16},{16,20},{20,24},{24,28},{28,32},{32,36}... | collective-permute-start | bytes 577544 | tf_op jit(solution)/shard_map/ppermute | solution.py:861
  27.5 10.9 %collective-permute-start.5 = (f32[376,128]{1,0:T(8,128)S(1)}, f32[376,128]{1,0:T(8,128)S(1)}, u32[]{:S(2)}, u32[]{:S(2)}) collective-permute-start(f32[376,128]{1,0:T(8,128)S(1)} %get-tuple-element.82), channel_id=1, source_target_pairs={{4,0},{8,4},{12,8},{16,12},{20,16},{24,20},{28,24},{32,28},{36,32}... | collective-permute-start | bytes 577544 | tf_op jit(solution)/shard_map/ppermute | solution.py:862
  39.3 8.3 %collective-permute-start.6 = (f32[3,40,128]{2,1,0:T(8,128)S(1)}, f32[3,40,128]{2,1,0:T(8,128)S(1)}, u32[]{:S(2)}, u32[]{:S(2)}) collective-permute-start(f32[3,40,128]{2,1,0:T(8,128)S(1)} %get-tuple-element.86), channel_id=1, source_target_pairs={{0,4},{4,8},{8,12},{12,16},{16,20},{20,24},{24,28},{28,32},{32,36}... | collective-permute-start | bytes 184328 | tf_op jit(solution)/shard_map/ppermute | solution.py:861
  39.4 8.2 %collective-permute-start.7 = (f32[3,40,128]{2,1,0:T(8,128)S(1)}, f32[3,40,128]{2,1,0:T(8,128)S(1)}, u32[]{:S(2)}, u32[]{:S(2)}) collective-permute-start(f32[3,40,128]{2,1,0:T(8,128)S(1)} %get-tuple-element.87), channel_id=1, source_target_pairs={{4,0},{8,4},{12,8},{16,12},{20,16},{24,20},{28,24},{32,28},{36,32}... | collective-permute-start | bytes 184328 | tf_op jit(solution)/shard_map/ppermute | solution.py:862
  49.0 8.6 %collective-permute-start.8 = (f32[280,128]{1,0:T(8,128)S(1)}, f32[280,128]{1,0:T(8,128)S(1)}, u32[]{:S(2)}, u32[]{:S(2)}) collective-permute-start(f32[280,128]{1,0:T(8,128)S(1)} %get-tuple-element.97), channel_id=1, source_target_pairs={{0,4},{4,8},{8,12},{12,16},{16,20},{20,24},{24,28},{28,32},{32,36}... | collective-permute-start | bytes 430088 | tf_op jit(solution)/shard_map/ppermute | solution.py:861
  49.1 8.5 %collective-permute-start.9 = (f32[280,128]{1,0:T(8,128)S(1)}, f32[280,128]{1,0:T(8,128)S(1)}, u32[]{:S(2)}, u32[]{:S(2)}) collective-permute-start(f32[280,128]{1,0:T(8,128)S(1)} %get-tuple-element.98), channel_id=1, source_target_pairs={{4,0},{8,4},{12,8},{16,12},{20,16},{24,20},{28,24},{32,28},{36,32}... | collective-permute-start | bytes 430088 | tf_op jit(solution)/shard_map/ppermute | solution.py:862
  58.3 6.6 %collective-permute-start.12 = (f32[1,256]{1,0:T(1,128)S(1)}, f32[1,256]{1,0:T(1,128)S(1)}, u32[]{:S(2)}, u32[]{:S(2)}) collective-permute-start(f32[1,256]{1,0:T(1,128)S(1)} %get-tuple-element.103), channel_id=1, source_target_pairs={{0,3},{1,0},{2,1},{3,2},{4,7},{5,4},{6,5},{7,6},{8,11},{9,8},{10,9... | collective-permute-start | bytes 3080 | tf_op jit(solution)/shard_map/ppermute | solution.py:941
  60.3 4.6 %collective-permute-start.11 = (f32[1,256]{1,0:T(1,128)S(1)}, f32[1,256]{1,0:T(1,128)S(1)}, u32[]{:S(2)}, u32[]{:S(2)}) collective-permute-start(f32[1,256]{1,0:T(1,128)S(1)} %get-tuple-element.103), channel_id=1, source_target_pairs={{0,2},{1,3},{2,0},{3,1},{4,6},{5,7},{6,4},{7,5},{8,10},{9,11},{10,... | collective-permute-start | bytes 3080 | tf_op jit(solution)/shard_map/ppermute | solution.py:941
  63.0 1.9 %collective-permute-start.10 = (f32[1,256]{1,0:T(1,128)S(1)}, f32[1,256]{1,0:T(1,128)S(1)}, u32[]{:S(2)}, u32[]{:S(2)}) collective-permute-start(f32[1,256]{1,0:T(1,128)S(1)} %get-tuple-element.103), channel_id=1, source_target_pairs={{0,1},{1,2},{2,3},{3,0},{4,5},{5,6},{6,7},{7,4},{8,9},{9,10},{10,1... | collective-permute-start | bytes 3080 | tf_op jit(solution)/shard_map/ppermute | solution.py:941

commit v6 on v5

--- a/solution.py
+++ b/solution.py
@@ -148,46 +148,38 @@
 
 
 def dual(r):
-    get = lambda i: r.get(i)
-    first, diagonal = [], []
-    plus_of, minus_of = [], []
+    rest = r.get(0)
+    even_of, odd_of = [], []
     for a in range(3):
-        p, m = get(axis_index_of(a, 1)), get(axis_index_of(a, -1))
-        even = scale(0.5, add(p, m))
-        odd = scale(0.5, sub(p, m))
-        plus_of.append(even)
-        minus_of.append(odd)
-        first.append(odd)
-        diagonal.append(sub(even, get(0)))
+        plus, minus = r.get(axis_index_of(a, 1)), r.get(axis_index_of(a, -1))
+        even_of.append(add(plus, minus))
+        odd_of.append(sub(plus, minus))
+    trace = add(scale(0.5 * TRACE, add(*even_of)), scale(-3.0 * TRACE - SHEAR, rest))
+    first = [scale(0.5 * SHEAR, odd) for odd in odd_of]
+    diagonal = [add(scale(0.5 * SHEAR, even), trace) for even in even_of]
+    even_part = [scale(0.5 * FOURTH, even) for even in even_of]
+    odd_part = [scale(0.5 * THIRD, odd) for odd in odd_of]
+    rest_part = scale(FOURTH, rest)
     mixed, third, fourth = {}, {}, {}
     for a, b in PLANES:
-        pp, mm = get(edge_index_of(a, b, 1, 1)), get(edge_index_of(a, b, -1, -1))
-        pm, mp = get(edge_index_of(a, b, 1, -1)), get(edge_index_of(a, b, -1, 1))
+        pp, mm = r.get(edge_index_of(a, b, 1, 1)), r.get(edge_index_of(a, b, -1, -1))
+        pm, mp = r.get(edge_index_of(a, b, 1, -1)), r.get(edge_index_of(a, b, -1, 1))
         even, odd, cross, skew = add(pp, mm), sub(pp, mm), add(pm, mp), sub(pm, mp)
-        fourth[a, b] = add(sub(sub(scale(0.25, add(even, cross)), plus_of[a]), plus_of[b]), get(0))
-        mixed[a, b] = scale(0.25, sub(even, cross))
-        third[a, b] = sub(scale(0.25, add(odd, skew)), minus_of[a])
-        third[b, a] = sub(scale(0.25, sub(odd, skew)), minus_of[b])
-    trace = scale(TRACE, add(*diagonal))
-    return (
-        [scale(SHEAR, m) for m in first],
-        [add(scale(SHEAR, m), trace) for m in diagonal],
-        {k: scale(SHEAR, m) for k, m in mixed.items()},
-        {k: scale(THIRD, m) for k, m in third.items()},
-        {k: scale(FOURTH, m) for k, m in fourth.items()},
-    )
+        whole = scale(0.25 * FOURTH, add(even, cross))
+        fourth[a, b] = add(sub(sub(whole, even_part[a]), even_part[b]), rest_part)
+        mixed[a, b] = scale(0.25 * SHEAR, sub(even, cross))
+        third[a, b] = sub(scale(0.25 * THIRD, add(odd, skew)), odd_part[a])
+        third[b, a] = sub(scale(0.25 * THIRD, sub(odd, skew)), odd_part[b])
+    return first, diagonal, mixed, third, fourth
 
 
 def flow_adjoint(first, diagonal, mixed, third, fourth, u):
+    level = scale(2.0 / 3.0, add(*fourth.values()))
     q = []
     for a in range(3):
         b, c = [k for k in range(3) if k != a]
         ab, ac, bc = tuple(sorted((a, b))), tuple(sorted((a, c))), tuple(sorted((b, c)))
-        along = add(
-            scale(2.0, diagonal[a]),
-            scale(2.0 / 3.0, add(fourth[ab], fourth[ac])),
-            scale(-1.0 / 3.0, fourth[bc]),
-        )
+        along = sub(add(scale(2.0, diagonal[a]), level), fourth[bc])
         q.append(
             add(
                 first[a],
@@ -213,12 +205,10 @@
             u[a] * (first[a] + (1.0 / 3.0) * (third[a, b] + third[a, c]) - q[a]),
             diagonal[a] * (1.0 / 3.0 + square[a]),
         )
-    for a, b in PLANES:
-        c = 3 - a - b
-        by_density = by_density + mixed[a, b] * (u[a] * u[b])
-        by_density = by_density + fourth[a, b] * (
-            1.0 / 9.0 + (square[a] + square[b]) * (1.0 / 3.0) - square[c] * (1.0 / 6.0)
-        )
+    level = 1.0 / 9.0 + (square[0] + square[1] + square[2]) * (1.0 / 3.0)
+    by_density = by_density + (fourth[0, 1] + fourth[1, 2] + fourth[0, 2]) * level
+    by_density = by_density - 0.5 * add(*[fourth[a, b] * square[3 - a - b] for a, b in PLANES])
+    by_density = by_density + add(*[mixed[a, b] * (u[a] * u[b]) for a, b in PLANES])
     drift = [q[a] - first[a] for a in range(3)]
     base = {0: r[0]}
     for a in range(3):
@@ -663,7 +653,7 @@
                     open_ = far_masks[(-cz) % 3, (p + cx) // 5, rows(cy), :] > 0
                 else:
                     open_ = mask_ahead(masks, i, p, rows)
-                r[i] = s * jnp.where(open_, there, here)
+                r[i] = jnp.where(open_, there, here)
             psi = field[p, rows(0), :]
             u = [speed[a, p - 1, mid(t), :] for a in range(3)]
             if p in (2, 3):
@@ -674,7 +664,7 @@
                     base[i, p - 2, flat(t), :] = rest[i] + const
             else:
                 q = flow_adjoint(*dual(r), u)
-            put_pulled(pulled, pulled_doubled, p - 1, rows, psi, q)
+            put_pulled(pulled, pulled_doubled, p - 1, rows, s * psi, q)
 
     each_chunk(collide, 0, MID // 8)
 
@@ -826,12 +816,14 @@
 
 
 def exact_dot(values, zero_one):
+    rows = values.shape[0]
     high = values.astype(jnp.bfloat16)
     left = values - high.astype(jnp.float32)
     middle = left.astype(jnp.bfloat16)
     low = (left - middle.astype(jnp.float32)).astype(jnp.bfloat16)
-    dot = lambda part: jnp.dot(part, zero_one, preferred_element_type=jnp.float32)
-    return dot(high) + (dot(middle) + dot(low))
+    parts = jnp.concatenate([high, middle, low], axis=0)
+    sums = jnp.dot(parts, zero_one, preferred_element_type=jnp.float32)
+    return sums[:rows] + (sums[rows : 2 * rows] + sums[2 * rows :])
 
 
 def call(kernel, args, outs, scratch, anywhere=0, grant=12, filled=0):

time: 66 us -> 65.7 us (level)
  no operation moved by 1% of the time
where the time goes in v6:
time: 65.7 us; the launch traced here: 65.1 us
  starting transfers between devices  35.8 us (54%)
  waiting for transfers between devices  18 us (27%)
  Pallas kernels  8.01 us (12%)
  local copies, waits for them, and re-layouts  1.98 us (3%)
  between operations  0.73 us (1%)
    ppermute x5, starting transfers between devices, both_ways(): from_upper = lax.ppermute(to_lower, axis, down)  24.8 us
    ppermute x5, waiting for transfers between devices, both_ways(): from_lower = lax.ppermute(to_upper, axis, up)  13.9 us
    pallas_call x10, Pallas kernels, call(): pl.pallas_call(kernel, out_shape=[s if hasattr(s, 'dtype') else jax.Shape...  8.01 us
    ppermute x5, starting transfers between devices, both_ways(): from_lower = lax.ppermute(to_upper, axis, up)  5.74 us
    ppermute x3, starting transfers between devices, per_device(): lax.ppermute(label_part, 'gy', [(i, (i + step) % count) for i in range(co...  5.23 us
    ppermute x5, waiting for transfers between devices, both_ways(): from_upper = lax.ppermute(to_lower, axis, down)  4.07 us
    unnamed x4, local copies, waits for them, and re-layouts  1.98 us
  transfers between devices with their start and end apart: 13, of which 6 were waited for; matrix products, arithmetic and copies ran while one was open for 0% of the time, Pallas kernels for 3%

profile of v6, /device:TPU:1, one launch (start us, length us, event | category | flops | bytes accessed | tf_op | source)
XLA Modules:
  0.0 65.1 jit_solution(5667847647711479238)
XLA Ops:
  0.6 1.9 %shard_map.68 = (f32[22,2,8,128]{3,2,1,0:T(8,128)}, f32[22,2,8,128]{3,2,1,0:T(8,128)}, f32[4,2,32,128]{3,2,1,0:T(8,128)}) custom-call(f32[19,2,32,128]{3,2,1,0:T(8,128)} %pops.3, s32[2,32,128]{2,1,0:T(8,128)} %fluid.1, s32[2,32,128]{2,1,0:T(8,128)} %label.1, f32[2,32,128]{2,1,0:T(8,128)} %target.1, f32[2,128]{1,0:T(2,128)} %bitcast.2), custom_call_target="tpu_custom_call" | custom-call | bytes 721920 | tf_op jit(solution)/shard_map/pallas_call | solution.py:833
  2.5 4.4 %collective-permute-start = (f32[22,2,8,128]{3,2,1,0:T(8,128)}, f32[22,2,8,128]{3,2,1,0:T(8,128)S(1)}, u32[]{:S(2)}, u32[]{:S(2)}) collective-permute-start(f32[22,2,8,128]{3,2,1,0:T(8,128)} %get-tuple-element.54), channel_id=1, source_target_pairs={{0,1},{1,2},{2,3},{3,0},{4,5},{5,6},{6,7},{7,4},{8,9},{9,10},{10,1... | collective-permute-start | bytes 540680 | tf_op jit(solution)/shard_map/ppermute | solution.py:853
  6.9 0.0 collective-permute-start.1
  6.9 0.0 copy-start
  6.9 1.1 %copy-done = f32[19,2,32,128]{3,2,1,0:T(8,128)S(1)} copy-done((f32[19,2,32,128]{3,2,1,0:T(8,128)S(1)}, f32[19,2,32,128]{3,2,1,0:T(8,128)}, u32[]{:S(2)}) %copy-start) | copy-done | bytes 622616
  8.0 0.0 copy-start.1
  8.0 0.9 %copy-done.1 = f32[4,2,32,128]{3,2,1,0:T(8,128)S(1)} copy-done((f32[4,2,32,128]{3,2,1,0:T(8,128)S(1)}, f32[4,2,32,128]{3,2,1,0:T(8,128)}, u32[]{:S(2)}) %copy-start.1) | copy-done | bytes 131096
  8.9 0.4 shard_map.69
  9.3 0.4 collective-permute-done.below
  9.7 4.1 %collective-permute-done.1.above = f32[22,2,8,128]{3,2,1,0:T(8,128)S(1)} collective-permute-done((f32[22,2,8,128]{3,2,1,0:T(8,128)}, f32[22,2,8,128]{3,2,1,0:T(8,128)S(1)}, u32[]{:S(2)}, u32[]{:S(2)}) %collective-permute-start.1) | collective-permute-done | bytes 180256 | tf_op jit(solution)/shard_map/ppermute | solution.py:854
  13.7 0.2 shard_map.70
  13.9 1.1 %collective-permute-start.2 = (f32[456,128]{1,0:T(8,128)S(1)}, f32[456,128]{1,0:T(8,128)S(1)}, u32[]{:S(2)}, u32[]{:S(2)}) collective-permute-start(f32[456,128]{1,0:T(8,128)S(1)} %get-tuple-element.69), channel_id=1, source_target_pairs={{0,4},{4,8},{8,12},{12,16},{16,20},{20,24},{24,28},{28,32},{32,36}... | collective-permute-start | bytes 700424 | tf_op jit(solution)/shard_map/ppermute | solution.py:853
  15.1 6.8 %collective-permute-start.3 = (f32[456,128]{1,0:T(8,128)S(1)}, f32[456,128]{1,0:T(8,128)S(1)}, u32[]{:S(2)}, u32[]{:S(2)}) collective-permute-start(f32[456,128]{1,0:T(8,128)S(1)} %get-tuple-element.70), channel_id=1, source_target_pairs={{4,0},{8,4},{12,8},{16,12},{20,16},{24,20},{28,24},{32,28},{36,32}... | collective-permute-start | bytes 700424 | tf_op jit(solution)/shard_map/ppermute | solution.py:854
  21.8 0.1 shard_map.71
  21.9 4.4 %collective-permute-done.2.refs_5_ = f32[456,128]{1,0:T(8,128)S(1)} collective-permute-done((f32[456,128]{1,0:T(8,128)S(1)}, f32[456,128]{1,0:T(8,128)S(1)}, u32[]{:S(2)}, u32[]{:S(2)}) %collective-permute-start.2) | collective-permute-done | bytes 233504 | tf_op jit(solution)/shard_map/ppermute | solution.py:853
  26.3 0.0 collective-permute-done.3.refs_6_
  26.3 1.1 %shard_map.72 = (f32[3,6,64,128]{3,2,1,0:T(8,128)S(1)}, f32[6,64,128]{2,1,0:T(8,128)S(1)}, f32[6,64,128]{2,1,0:T(8,128)S(1)}, f32[3,4,48,128]{3,2,1,0:T(8,128)S(...) custom-call(f32[19,2,48,128]{3,2,1,0:T(8,128)S(1)} %get-tuple-elemen, ...), custom_call_target="tpu_custom_call", output_to_operand_aliasing={{0}: (7, {}), {1}: (8, {}), {2}: (9, {})} | custom-call | bytes 2678784 | tf_op jit(solution)/shard_map/pallas_call | solution.py:833
  27.5 0.1 collective-permute-start.4
  27.5 6.1 %collective-permute-start.5 = (f32[376,128]{1,0:T(8,128)S(1)}, f32[376,128]{1,0:T(8,128)S(1)}, u32[]{:S(2)}, u32[]{:S(2)}) collective-permute-start(f32[376,128]{1,0:T(8,128)S(1)} %get-tuple-element.82), channel_id=1, source_target_pairs={{4,0},{8,4},{12,8},{16,12},{20,16},{24,20},{28,24},{32,28},{36,32}... | collective-permute-start | bytes 577544 | tf_op jit(solution)/shard_map/ppermute | solution.py:854
  33.7 0.3 shard_map.73
  34.0 4.5 %collective-permute-done.4.refs_6_ = f32[376,128]{1,0:T(8,128)S(1)} collective-permute-done((f32[376,128]{1,0:T(8,128)S(1)}, f32[376,128]{1,0:T(8,128)S(1)}, u32[]{:S(2)}, u32[]{:S(2)}) %collective-permute-start.4) | collective-permute-done | bytes 192544 | tf_op jit(solution)/shard_map/ppermute | solution.py:853
  38.5 0.0 collective-permute-done.5.refs_7_
  38.5 0.9 %shard_map.74 = (f32[6,64,128]{2,1,0:T(8,128)S(1)}, f32[6,64,128]{2,1,0:T(8,128)S(1)}, f32[3,4,48,128]{3,2,1,0:T(8,128)S(1)}, f32[3,2,48,128]{3,2,1,0:T(8,128)S(...) custom-call(f32[19,2,48,128]{3,2,1,0:T(8,128)S(1)} %get-tuple-elemen, ...), custom_call_target="tpu_custom_call", output_to_operand_aliasing={{0}: (8, {}), {1}: (9, {})} | custom-call | bytes 2596864 | tf_op jit(solution)/shard_map/pallas_call | solution.py:833
  39.3 0.1 collective-permute-start.6
  39.4 6.3 %collective-permute-start.7 = (f32[3,40,128]{2,1,0:T(8,128)S(1)}, f32[3,40,128]{2,1,0:T(8,128)S(1)}, u32[]{:S(2)}, u32[]{:S(2)}) collective-permute-start(f32[3,40,128]{2,1,0:T(8,128)S(1)} %get-tuple-element.87), channel_id=1, source_target_pairs={{4,0},{8,4},{12,8},{16,12},{20,16},{24,20},{28,24},{32,28},{36,32}... | collective-permute-start | bytes 184328 | tf_op jit(solution)/shard_map/ppermute | solution.py:854
  45.7 1.9 %collective-permute-done.6.from_left = f32[3,40,128]{2,1,0:T(8,128)S(1)} collective-permute-done((f32[3,40,128]{2,1,0:T(8,128)S(1)}, f32[3,40,128]{2,1,0:T(8,128)S(1)}, u32[]{:S(2)}, u32[]{:S(2)}) %collective-permute-start.6) | collective-permute-done | bytes 61472 | tf_op jit(solution)/shard_map/ppermute | solution.py:853
  47.6 0.0 collective-permute-done.7.from_right
  47.6 1.2 %shard_map.75 = (f32[19,2,64,128]{3,2,1,0:T(8,128)S(1)}, f32[10,2,64,128]{3,2,1,0:T(8,128)S(1)}, f32[2,40,128]{2,1,0:T(8,128)S(1)}, f32[280,128]{1,0:T(8,128)S(1...) custom-call(f32[2,40,128]{2,1,0:T(8,128)S(1)} %get-tuple-element.85.misfit, ...), custom_call_target="tpu_custom_call" | custom-call | bytes 1687552 | tf_op jit(solution)/shard_map/pallas_call | solution.py:833
  48.9 0.1 collective-permute-start.8
  49.0 5.7 %collective-permute-start.9 = (f32[280,128]{1,0:T(8,128)S(1)}, f32[280,128]{1,0:T(8,128)S(1)}, u32[]{:S(2)}, u32[]{:S(2)}) collective-permute-start(f32[280,128]{1,0:T(8,128)S(1)} %get-tuple-element.98), channel_id=1, source_target_pairs={{4,0},{8,4},{12,8},{16,12},{20,16},{24,20},{28,24},{32,28},{36,32}... | collective-permute-start | bytes 430088 | tf_op jit(solution)/shard_map/ppermute | solution.py:854
  54.6 2.8 %collective-permute-done.8.from_left = f32[280,128]{1,0:T(8,128)S(1)} collective-permute-done((f32[280,128]{1,0:T(8,128)S(1)}, f32[280,128]{1,0:T(8,128)S(1)}, u32[]{:S(2)}, u32[]{:S(2)}) %collective-permute-start.8) | collective-permute-done | bytes 143392 | tf_op jit(solution)/shard_map/ppermute | solution.py:853
  57.4 0.0 collective-permute-done.9.from_right
  57.4 0.6 shard_map.76
  58.0 2.0 %collective-permute-start.12 = (f32[1,256]{1,0:T(1,128)S(1)}, f32[1,256]{1,0:T(1,128)S(1)}, u32[]{:S(2)}, u32[]{:S(2)}) collective-permute-start(f32[1,256]{1,0:T(1,128)S(1)} %get-tuple-element.103), channel_id=1, source_target_pairs={{0,3},{1,0},{2,1},{3,2},{4,7},{5,4},{6,5},{7,6},{8,11},{9,8},{10,9... | collective-permute-start | bytes 3080 | tf_op jit(solution)/shard_map/ppermute | solution.py:933
  60.0 2.7 %collective-permute-start.11 = (f32[1,256]{1,0:T(1,128)S(1)}, f32[1,256]{1,0:T(1,128)S(1)}, u32[]{:S(2)}, u32[]{:S(2)}) collective-permute-start(f32[1,256]{1,0:T(1,128)S(1)} %get-tuple-element.103), channel_id=1, source_target_pairs={{0,2},{1,3},{2,0},{3,1},{4,6},{5,7},{6,4},{7,5},{8,10},{9,11},{10,... | collective-permute-start | bytes 3080 | tf_op jit(solution)/shard_map/ppermute | solution.py:933
  62.7 0.6 collective-permute-start.10
  63.3 1.3 %shard_map.77 = f32[19,2,32,128]{3,2,1,0:T(8,128)} custom-call(f32[19,2,64,128]{3,2,1,0:T(8,128)S(1)} %get-tuple-element.92.adjoint, f32[10,2,64,128]{3,2,1,0:T(8,128)S(1)} %get-tuple-element.93.turned, f32[2,32,128]{2,1,0:T(8,128)S(1)} %get-tuple-element.101.more, f32[280,128]{1,0:T(8,128)S(1)} %collective-permute-done.8.from_left, ...), custom_call_target="tpu_custom_call" | custom-call | bytes 3448832 | tf_op jit(solution)/shard_map/pallas_call | solution.py:833
  64.5 0.0 collective-permute-done.12
  64.5 0.0 collective-permute-done.11
  64.5 0.0 collective-permute-done.10
  64.6 0.6 add_add_fusion
Async XLA Ops:
  2.5 7.1 %collective-permute-start = (f32[22,2,8,128]{3,2,1,0:T(8,128)}, f32[22,2,8,128]{3,2,1,0:T(8,128)S(1)}, u32[]{:S(2)}, u32[]{:S(2)}) collective-permute-start(f32[22,2,8,128]{3,2,1,0:T(8,128)} %get-tuple-element.54), channel_id=1, source_target_pairs={{0,1},{1,2},{2,3},{3,0},{4,5},{5,6},{6,7},{7,4},{8,9},{9,10},{10,1... | collective-permute-start | bytes 540680 | tf_op jit(solution)/shard_map/ppermute | solution.py:853
  6.9 6.8 %collective-permute-start.1 = (f32[22,2,8,128]{3,2,1,0:T(8,128)}, f32[22,2,8,128]{3,2,1,0:T(8,128)S(1)}, u32[]{:S(2)}, u32[]{:S(2)}) collective-permute-start(f32[22,2,8,128]{3,2,1,0:T(8,128)} %get-tuple-element.55), channel_id=1, source_target_pairs={{1,0},{2,1},{3,2},{0,3},{5,4},{6,5},{7,6},{4,7},{9,8},{10,9},{11,1... | collective-permute-start | bytes 540680 | tf_op jit(solution)/shard_map/ppermute | solution.py:854
  6.9 1.1 %copy-start = (f32[19,2,32,128]{3,2,1,0:T(8,128)S(1)}, f32[19,2,32,128]{3,2,1,0:T(8,128)}, u32[]{:S(2)}) copy-start(f32[19,2,32,128]{3,2,1,0:T(8,128)} %pops.3) | copy-start | bytes 1867780
  8.0 0.9 %copy-start.1 = (f32[4,2,32,128]{3,2,1,0:T(8,128)S(1)}, f32[4,2,32,128]{3,2,1,0:T(8,128)}, u32[]{:S(2)}) copy-start(f32[4,2,32,128]{3,2,1,0:T(8,128)} %get-tuple-element.53.small) | copy-start | bytes 393220
  13.9 12.4 %collective-permute-start.2 = (f32[456,128]{1,0:T(8,128)S(1)}, f32[456,128]{1,0:T(8,128)S(1)}, u32[]{:S(2)}, u32[]{:S(2)}) collective-permute-start(f32[456,128]{1,0:T(8,128)S(1)} %get-tuple-element.69), channel_id=1, source_target_pairs={{0,4},{4,8},{8,12},{12,16},{16,20},{20,24},{24,28},{28,32},{32,36}... | collective-permute-start | bytes 700424 | tf_op jit(solution)/shard_map/ppermute | solution.py:853
  15.1 11.3 %collective-permute-start.3 = (f32[456,128]{1,0:T(8,128)S(1)}, f32[456,128]{1,0:T(8,128)S(1)}, u32[]{:S(2)}, u32[]{:S(2)}) collective-permute-start(f32[456,128]{1,0:T(8,128)S(1)} %get-tuple-element.70), channel_id=1, source_target_pairs={{4,0},{8,4},{12,8},{16,12},{20,16},{24,20},{28,24},{32,28},{36,32}... | collective-permute-start | bytes 700424 | tf_op jit(solution)/shard_map/ppermute | solution.py:854
  27.5 11.0 %collective-permute-start.4 = (f32[376,128]{1,0:T(8,128)S(1)}, f32[376,128]{1,0:T(8,128)S(1)}, u32[]{:S(2)}, u32[]{:S(2)}) collective-permute-start(f32[376,128]{1,0:T(8,128)S(1)} %get-tuple-element.81), channel_id=1, source_target_pairs={{0,4},{4,8},{8,12},{12,16},{16,20},{20,24},{24,28},{28,32},{32,36}... | collective-permute-start | bytes 577544 | tf_op jit(solution)/shard_map/ppermute | solution.py:853
  27.5 10.9 %collective-permute-start.5 = (f32[376,128]{1,0:T(8,128)S(1)}, f32[376,128]{1,0:T(8,128)S(1)}, u32[]{:S(2)}, u32[]{:S(2)}) collective-permute-start(f32[376,128]{1,0:T(8,128)S(1)} %get-tuple-element.82), channel_id=1, source_target_pairs={{4,0},{8,4},{12,8},{16,12},{20,16},{24,20},{28,24},{32,28},{36,32}... | collective-permute-start | bytes 577544 | tf_op jit(solution)/shard_map/ppermute | solution.py:854
  39.3 8.3 %collective-permute-start.6 = (f32[3,40,128]{2,1,0:T(8,128)S(1)}, f32[3,40,128]{2,1,0:T(8,128)S(1)}, u32[]{:S(2)}, u32[]{:S(2)}) collective-permute-start(f32[3,40,128]{2,1,0:T(8,128)S(1)} %get-tuple-element.86), channel_id=1, source_target_pairs={{0,4},{4,8},{8,12},{12,16},{16,20},{20,24},{24,28},{28,32},{32,36}... | collective-permute-start | bytes 184328 | tf_op jit(solution)/shard_map/ppermute | solution.py:853
  39.4 8.2 %collective-permute-start.7 = (f32[3,40,128]{2,1,0:T(8,128)S(1)}, f32[3,40,128]{2,1,0:T(8,128)S(1)}, u32[]{:S(2)}, u32[]{:S(2)}) collective-permute-start(f32[3,40,128]{2,1,0:T(8,128)S(1)} %get-tuple-element.87), channel_id=1, source_target_pairs={{4,0},{8,4},{12,8},{16,12},{20,16},{24,20},{28,24},{32,28},{36,32}... | collective-permute-start | bytes 184328 | tf_op jit(solution)/shard_map/ppermute | solution.py:854
  48.9 8.6 %collective-permute-start.8 = (f32[280,128]{1,0:T(8,128)S(1)}, f32[280,128]{1,0:T(8,128)S(1)}, u32[]{:S(2)}, u32[]{:S(2)}) collective-permute-start(f32[280,128]{1,0:T(8,128)S(1)} %get-tuple-element.97), channel_id=1, source_target_pairs={{0,4},{4,8},{8,12},{12,16},{16,20},{20,24},{24,28},{28,32},{32,36}... | collective-permute-start | bytes 430088 | tf_op jit(solution)/shard_map/ppermute | solution.py:853
  49.0 8.5 %collective-permute-start.9 = (f32[280,128]{1,0:T(8,128)S(1)}, f32[280,128]{1,0:T(8,128)S(1)}, u32[]{:S(2)}, u32[]{:S(2)}) collective-permute-start(f32[280,128]{1,0:T(8,128)S(1)} %get-tuple-element.98), channel_id=1, source_target_pairs={{4,0},{8,4},{12,8},{16,12},{20,16},{24,20},{28,24},{32,28},{36,32}... | collective-permute-start | bytes 430088 | tf_op jit(solution)/shard_map/ppermute | solution.py:854
  58.0 6.5 %collective-permute-start.12 = (f32[1,256]{1,0:T(1,128)S(1)}, f32[1,256]{1,0:T(1,128)S(1)}, u32[]{:S(2)}, u32[]{:S(2)}) collective-permute-start(f32[1,256]{1,0:T(1,128)S(1)} %get-tuple-element.103), channel_id=1, source_target_pairs={{0,3},{1,0},{2,1},{3,2},{4,7},{5,4},{6,5},{7,6},{8,11},{9,8},{10,9... | collective-permute-start | bytes 3080 | tf_op jit(solution)/shard_map/ppermute | solution.py:933
  60.0 4.5 %collective-permute-start.11 = (f32[1,256]{1,0:T(1,128)S(1)}, f32[1,256]{1,0:T(1,128)S(1)}, u32[]{:S(2)}, u32[]{:S(2)}) collective-permute-start(f32[1,256]{1,0:T(1,128)S(1)} %get-tuple-element.103), channel_id=1, source_target_pairs={{0,2},{1,3},{2,0},{3,1},{4,6},{5,7},{6,4},{7,5},{8,10},{9,11},{10,... | collective-permute-start | bytes 3080 | tf_op jit(solution)/shard_map/ppermute | solution.py:933
  62.7 1.8 %collective-permute-start.10 = (f32[1,256]{1,0:T(1,128)S(1)}, f32[1,256]{1,0:T(1,128)S(1)}, u32[]{:S(2)}, u32[]{:S(2)}) collective-permute-start(f32[1,256]{1,0:T(1,128)S(1)} %get-tuple-element.103), channel_id=1, source_target_pairs={{0,1},{1,2},{2,3},{3,0},{4,5},{5,6},{6,7},{7,4},{8,9},{9,10},{10,1... | collective-permute-start | bytes 3080 | tf_op jit(solution)/shard_map/ppermute | solution.py:933

commit v7 on v6

--- a/solution.py
+++ b/solution.py
@@ -839,7 +839,7 @@
         input_output_aliases={len(args) - filled + k: k for k in range(filled)},
         compiler_params=pltpu.CompilerParams(vmem_limit_bytes=grant * 1024 * 1024),
         cost_estimate=pl.CostEstimate(flops=0, bytes_accessed=size, transcendentals=0),
-    )(*args)
+    )(*[pltpu.with_memory_space_constraint(a, pltpu.HBM) for a in args[:anywhere]], *args[anywhere:])
 
 
 def ring(axis):
@@ -870,7 +870,6 @@
             pltpu.SemaphoreType.DMA((6,)),
         ),
         anywhere=5,
-        grant=56,
     )
     below, above = both_ways(low, high, "gy")
     blocks = (OWN // 2) * (DEPTH // 4)

time: 65.7 us -> 64.7 us (0.985)
  local copies, waits for them, and re-layouts: 1.98 us -> 1.08 us
  Pallas kernels: 8.01 us -> 7.25 us
    unnamed x4 -> x2, local copies, waits for them, and re-layouts: 1.98 us -> 1.08 us
    pallas_call x10, Pallas kernels: 8.01 us -> 7.25 us  [call(): pl.pallas_call(kernel, out_shape=[s if hasattr(s, 'dtype') else jax.Shape...]
where the time goes in v7:
time: 64.7 us; the launch traced here: 64 us
  starting transfers between devices  35.7 us (55%)
  waiting for transfers between devices  18.6 us (29%)
  Pallas kernels  7.25 us (11%)
  local copies, waits for them, and re-layouts  1.08 us (2%)
  between operations  0.73 us (1%)
    ppermute x5, starting transfers between devices, both_ways(): from_upper = lax.ppermute(to_lower, axis, down)  24.9 us
    ppermute x5, waiting for transfers between devices, both_ways(): from_lower = lax.ppermute(to_upper, axis, up)  14.4 us
    pallas_call x10, Pallas kernels, call(): pl.pallas_call(kernel, out_shape=[s if hasattr(s, 'dtype') else jax.Shape...  7.25 us
    ppermute x5, starting transfers between devices, both_ways(): from_lower = lax.ppermute(to_upper, axis, up)  5.74 us
    ppermute x3, starting transfers between devices, per_device(): lax.ppermute(label_part, 'gy', [(i, (i + step) % count) for i in range(co...  5.13 us
    ppermute x5, waiting for transfers between devices, both_ways(): from_upper = lax.ppermute(to_lower, axis, down)  4.17 us
  transfers between devices with their start and end apart: 13, of which 6 were waited for; matrix products, arithmetic and copies ran while one was open for 0% of the time, Pallas kernels for 3%

profile of v7, /device:TPU:1, one launch (start us, length us, event | category | flops | bytes accessed | tf_op | source)
XLA Modules:
  0.0 64.0 jit_solution(3179358127199067876)
XLA Ops:
  0.6 1.1 %shard_map.68 = (f32[22,2,8,128]{3,2,1,0:T(8,128)S(1)}, f32[22,2,8,128]{3,2,1,0:T(8,128)S(1)}, f32[4,2,32,128]{3,2,1,0:T(8,128)S(1)}) custom-call(f32[19,2,32,128]{3,2,1,0:T(8,128)} %pops.3, s32[2,32,128]{2,1,0:T(8,128)} %fluid.1, s32[2,32,128]{2,1,0:T(8,128)} %label.1, f32[2,32,128]{2,1,0:T(8,128)} %target.1, f32[2,128]{1,0:T(2,128)} %bitcast.2), custom_call_target="tpu_custom_call" | custom-call | bytes 721920 | tf_op jit(solution)/shard_map/pallas_call | solution.py:833
  1.8 4.4 %collective-permute-start = (f32[22,2,8,128]{3,2,1,0:T(8,128)S(1)}, f32[22,2,8,128]{3,2,1,0:T(8,128)S(1)}, u32[]{:S(2)}, u32[]{:S(2)}) collective-permute-start(f32[22,2,8,128]{3,2,1,0:T(8,128)S(1)} %get-tuple-element.54), channel_id=1, source_target_pairs={{0,1},{1,2},{2,3},{3,0},{4,5},{5,6},{6,7},{7,4},{8,9},{9,10},{10,1... | collective-permute-start | bytes 540680 | tf_op jit(solution)/shard_map/ppermute | solution.py:853
  6.1 0.0 collective-permute-start.1
  6.2 0.0 copy-start
  6.2 1.1 %copy-done = f32[19,2,32,128]{3,2,1,0:T(8,128)S(1)} copy-done((f32[19,2,32,128]{3,2,1,0:T(8,128)S(1)}, f32[19,2,32,128]{3,2,1,0:T(8,128)}, u32[]{:S(2)}) %copy-start) | copy-done | bytes 622616
  7.2 0.4 shard_map.69
  7.6 1.0 %collective-permute-done.below = f32[22,2,8,128]{3,2,1,0:T(8,128)S(1)} collective-permute-done((f32[22,2,8,128]{3,2,1,0:T(8,128)S(1)}, f32[22,2,8,128]{3,2,1,0:T(8,128)S(1)}, u32[]{:S(2)}, u32[]{:S(2)}) %collective-permute-start) | collective-permute-done | bytes 180256 | tf_op jit(solution)/shard_map/ppermute | solution.py:853
  8.6 4.2 %collective-permute-done.1.above = f32[22,2,8,128]{3,2,1,0:T(8,128)S(1)} collective-permute-done((f32[22,2,8,128]{3,2,1,0:T(8,128)S(1)}, f32[22,2,8,128]{3,2,1,0:T(8,128)S(1)}, u32[]{:S(2)}, u32[]{:S(2)}) %collective-permute-start.1) | collective-permute-done | bytes 180256 | tf_op jit(solution)/shard_map/ppermute | solution.py:854
  12.8 0.2 shard_map.70
  13.0 1.1 %collective-permute-start.2 = (f32[456,128]{1,0:T(8,128)S(1)}, f32[456,128]{1,0:T(8,128)S(1)}, u32[]{:S(2)}, u32[]{:S(2)}) collective-permute-start(f32[456,128]{1,0:T(8,128)S(1)} %get-tuple-element.69), channel_id=1, source_target_pairs={{0,4},{4,8},{8,12},{12,16},{16,20},{20,24},{24,28},{28,32},{32,36}... | collective-permute-start | bytes 700424 | tf_op jit(solution)/shard_map/ppermute | solution.py:853
  14.1 6.8 %collective-permute-start.3 = (f32[456,128]{1,0:T(8,128)S(1)}, f32[456,128]{1,0:T(8,128)S(1)}, u32[]{:S(2)}, u32[]{:S(2)}) collective-permute-start(f32[456,128]{1,0:T(8,128)S(1)} %get-tuple-element.70), channel_id=1, source_target_pairs={{4,0},{8,4},{12,8},{16,12},{20,16},{24,20},{28,24},{32,28},{36,32}... | collective-permute-start | bytes 700424 | tf_op jit(solution)/shard_map/ppermute | solution.py:854
  20.8 0.1 shard_map.71
  21.0 4.3 %collective-permute-done.2.refs_5_ = f32[456,128]{1,0:T(8,128)S(1)} collective-permute-done((f32[456,128]{1,0:T(8,128)S(1)}, f32[456,128]{1,0:T(8,128)S(1)}, u32[]{:S(2)}, u32[]{:S(2)}) %collective-permute-start.2) | collective-permute-done | bytes 233504 | tf_op jit(solution)/shard_map/ppermute | solution.py:853
  25.2 0.0 collective-permute-done.3.refs_6_
  25.2 1.1 %shard_map.72 = (f32[3,6,64,128]{3,2,1,0:T(8,128)S(1)}, f32[6,64,128]{2,1,0:T(8,128)S(1)}, f32[6,64,128]{2,1,0:T(8,128)S(1)}, f32[3,4,48,128]{3,2,1,0:T(8,128)S(...) custom-call(f32[19,2,48,128]{3,2,1,0:T(8,128)S(1)} %get-tuple-elemen, ...), custom_call_target="tpu_custom_call", output_to_operand_aliasing={{0}: (7, {}), {1}: (8, {}), {2}: (9, {})} | custom-call | bytes 2678784 | tf_op jit(solution)/shard_map/pallas_call | solution.py:833
  26.4 0.1 collective-permute-start.4
  26.5 6.1 %collective-permute-start.5 = (f32[376,128]{1,0:T(8,128)S(1)}, f32[376,128]{1,0:T(8,128)S(1)}, u32[]{:S(2)}, u32[]{:S(2)}) collective-permute-start(f32[376,128]{1,0:T(8,128)S(1)} %get-tuple-element.82), channel_id=1, source_target_pairs={{4,0},{8,4},{12,8},{16,12},{20,16},{24,20},{28,24},{32,28},{36,32}... | collective-permute-start | bytes 577544 | tf_op jit(solution)/shard_map/ppermute | solution.py:854
  32.6 0.3 shard_map.73
  32.9 4.3 %collective-permute-done.4.refs_6_ = f32[376,128]{1,0:T(8,128)S(1)} collective-permute-done((f32[376,128]{1,0:T(8,128)S(1)}, f32[376,128]{1,0:T(8,128)S(1)}, u32[]{:S(2)}, u32[]{:S(2)}) %collective-permute-start.4) | collective-permute-done | bytes 192544 | tf_op jit(solution)/shard_map/ppermute | solution.py:853
  37.2 0.0 collective-permute-done.5.refs_7_
  37.3 0.9 %shard_map.74 = (f32[6,64,128]{2,1,0:T(8,128)S(1)}, f32[6,64,128]{2,1,0:T(8,128)S(1)}, f32[3,4,48,128]{3,2,1,0:T(8,128)S(1)}, f32[3,2,48,128]{3,2,1,0:T(8,128)S(...) custom-call(f32[19,2,48,128]{3,2,1,0:T(8,128)S(1)} %get-tuple-elemen, ...), custom_call_target="tpu_custom_call", output_to_operand_aliasing={{0}: (8, {}), {1}: (9, {})} | custom-call | bytes 2596864 | tf_op jit(solution)/shard_map/pallas_call | solution.py:833
  38.1 0.1 collective-permute-start.6
  38.2 6.3 %collective-permute-start.7 = (f32[3,40,128]{2,1,0:T(8,128)S(1)}, f32[3,40,128]{2,1,0:T(8,128)S(1)}, u32[]{:S(2)}, u32[]{:S(2)}) collective-permute-start(f32[3,40,128]{2,1,0:T(8,128)S(1)} %get-tuple-element.87), channel_id=1, source_target_pairs={{4,0},{8,4},{12,8},{16,12},{20,16},{24,20},{28,24},{32,28},{36,32}... | collective-permute-start | bytes 184328 | tf_op jit(solution)/shard_map/ppermute | solution.py:854
  44.5 2.0 %collective-permute-done.6.from_left = f32[3,40,128]{2,1,0:T(8,128)S(1)} collective-permute-done((f32[3,40,128]{2,1,0:T(8,128)S(1)}, f32[3,40,128]{2,1,0:T(8,128)S(1)}, u32[]{:S(2)}, u32[]{:S(2)}) %collective-permute-start.6) | collective-permute-done | bytes 61472 | tf_op jit(solution)/shard_map/ppermute | solution.py:853
  46.5 0.0 collective-permute-done.7.from_right
  46.5 1.2 %shard_map.75 = (f32[19,2,64,128]{3,2,1,0:T(8,128)S(1)}, f32[10,2,64,128]{3,2,1,0:T(8,128)S(1)}, f32[2,40,128]{2,1,0:T(8,128)S(1)}, f32[280,128]{1,0:T(8,128)S(1...) custom-call(f32[2,40,128]{2,1,0:T(8,128)S(1)} %get-tuple-element.85.misfit, ...), custom_call_target="tpu_custom_call" | custom-call | bytes 1687552 | tf_op jit(solution)/shard_map/pallas_call | solution.py:833
  47.7 0.1 collective-permute-start.8
  47.8 5.7 %collective-permute-start.9 = (f32[280,128]{1,0:T(8,128)S(1)}, f32[280,128]{1,0:T(8,128)S(1)}, u32[]{:S(2)}, u32[]{:S(2)}) collective-permute-start(f32[280,128]{1,0:T(8,128)S(1)} %get-tuple-element.98), channel_id=1, source_target_pairs={{4,0},{8,4},{12,8},{16,12},{20,16},{24,20},{28,24},{32,28},{36,32}... | collective-permute-start | bytes 430088 | tf_op jit(solution)/shard_map/ppermute | solution.py:854
  53.5 2.9 %collective-permute-done.8.from_left = f32[280,128]{1,0:T(8,128)S(1)} collective-permute-done((f32[280,128]{1,0:T(8,128)S(1)}, f32[280,128]{1,0:T(8,128)S(1)}, u32[]{:S(2)}, u32[]{:S(2)}) %collective-permute-start.8) | collective-permute-done | bytes 143392 | tf_op jit(solution)/shard_map/ppermute | solution.py:853
  56.4 0.0 collective-permute-done.9.from_right
  56.4 0.6 shard_map.76
  57.0 1.9 %collective-permute-start.12 = (f32[1,256]{1,0:T(1,128)S(1)}, f32[1,256]{1,0:T(1,128)S(1)}, u32[]{:S(2)}, u32[]{:S(2)}) collective-permute-start(f32[1,256]{1,0:T(1,128)S(1)} %get-tuple-element.103), channel_id=1, source_target_pairs={{0,3},{1,0},{2,1},{3,2},{4,7},{5,4},{6,5},{7,6},{8,11},{9,8},{10,9... | collective-permute-start | bytes 3080 | tf_op jit(solution)/shard_map/ppermute | solution.py:932
  58.9 2.8 %collective-permute-start.11 = (f32[1,256]{1,0:T(1,128)S(1)}, f32[1,256]{1,0:T(1,128)S(1)}, u32[]{:S(2)}, u32[]{:S(2)}) collective-permute-start(f32[1,256]{1,0:T(1,128)S(1)} %get-tuple-element.103), channel_id=1, source_target_pairs={{0,2},{1,3},{2,0},{3,1},{4,6},{5,7},{6,4},{7,5},{8,10},{9,11},{10,... | collective-permute-start | bytes 3080 | tf_op jit(solution)/shard_map/ppermute | solution.py:932
  61.7 0.4 collective-permute-start.10
  62.1 1.3 %shard_map.77 = f32[19,2,32,128]{3,2,1,0:T(8,128)} custom-call(f32[19,2,64,128]{3,2,1,0:T(8,128)S(1)} %get-tuple-element.92.adjoint, f32[10,2,64,128]{3,2,1,0:T(8,128)S(1)} %get-tuple-element.93.turned, f32[2,32,128]{2,1,0:T(8,128)S(1)} %get-tuple-element.101.more, f32[280,128]{1,0:T(8,128)S(1)} %collective-permute-done.8.from_left, ...), custom_call_target="tpu_custom_call" | custom-call | bytes 3448832 | tf_op jit(solution)/shard_map/pallas_call | solution.py:833
  63.4 0.0 collective-permute-done.12
  63.4 0.0 collective-permute-done.11
  63.4 0.0 collective-permute-done.10
  63.4 0.6 add_add_fusion
Async XLA Ops:
  1.8 6.8 %collective-permute-start = (f32[22,2,8,128]{3,2,1,0:T(8,128)S(1)}, f32[22,2,8,128]{3,2,1,0:T(8,128)S(1)}, u32[]{:S(2)}, u32[]{:S(2)}) collective-permute-start(f32[22,2,8,128]{3,2,1,0:T(8,128)S(1)} %get-tuple-element.54), channel_id=1, source_target_pairs={{0,1},{1,2},{2,3},{3,0},{4,5},{5,6},{6,7},{7,4},{8,9},{9,10},{10,1... | collective-permute-start | bytes 540680 | tf_op jit(solution)/shard_map/ppermute | solution.py:853
  6.1 6.6 %collective-permute-start.1 = (f32[22,2,8,128]{3,2,1,0:T(8,128)S(1)}, f32[22,2,8,128]{3,2,1,0:T(8,128)S(1)}, u32[]{:S(2)}, u32[]{:S(2)}) collective-permute-start(f32[22,2,8,128]{3,2,1,0:T(8,128)S(1)} %get-tuple-element.55), channel_id=1, source_target_pairs={{1,0},{2,1},{3,2},{0,3},{5,4},{6,5},{7,6},{4,7},{9,8},{10,9},{11,1... | collective-permute-start | bytes 540680 | tf_op jit(solution)/shard_map/ppermute | solution.py:854
  6.2 1.1 %copy-start = (f32[19,2,32,128]{3,2,1,0:T(8,128)S(1)}, f32[19,2,32,128]{3,2,1,0:T(8,128)}, u32[]{:S(2)}) copy-start(f32[19,2,32,128]{3,2,1,0:T(8,128)} %pops.3) | copy-start | bytes 1867780
  13.0 12.3 %collective-permute-start.2 = (f32[456,128]{1,0:T(8,128)S(1)}, f32[456,128]{1,0:T(8,128)S(1)}, u32[]{:S(2)}, u32[]{:S(2)}) collective-permute-start(f32[456,128]{1,0:T(8,128)S(1)} %get-tuple-element.69), channel_id=1, source_target_pairs={{0,4},{4,8},{8,12},{12,16},{16,20},{20,24},{24,28},{28,32},{32,36}... | collective-permute-start | bytes 700424 | tf_op jit(solution)/shard_map/ppermute | solution.py:853
  14.1 11.2 %collective-permute-start.3 = (f32[456,128]{1,0:T(8,128)S(1)}, f32[456,128]{1,0:T(8,128)S(1)}, u32[]{:S(2)}, u32[]{:S(2)}) collective-permute-start(f32[456,128]{1,0:T(8,128)S(1)} %get-tuple-element.70), channel_id=1, source_target_pairs={{4,0},{8,4},{12,8},{16,12},{20,16},{24,20},{28,24},{32,28},{36,32}... | collective-permute-start | bytes 700424 | tf_op jit(solution)/shard_map/ppermute | solution.py:854
  26.4 10.9 %collective-permute-start.4 = (f32[376,128]{1,0:T(8,128)S(1)}, f32[376,128]{1,0:T(8,128)S(1)}, u32[]{:S(2)}, u32[]{:S(2)}) collective-permute-start(f32[376,128]{1,0:T(8,128)S(1)} %get-tuple-element.81), channel_id=1, source_target_pairs={{0,4},{4,8},{8,12},{12,16},{16,20},{20,24},{24,28},{28,32},{32,36}... | collective-permute-start | bytes 577544 | tf_op jit(solution)/shard_map/ppermute | solution.py:853
  26.5 10.8 %collective-permute-start.5 = (f32[376,128]{1,0:T(8,128)S(1)}, f32[376,128]{1,0:T(8,128)S(1)}, u32[]{:S(2)}, u32[]{:S(2)}) collective-permute-start(f32[376,128]{1,0:T(8,128)S(1)} %get-tuple-element.82), channel_id=1, source_target_pairs={{4,0},{8,4},{12,8},{16,12},{20,16},{24,20},{28,24},{32,28},{36,32}... | collective-permute-start | bytes 577544 | tf_op jit(solution)/shard_map/ppermute | solution.py:854
  38.1 8.4 %collective-permute-start.6 = (f32[3,40,128]{2,1,0:T(8,128)S(1)}, f32[3,40,128]{2,1,0:T(8,128)S(1)}, u32[]{:S(2)}, u32[]{:S(2)}) collective-permute-start(f32[3,40,128]{2,1,0:T(8,128)S(1)} %get-tuple-element.86), channel_id=1, source_target_pairs={{0,4},{4,8},{8,12},{12,16},{16,20},{20,24},{24,28},{28,32},{32,36}... | collective-permute-start | bytes 184328 | tf_op jit(solution)/shard_map/ppermute | solution.py:853
  38.2 8.3 %collective-permute-start.7 = (f32[3,40,128]{2,1,0:T(8,128)S(1)}, f32[3,40,128]{2,1,0:T(8,128)S(1)}, u32[]{:S(2)}, u32[]{:S(2)}) collective-permute-start(f32[3,40,128]{2,1,0:T(8,128)S(1)} %get-tuple-element.87), channel_id=1, source_target_pairs={{4,0},{8,4},{12,8},{16,12},{20,16},{24,20},{28,24},{32,28},{36,32}... | collective-permute-start | bytes 184328 | tf_op jit(solution)/shard_map/ppermute | solution.py:854
  47.7 8.7 %collective-permute-start.8 = (f32[280,128]{1,0:T(8,128)S(1)}, f32[280,128]{1,0:T(8,128)S(1)}, u32[]{:S(2)}, u32[]{:S(2)}) collective-permute-start(f32[280,128]{1,0:T(8,128)S(1)} %get-tuple-element.97), channel_id=1, source_target_pairs={{0,4},{4,8},{8,12},{12,16},{16,20},{20,24},{24,28},{28,32},{32,36}... | collective-permute-start | bytes 430088 | tf_op jit(solution)/shard_map/ppermute | solution.py:853
  47.8 8.6 %collective-permute-start.9 = (f32[280,128]{1,0:T(8,128)S(1)}, f32[280,128]{1,0:T(8,128)S(1)}, u32[]{:S(2)}, u32[]{:S(2)}) collective-permute-start(f32[280,128]{1,0:T(8,128)S(1)} %get-tuple-element.98), channel_id=1, source_target_pairs={{4,0},{8,4},{12,8},{16,12},{20,16},{24,20},{28,24},{32,28},{36,32}... | collective-permute-start | bytes 430088 | tf_op jit(solution)/shard_map/ppermute | solution.py:854
  57.0 6.4 %collective-permute-start.12 = (f32[1,256]{1,0:T(1,128)S(1)}, f32[1,256]{1,0:T(1,128)S(1)}, u32[]{:S(2)}, u32[]{:S(2)}) collective-permute-start(f32[1,256]{1,0:T(1,128)S(1)} %get-tuple-element.103), channel_id=1, source_target_pairs={{0,3},{1,0},{2,1},{3,2},{4,7},{5,4},{6,5},{7,6},{8,11},{9,8},{10,9... | collective-permute-start | bytes 3080 | tf_op jit(solution)/shard_map/ppermute | solution.py:932
  58.9 4.5 %collective-permute-start.11 = (f32[1,256]{1,0:T(1,128)S(1)}, f32[1,256]{1,0:T(1,128)S(1)}, u32[]{:S(2)}, u32[]{:S(2)}) collective-permute-start(f32[1,256]{1,0:T(1,128)S(1)} %get-tuple-element.103), channel_id=1, source_target_pairs={{0,2},{1,3},{2,0},{3,1},{4,6},{5,7},{6,4},{7,5},{8,10},{9,11},{10,... | collective-permute-start | bytes 3080 | tf_op jit(solution)/shard_map/ppermute | solution.py:932
  61.7 1.7 %collective-permute-start.10 = (f32[1,256]{1,0:T(1,128)S(1)}, f32[1,256]{1,0:T(1,128)S(1)}, u32[]{:S(2)}, u32[]{:S(2)}) collective-permute-start(f32[1,256]{1,0:T(1,128)S(1)} %get-tuple-element.103), channel_id=1, source_target_pairs={{0,1},{1,2},{2,3},{3,0},{4,5},{5,6},{6,7},{7,4},{8,9},{9,10},{10,1... | collective-permute-start | bytes 3080 | tf_op jit(solution)/shard_map/ppermute | solution.py:932

commit v8 on v7

--- a/solution.py
+++ b/solution.py
@@ -351,17 +351,20 @@
 
     copy(fluid, whole.at[0])
     copy(label, whole.at[1])
+    copy(table, values)
     copy(target, small.at[2])
-    copy(table, values)
-    copy(pops.at[:, :, pl.ds(0, HALO), :], low.at[pl.ds(0, 19)])
-    copy(pops.at[:, :, pl.ds(OWN - HALO, HALO), :], high.at[pl.ds(0, 19)])
-    for one in copies:
+    for rows, goal in ((pl.ds(0, HALO), low), (pl.ds(OWN - HALO, HALO), high)):
+        copy(target.at[:, rows, :], goal.at[21])
+        copy(pops.at[:, :, rows, :], goal.at[pl.ds(0, 19)])
+    for one in copies[:3]:
         one.wait()
     small[0] = whole[0].astype(jnp.float32)
     small[1] = whole[1].astype(jnp.float32)
     small[3, 0, 0:2, :] = values[...]
-    low[19:22] = small[0:3, :, 0:HALO, :]
-    high[19:22] = small[0:3, :, OWN - HALO : OWN, :]
+    low[19:21] = small[0:2, :, 0:HALO, :]
+    high[19:21] = small[0:2, :, OWN - HALO : OWN, :]
+    for one in copies[3:]:
+        one.wait()
 
 
 def put_sends(packed, send_left, send_right, t, lin, chosen):
@@ -615,23 +618,29 @@
     return lambda dy: mid_tall(t, dy)
 
 
+def put_ahead(ahead, p, rows, value):
+    ahead[0, p, rows(0), :] = value
+    ahead[1, p, rows(0), :] = rolled(value, 1)
+    ahead[2, p, rows(0), :] = rolled(value, -1)
+
+
+def third_flight_kernel(misfit, ahead):
+    def body(t):
+        for x in range(2):
+            put_ahead(ahead, 2 + x, middle(t), misfit[x, flat(t), :])
+
+    each_chunk(body, 0, MID // 8)
+
+
 def last_reverse_kernel(
-    misfit, from_left, from_right, masks, field, speed, pull, early_speed,
-    adjoint, turned, wall_out, send_left, send_right, part_left, part_right,
-    ahead, far_masks, pulled, pulled_doubled, base,
+    from_left, from_right, masks, field, speed, pull, early_speed, _,
+    ahead, adjoint, turned, wall_out, send_left, send_right, part_left, part_right,
+    far_masks, pulled, pulled_doubled, base,
 ):
     def place(t):
         rows = middle(t)
-        for p in range(6):
-            if p < 2:
-                d = from_left[1 - p, flat(t), :]
-            elif p < 4:
-                d = misfit[p - 2, flat(t), :]
-            else:
-                d = from_right[p - 4, flat(t), :]
-            ahead[0, p, rows(0), :] = d
-            ahead[1, p, rows(0), :] = rolled(d, 1)
-            ahead[2, p, rows(0), :] = rolled(d, -1)
+        for p in (0, 1, 4, 5):
+            put_ahead(ahead, p, rows, from_left[1 - p, flat(t), :] if p < 2 else from_right[p - 4, flat(t), :])
         for k, source in enumerate((from_left, from_right)):
             s = source[2, flat(t), :]
             far_masks[0, k, rows(0), :] = s
@@ -867,7 +876,7 @@
         (
             pltpu.VMEM((2, 2, OWN, DEPTH), jnp.int32),
             vmem(2, DEPTH),
-            pltpu.SemaphoreType.DMA((6,)),
+            pltpu.SemaphoreType.DMA((8,)),
         ),
         anywhere=5,
     )
@@ -912,11 +921,13 @@
     )
     from_left, from_right = both_ways(to_left, to_right, "gx")
     pulled = (vmem(3, 4, TALL, DEPTH), vmem(2, 4, TALL, DEPTH))
-    adjoint, turned, wall, to_left, to_right, part_left, part_right = call(
+    (ahead,) = call(third_flight_kernel, (misfit,), ((3, *wide6),), ())
+    _, adjoint, turned, wall, to_left, to_right, part_left, part_right = call(
         last_reverse_kernel,
-        (misfit, from_left, from_right, masks, field1, speed1, pull1, speed0),
-        ((19, 2, TALL, DEPTH), (10, 2, TALL, DEPTH), (2, *less), BACK[RIGHTWARD].shape, BACK[LEFTWARD].shape, (3, *less), (3, *less)),
-        (vmem(3, *wide6), vmem(3, 2, TALL, DEPTH), *pulled, vmem(19, 2, *less)),
+        (from_left, from_right, masks, field1, speed1, pull1, speed0, ahead),
+        ((3, *wide6), (19, 2, TALL, DEPTH), (10, 2, TALL, DEPTH), (2, *less), BACK[RIGHTWARD].shape, BACK[LEFTWARD].shape, (3, *less), (3, *less)),
+        (vmem(3, 2, TALL, DEPTH), *pulled, vmem(19, 2, *less)),
+        filled=1,
     )
     from_left, from_right = both_ways(to_left, to_right, "gx")
     come = vmem(2, 5, TALL, DEPTH)

time: 64.7 us -> 64.6 us (level)
    pallas_call x10 -> x11, Pallas kernels: 7.25 us -> 7.2 us  [call(): pl.pallas_call(kernel, out_shape=[s if hasattr(s, 'dtype') else jax.Shape...]
where the time goes in v8:
time: 64.6 us; the launch traced here: 63.8 us
  starting transfers between devices  35.7 us (55%)
  waiting for transfers between devices  18.5 us (29%)
  Pallas kernels  7.2 us (11%)
  local copies, waits for them, and re-layouts  1.08 us (2%)
  between operations  0.74 us (1%)
    ppermute x5, starting transfers between devices, both_ways(): from_upper = lax.ppermute(to_lower, axis, down)  24.9 us
    ppermute x5, waiting for transfers between devices, both_ways(): from_lower = lax.ppermute(to_upper, axis, up)  14.3 us
    pallas_call x11, Pallas kernels, call(): pl.pallas_call(kernel, out_shape=[s if hasattr(s, 'dtype') else jax.Shape...  7.2 us
    ppermute x5, starting transfers between devices, both_ways(): from_lower = lax.ppermute(to_upper, axis, up)  5.74 us
    ppermute x3, starting transfers between devices, per_device(): lax.ppermute(label_part, 'gy', [(i, (i + step) % count) for i in range(co...  5.13 us
    ppermute x5, waiting for transfers between devices, both_ways(): from_upper = lax.ppermute(to_lower, axis, down)  4.17 us
  transfers between devices with their start and end apart: 13, of which 6 were waited for; matrix products, arithmetic and copies ran while one was open for 0% of the time, Pallas kernels for 3%

profile of v8, /device:TPU:1, one launch (start us, length us, event | category | flops | bytes accessed | tf_op | source)
XLA Modules:
  0.0 63.8 jit_solution(6390470348389476806)
XLA Ops:
  0.6 1.2 %shard_map.68 = (f32[22,2,8,128]{3,2,1,0:T(8,128)S(1)}, f32[22,2,8,128]{3,2,1,0:T(8,128)S(1)}, f32[4,2,32,128]{3,2,1,0:T(8,128)S(1)}) custom-call(f32[19,2,32,128]{3,2,1,0:T(8,128)} %pops.3, s32[2,32,128]{2,1,0:T(8,128)} %fluid.1, s32[2,32,128]{2,1,0:T(8,128)} %label.1, f32[2,32,128]{2,1,0:T(8,128)} %target.1, f32[2,128]{1,0:T(2,128)} %bitcast.2), custom_call_target="tpu_custom_call" | custom-call | bytes 721920 | tf_op jit(solution)/shard_map/pallas_call | solution.py:842
  1.8 4.4 %collective-permute-start = (f32[22,2,8,128]{3,2,1,0:T(8,128)S(1)}, f32[22,2,8,128]{3,2,1,0:T(8,128)S(1)}, u32[]{:S(2)}, u32[]{:S(2)}) collective-permute-start(f32[22,2,8,128]{3,2,1,0:T(8,128)S(1)} %get-tuple-element.54), channel_id=1, source_target_pairs={{0,1},{1,2},{2,3},{3,0},{4,5},{5,6},{6,7},{7,4},{8,9},{9,10},{10,1... | collective-permute-start | bytes 540680 | tf_op jit(solution)/shard_map/ppermute | solution.py:862
  6.2 0.0 collective-permute-start.1
  6.2 0.0 copy-start
  6.2 1.1 %copy-done = f32[19,2,32,128]{3,2,1,0:T(8,128)S(1)} copy-done((f32[19,2,32,128]{3,2,1,0:T(8,128)S(1)}, f32[19,2,32,128]{3,2,1,0:T(8,128)}, u32[]{:S(2)}) %copy-start) | copy-done | bytes 622616
  7.3 0.4 shard_map.69
  7.7 1.0 %collective-permute-done.below = f32[22,2,8,128]{3,2,1,0:T(8,128)S(1)} collective-permute-done((f32[22,2,8,128]{3,2,1,0:T(8,128)S(1)}, f32[22,2,8,128]{3,2,1,0:T(8,128)S(1)}, u32[]{:S(2)}, u32[]{:S(2)}) %collective-permute-start) | collective-permute-done | bytes 180256 | tf_op jit(solution)/shard_map/ppermute | solution.py:862
  8.6 4.2 %collective-permute-done.1.above = f32[22,2,8,128]{3,2,1,0:T(8,128)S(1)} collective-permute-done((f32[22,2,8,128]{3,2,1,0:T(8,128)S(1)}, f32[22,2,8,128]{3,2,1,0:T(8,128)S(1)}, u32[]{:S(2)}, u32[]{:S(2)}) %collective-permute-start.1) | collective-permute-done | bytes 180256 | tf_op jit(solution)/shard_map/ppermute | solution.py:863
  12.8 0.2 shard_map.70
  13.0 1.1 %collective-permute-start.2 = (f32[456,128]{1,0:T(8,128)S(1)}, f32[456,128]{1,0:T(8,128)S(1)}, u32[]{:S(2)}, u32[]{:S(2)}) collective-permute-start(f32[456,128]{1,0:T(8,128)S(1)} %get-tuple-element.69), channel_id=1, source_target_pairs={{0,4},{4,8},{8,12},{12,16},{16,20},{20,24},{24,28},{28,32},{32,36}... | collective-permute-start | bytes 700424 | tf_op jit(solution)/shard_map/ppermute | solution.py:862
  14.1 6.8 %collective-permute-start.3 = (f32[456,128]{1,0:T(8,128)S(1)}, f32[456,128]{1,0:T(8,128)S(1)}, u32[]{:S(2)}, u32[]{:S(2)}) collective-permute-start(f32[456,128]{1,0:T(8,128)S(1)} %get-tuple-element.70), channel_id=1, source_target_pairs={{4,0},{8,4},{12,8},{16,12},{20,16},{24,20},{28,24},{32,28},{36,32}... | collective-permute-start | bytes 700424 | tf_op jit(solution)/shard_map/ppermute | solution.py:863
  20.9 0.1 shard_map.71
  21.0 4.3 %collective-permute-done.2.refs_5_ = f32[456,128]{1,0:T(8,128)S(1)} collective-permute-done((f32[456,128]{1,0:T(8,128)S(1)}, f32[456,128]{1,0:T(8,128)S(1)}, u32[]{:S(2)}, u32[]{:S(2)}) %collective-permute-start.2) | collective-permute-done | bytes 233504 | tf_op jit(solution)/shard_map/ppermute | solution.py:862
  25.3 0.0 collective-permute-done.3.refs_6_
  25.3 1.1 %shard_map.72 = (f32[3,6,64,128]{3,2,1,0:T(8,128)S(1)}, f32[6,64,128]{2,1,0:T(8,128)S(1)}, f32[6,64,128]{2,1,0:T(8,128)S(1)}, f32[3,4,48,128]{3,2,1,0:T(8,128)S(...) custom-call(f32[19,2,48,128]{3,2,1,0:T(8,128)S(1)} %get-tuple-elemen, ...), custom_call_target="tpu_custom_call", output_to_operand_aliasing={{0}: (7, {}), {1}: (8, {}), {2}: (9, {})} | custom-call | bytes 2678784 | tf_op jit(solution)/shard_map/pallas_call | solution.py:842
  26.4 0.1 collective-permute-start.4
  26.5 6.1 %collective-permute-start.5 = (f32[376,128]{1,0:T(8,128)S(1)}, f32[376,128]{1,0:T(8,128)S(1)}, u32[]{:S(2)}, u32[]{:S(2)}) collective-permute-start(f32[376,128]{1,0:T(8,128)S(1)} %get-tuple-element.82), channel_id=1, source_target_pairs={{4,0},{8,4},{12,8},{16,12},{20,16},{24,20},{28,24},{32,28},{36,32}... | collective-permute-start | bytes 577544 | tf_op jit(solution)/shard_map/ppermute | solution.py:863
  32.6 0.3 shard_map.73
  32.9 4.3 %collective-permute-done.4.refs_6_ = f32[376,128]{1,0:T(8,128)S(1)} collective-permute-done((f32[376,128]{1,0:T(8,128)S(1)}, f32[376,128]{1,0:T(8,128)S(1)}, u32[]{:S(2)}, u32[]{:S(2)}) %collective-permute-start.4) | collective-permute-done | bytes 192544 | tf_op jit(solution)/shard_map/ppermute | solution.py:862
  37.3 0.0 collective-permute-done.5.refs_7_
  37.3 0.9 %shard_map.74 = (f32[6,64,128]{2,1,0:T(8,128)S(1)}, f32[6,64,128]{2,1,0:T(8,128)S(1)}, f32[3,4,48,128]{3,2,1,0:T(8,128)S(1)}, f32[3,2,48,128]{3,2,1,0:T(8,128)S(...) custom-call(f32[19,2,48,128]{3,2,1,0:T(8,128)S(1)} %get-tuple-elemen, ...), custom_call_target="tpu_custom_call", output_to_operand_aliasing={{0}: (8, {}), {1}: (9, {})} | custom-call | bytes 2596864 | tf_op jit(solution)/shard_map/pallas_call | solution.py:842
  38.2 0.1 collective-permute-start.6
  38.2 6.3 %collective-permute-start.7 = (f32[3,40,128]{2,1,0:T(8,128)S(1)}, f32[3,40,128]{2,1,0:T(8,128)S(1)}, u32[]{:S(2)}, u32[]{:S(2)}) collective-permute-start(f32[3,40,128]{2,1,0:T(8,128)S(1)} %get-tuple-element.86), channel_id=1, source_target_pairs={{4,0},{8,4},{12,8},{16,12},{20,16},{24,20},{28,24},{32,28},{36,32}... | collective-permute-start | bytes 184328 | tf_op jit(solution)/shard_map/ppermute | solution.py:863
  44.6 0.1 shard_map.75._
  44.6 1.9 %collective-permute-done.6.from_left = f32[3,40,128]{2,1,0:T(8,128)S(1)} collective-permute-done((f32[3,40,128]{2,1,0:T(8,128)S(1)}, f32[3,40,128]{2,1,0:T(8,128)S(1)}, u32[]{:S(2)}, u32[]{:S(2)}) %collective-permute-start.6) | collective-permute-done | bytes 61472 | tf_op jit(solution)/shard_map/ppermute | solution.py:862
  46.5 0.0 collective-permute-done.7.from_right
  46.5 1.1 %shard_map.76 = (f32[3,6,64,128]{3,2,1,0:T(8,128)S(1)}, f32[19,2,64,128]{3,2,1,0:T(8,128)S(1)}, f32[10,2,64,128]{3,2,1,0:T(8,128)S(1)}, f32[2,40,128]{2,1,0:T(8,...) custom-call(f32[3,40,128]{2,1,0:T(8,128)S(1)} %collective-permute-do, ...), custom_call_target="tpu_custom_call", output_to_operand_aliasing={{0}: (7, {})} | custom-call | bytes 2236416 | tf_op jit(solution)/shard_map/pallas_call | solution.py:842
  47.6 0.1 collective-permute-start.8
  47.7 5.7 %collective-permute-start.9 = (f32[280,128]{1,0:T(8,128)S(1)}, f32[280,128]{1,0:T(8,128)S(1)}, u32[]{:S(2)}, u32[]{:S(2)}) collective-permute-start(f32[280,128]{1,0:T(8,128)S(1)} %get-tuple-element.98), channel_id=1, source_target_pairs={{4,0},{8,4},{12,8},{16,12},{20,16},{24,20},{28,24},{32,28},{36,32}... | collective-permute-start | bytes 430088 | tf_op jit(solution)/shard_map/ppermute | solution.py:863
  53.4 2.9 %collective-permute-done.8.from_left = f32[280,128]{1,0:T(8,128)S(1)} collective-permute-done((f32[280,128]{1,0:T(8,128)S(1)}, f32[280,128]{1,0:T(8,128)S(1)}, u32[]{:S(2)}, u32[]{:S(2)}) %collective-permute-start.8) | collective-permute-done | bytes 143392 | tf_op jit(solution)/shard_map/ppermute | solution.py:862
  56.2 0.0 collective-permute-done.9.from_right
  56.2 0.6 shard_map.77
  56.9 1.9 %collective-permute-start.12 = (f32[1,256]{1,0:T(1,128)S(1)}, f32[1,256]{1,0:T(1,128)S(1)}, u32[]{:S(2)}, u32[]{:S(2)}) collective-permute-start(f32[1,256]{1,0:T(1,128)S(1)} %get-tuple-element.103), channel_id=1, source_target_pairs={{0,3},{1,0},{2,1},{3,2},{4,7},{5,4},{6,5},{7,6},{8,11},{9,8},{10,9... | collective-permute-start | bytes 3080 | tf_op jit(solution)/shard_map/ppermute | solution.py:943
  58.8 2.8 %collective-permute-start.11 = (f32[1,256]{1,0:T(1,128)S(1)}, f32[1,256]{1,0:T(1,128)S(1)}, u32[]{:S(2)}, u32[]{:S(2)}) collective-permute-start(f32[1,256]{1,0:T(1,128)S(1)} %get-tuple-element.103), channel_id=1, source_target_pairs={{0,2},{1,3},{2,0},{3,1},{4,6},{5,7},{6,4},{7,5},{8,10},{9,11},{10,... | collective-permute-start | bytes 3080 | tf_op jit(solution)/shard_map/ppermute | solution.py:943
  61.6 0.4 collective-permute-start.10
  62.0 1.3 %shard_map.78 = f32[19,2,32,128]{3,2,1,0:T(8,128)} custom-call(f32[19,2,64,128]{3,2,1,0:T(8,128)S(1)} %get-tuple-element.92.adjoint, f32[10,2,64,128]{3,2,1,0:T(8,128)S(1)} %get-tuple-element.93.turned, f32[2,32,128]{2,1,0:T(8,128)S(1)} %get-tuple-element.101.more, f32[280,128]{1,0:T(8,128)S(1)} %collective-permute-done.8.from_left, ...), custom_call_target="tpu_custom_call" | custom-call | bytes 3448832 | tf_op jit(solution)/shard_map/pallas_call | solution.py:842
  63.3 0.0 collective-permute-done.12
  63.3 0.0 collective-permute-done.11
  63.3 0.0 collective-permute-done.10
  63.3 0.6 add_add_fusion
Async XLA Ops:
  1.8 6.8 %collective-permute-start = (f32[22,2,8,128]{3,2,1,0:T(8,128)S(1)}, f32[22,2,8,128]{3,2,1,0:T(8,128)S(1)}, u32[]{:S(2)}, u32[]{:S(2)}) collective-permute-start(f32[22,2,8,128]{3,2,1,0:T(8,128)S(1)} %get-tuple-element.54), channel_id=1, source_target_pairs={{0,1},{1,2},{2,3},{3,0},{4,5},{5,6},{6,7},{7,4},{8,9},{9,10},{10,1... | collective-permute-start | bytes 540680 | tf_op jit(solution)/shard_map/ppermute | solution.py:862
  6.2 6.6 %collective-permute-start.1 = (f32[22,2,8,128]{3,2,1,0:T(8,128)S(1)}, f32[22,2,8,128]{3,2,1,0:T(8,128)S(1)}, u32[]{:S(2)}, u32[]{:S(2)}) collective-permute-start(f32[22,2,8,128]{3,2,1,0:T(8,128)S(1)} %get-tuple-element.55), channel_id=1, source_target_pairs={{1,0},{2,1},{3,2},{0,3},{5,4},{6,5},{7,6},{4,7},{9,8},{10,9},{11,1... | collective-permute-start | bytes 540680 | tf_op jit(solution)/shard_map/ppermute | solution.py:863
  6.2 1.1 %copy-start = (f32[19,2,32,128]{3,2,1,0:T(8,128)S(1)}, f32[19,2,32,128]{3,2,1,0:T(8,128)}, u32[]{:S(2)}) copy-start(f32[19,2,32,128]{3,2,1,0:T(8,128)} %pops.3) | copy-start | bytes 1867780
  13.0 12.3 %collective-permute-start.2 = (f32[456,128]{1,0:T(8,128)S(1)}, f32[456,128]{1,0:T(8,128)S(1)}, u32[]{:S(2)}, u32[]{:S(2)}) collective-permute-start(f32[456,128]{1,0:T(8,128)S(1)} %get-tuple-element.69), channel_id=1, source_target_pairs={{0,4},{4,8},{8,12},{12,16},{16,20},{20,24},{24,28},{28,32},{32,36}... | collective-permute-start | bytes 700424 | tf_op jit(solution)/shard_map/ppermute | solution.py:862
  14.1 11.2 %collective-permute-start.3 = (f32[456,128]{1,0:T(8,128)S(1)}, f32[456,128]{1,0:T(8,128)S(1)}, u32[]{:S(2)}, u32[]{:S(2)}) collective-permute-start(f32[456,128]{1,0:T(8,128)S(1)} %get-tuple-element.70), channel_id=1, source_target_pairs={{4,0},{8,4},{12,8},{16,12},{20,16},{24,20},{28,24},{32,28},{36,32}... | collective-permute-start | bytes 700424 | tf_op jit(solution)/shard_map/ppermute | solution.py:863
  26.4 10.9 %collective-permute-start.4 = (f32[376,128]{1,0:T(8,128)S(1)}, f32[376,128]{1,0:T(8,128)S(1)}, u32[]{:S(2)}, u32[]{:S(2)}) collective-permute-start(f32[376,128]{1,0:T(8,128)S(1)} %get-tuple-element.81), channel_id=1, source_target_pairs={{0,4},{4,8},{8,12},{12,16},{16,20},{20,24},{24,28},{28,32},{32,36}... | collective-permute-start | bytes 577544 | tf_op jit(solution)/shard_map/ppermute | solution.py:862
  26.5 10.8 %collective-permute-start.5 = (f32[376,128]{1,0:T(8,128)S(1)}, f32[376,128]{1,0:T(8,128)S(1)}, u32[]{:S(2)}, u32[]{:S(2)}) collective-permute-start(f32[376,128]{1,0:T(8,128)S(1)} %get-tuple-element.82), channel_id=1, source_target_pairs={{4,0},{8,4},{12,8},{16,12},{20,16},{24,20},{28,24},{32,28},{36,32}... | collective-permute-start | bytes 577544 | tf_op jit(solution)/shard_map/ppermute | solution.py:863
  38.2 8.4 %collective-permute-start.6 = (f32[3,40,128]{2,1,0:T(8,128)S(1)}, f32[3,40,128]{2,1,0:T(8,128)S(1)}, u32[]{:S(2)}, u32[]{:S(2)}) collective-permute-start(f32[3,40,128]{2,1,0:T(8,128)S(1)} %get-tuple-element.85), channel_id=1, source_target_pairs={{0,4},{4,8},{8,12},{12,16},{16,20},{20,24},{24,28},{28,32},{32,36}... | collective-permute-start | bytes 184328 | tf_op jit(solution)/shard_map/ppermute | solution.py:862
  38.2 8.3 %collective-permute-start.7 = (f32[3,40,128]{2,1,0:T(8,128)S(1)}, f32[3,40,128]{2,1,0:T(8,128)S(1)}, u32[]{:S(2)}, u32[]{:S(2)}) collective-permute-start(f32[3,40,128]{2,1,0:T(8,128)S(1)} %get-tuple-element.86), channel_id=1, source_target_pairs={{4,0},{8,4},{12,8},{16,12},{20,16},{24,20},{28,24},{32,28},{36,32}... | collective-permute-start | bytes 184328 | tf_op jit(solution)/shard_map/ppermute | solution.py:863
  47.6 8.7 %collective-permute-start.8 = (f32[280,128]{1,0:T(8,128)S(1)}, f32[280,128]{1,0:T(8,128)S(1)}, u32[]{:S(2)}, u32[]{:S(2)}) collective-permute-start(f32[280,128]{1,0:T(8,128)S(1)} %get-tuple-element.97), channel_id=1, source_target_pairs={{0,4},{4,8},{8,12},{12,16},{16,20},{20,24},{24,28},{28,32},{32,36}... | collective-permute-start | bytes 430088 | tf_op jit(solution)/shard_map/ppermute | solution.py:862
  47.7 8.6 %collective-permute-start.9 = (f32[280,128]{1,0:T(8,128)S(1)}, f32[280,128]{1,0:T(8,128)S(1)}, u32[]{:S(2)}, u32[]{:S(2)}) collective-permute-start(f32[280,128]{1,0:T(8,128)S(1)} %get-tuple-element.98), channel_id=1, source_target_pairs={{4,0},{8,4},{12,8},{16,12},{20,16},{24,20},{28,24},{32,28},{36,32}... | collective-permute-start | bytes 430088 | tf_op jit(solution)/shard_map/ppermute | solution.py:863
  56.9 6.4 %collective-permute-start.12 = (f32[1,256]{1,0:T(1,128)S(1)}, f32[1,256]{1,0:T(1,128)S(1)}, u32[]{:S(2)}, u32[]{:S(2)}) collective-permute-start(f32[1,256]{1,0:T(1,128)S(1)} %get-tuple-element.103), channel_id=1, source_target_pairs={{0,3},{1,0},{2,1},{3,2},{4,7},{5,4},{6,5},{7,6},{8,11},{9,8},{10,9... | collective-permute-start | bytes 3080 | tf_op jit(solution)/shard_map/ppermute | solution.py:943
  58.8 4.5 %collective-permute-start.11 = (f32[1,256]{1,0:T(1,128)S(1)}, f32[1,256]{1,0:T(1,128)S(1)}, u32[]{:S(2)}, u32[]{:S(2)}) collective-permute-start(f32[1,256]{1,0:T(1,128)S(1)} %get-tuple-element.103), channel_id=1, source_target_pairs={{0,2},{1,3},{2,0},{3,1},{4,6},{5,7},{6,4},{7,5},{8,10},{9,11},{10,... | collective-permute-start | bytes 3080 | tf_op jit(solution)/shard_map/ppermute | solution.py:943
  61.6 1.7 %collective-permute-start.10 = (f32[1,256]{1,0:T(1,128)S(1)}, f32[1,256]{1,0:T(1,128)S(1)}, u32[]{:S(2)}, u32[]{:S(2)}) collective-permute-start(f32[1,256]{1,0:T(1,128)S(1)} %get-tuple-element.103), channel_id=1, source_target_pairs={{0,1},{1,2},{2,3},{3,0},{4,5},{5,6},{6,7},{7,4},{8,9},{9,10},{10,1... | collective-permute-start | bytes 3080 | tf_op jit(solution)/shard_map/ppermute | solution.py:943

commit v9 on v8

--- a/solution.py
+++ b/solution.py
@@ -375,7 +375,7 @@
 
 
 def start_rows(t, populations, shares, marks, table, outs):
-    lin_out, flow_out, density_out, effective_out, share_out, _, send_left, send_right = outs
+    lin_out, flow_out, density_out, effective_out, share_out, _, send_left, send_right = outs[:8]
     half_low = jnp.broadcast_to(table[0:1, :], (8, DEPTH))
     half_high = jnp.broadcast_to(table[1:2, :], (8, DEPTH))
     lin, chosen = [], []
@@ -402,8 +402,19 @@
     START[RIGHTWARD].put(send_right, 9, t, shares[1])
 
 
+def place_own(outs, t):
+    for x in range(2):
+        value = outs[3][x, flat(t), :]
+        outs[8][x, tall(t), :] = value
+        outs[9][x, tall(t), :] = with_sides(value)
+
+
+def send_own(outs, t):
+    send_flow(START, outs[6], outs[7], outs[1], outs[8], outs[9], t)
+
+
 def own_kernel(pops, small, *refs):
-    outs, chooser, turned_label = refs[:8], refs[8], refs[9]
+    outs, chooser, turned_label = refs[:10], refs[10], refs[11]
     outs[5][:, HALO : HALO + OWN, :] = small[2]
 
     def body(t):
@@ -419,6 +430,9 @@
 
     each_chunk(body, HALO // 8, (HALO + OWN) // 8)
 
+    each_chunk(functools.partial(place_own, outs), HALO // 8, (HALO + OWN) // 8)
+    each_chunk(functools.partial(send_own, outs), HALO // 8 + 1, (HALO + OWN) // 8 - 1)
+
     marks = jnp.bitwise_and(small[1, 0].astype(jnp.int32), LABELS - 1).astype(jnp.float32)
     turned_label[...] = jnp.transpose(marks)
     quads = DEPTH // 4
@@ -430,7 +444,7 @@
 
 
 def halo_kernel(small, below, above, *refs):
-    outs, field, doubled = refs[8:16], refs[16], refs[17]
+    outs = refs[10:]
     for t, edge in ((0, below), (CHUNKS - 1, above)):
         outs[5][:, 8 * t : 8 * t + 8, :] = edge[21]
         start_rows(
@@ -441,16 +455,9 @@
             small[3, 0, 0:2, :],
             outs,
         )
-    flow, effective, send_left, send_right = outs[1], outs[3], outs[6], outs[7]
-
-    def place(t):
-        for x in range(2):
-            value = effective[x, flat(t), :]
-            field[x, tall(t), :] = value
-            doubled[x, tall(t), :] = with_sides(value)
-
-    each_chunk(place)
-    each_chunk(functools.partial(send_flow, START, send_left, send_right, flow, field, doubled))
+        place_own(outs, t)
+    for t in (0, 1, CHUNKS - 2, CHUNKS - 1):
+        send_own(outs, t)
 
 
 def put_field(field, doubled, p, t, value):
@@ -883,6 +890,7 @@
     below, above = both_ways(low, high, "gy")
     blocks = (OWN // 2) * (DEPTH // 4)
     started = ((19, *two), (3, *two), two, two, two, two, START[LEFTWARD].shape, START[RIGHTWARD].shape)
+    started += ((2, TALL, DEPTH),) * 2
     *own, chooser = call(
         own_kernel,
         (populations, small),
@@ -890,8 +898,8 @@
         (vmem(DEPTH, OWN),),
     )
     beside = (vmem(2, TALL, DEPTH), vmem(2, TALL, DEPTH))
-    lin, flow, density, effective, share, target_wide, to_left, to_right = call(
-        halo_kernel, (small, below, above, *own), started, beside, filled=len(started)
+    lin, flow, density, effective, share, target_wide, to_left, to_right, _, _ = call(
+        halo_kernel, (small, below, above, *own), started, (), filled=len(started)
     )
     from_left, from_right = both_ways(to_left, to_right, "gx")
     wide6 = (6, TALL, DEPTH)

time: 64.6 us -> 64.6 us (level)
  no operation moved by 1% of the time
where the time goes in v9:
time: 64.6 us; the launch traced here: 63.8 us
  starting transfers between devices  35.7 us (55%)
  waiting for transfers between devices  18.4 us (28%)
  Pallas kernels  7.28 us (11%)
  local copies, waits for them, and re-layouts  1.08 us (2%)
  between operations  0.74 us (1%)
    ppermute x5, starting transfers between devices, both_ways(): from_upper = lax.ppermute(to_lower, axis, down)  24.9 us
    ppermute x5, waiting for transfers between devices, both_ways(): from_lower = lax.ppermute(to_upper, axis, up)  14.3 us
    pallas_call x11, Pallas kernels, call(): pl.pallas_call(kernel, out_shape=[s if hasattr(s, 'dtype') else jax.Shape...  7.28 us
    ppermute x5, starting transfers between devices, both_ways(): from_lower = lax.ppermute(to_upper, axis, up)  5.74 us
    ppermute x3, starting transfers between devices, per_device(): lax.ppermute(label_part, 'gy', [(i, (i + step) % count) for i in range(co...  5.13 us
    ppermute x5, waiting for transfers between devices, both_ways(): from_upper = lax.ppermute(to_lower, axis, down)  4.17 us
  transfers between devices with their start and end apart: 13, of which 6 were waited for; matrix products, arithmetic and copies ran while one was open for 0% of the time, Pallas kernels for 3%

profile of v9, /device:TPU:1, one launch (start us, length us, event | category | flops | bytes accessed | tf_op | source)
XLA Modules:
  0.0 63.8 jit_solution(17443734468547540811)
XLA Ops:
  0.6 1.2 %shard_map.68 = (f32[22,2,8,128]{3,2,1,0:T(8,128)S(1)}, f32[22,2,8,128]{3,2,1,0:T(8,128)S(1)}, f32[4,2,32,128]{3,2,1,0:T(8,128)S(1)}) custom-call(f32[19,2,32,128]{3,2,1,0:T(8,128)} %pops.3, s32[2,32,128]{2,1,0:T(8,128)} %fluid.1, s32[2,32,128]{2,1,0:T(8,128)} %label.1, f32[2,32,128]{2,1,0:T(8,128)} %target.1, f32[2,128]{1,0:T(2,128)} %bitcast.2), custom_call_target="tpu_custom_call" | custom-call | bytes 721920 | tf_op jit(solution)/shard_map/pallas_call | solution.py:849
  1.8 4.4 %collective-permute-start = (f32[22,2,8,128]{3,2,1,0:T(8,128)S(1)}, f32[22,2,8,128]{3,2,1,0:T(8,128)S(1)}, u32[]{:S(2)}, u32[]{:S(2)}) collective-permute-start(f32[22,2,8,128]{3,2,1,0:T(8,128)S(1)} %get-tuple-element.56), channel_id=1, source_target_pairs={{0,1},{1,2},{2,3},{3,0},{4,5},{5,6},{6,7},{7,4},{8,9},{9,10},{10,1... | collective-permute-start | bytes 540680 | tf_op jit(solution)/shard_map/ppermute | solution.py:869
  6.2 0.0 collective-permute-start.1
  6.2 0.0 copy-start
  6.2 1.1 %copy-done = f32[19,2,32,128]{3,2,1,0:T(8,128)S(1)} copy-done((f32[19,2,32,128]{3,2,1,0:T(8,128)S(1)}, f32[19,2,32,128]{3,2,1,0:T(8,128)}, u32[]{:S(2)}) %copy-start) | copy-done | bytes 622616
  7.3 0.5 shard_map.69
  7.7 0.9 %collective-permute-done.below = f32[22,2,8,128]{3,2,1,0:T(8,128)S(1)} collective-permute-done((f32[22,2,8,128]{3,2,1,0:T(8,128)S(1)}, f32[22,2,8,128]{3,2,1,0:T(8,128)S(1)}, u32[]{:S(2)}, u32[]{:S(2)}) %collective-permute-start) | collective-permute-done | bytes 180256 | tf_op jit(solution)/shard_map/ppermute | solution.py:869
  8.6 4.2 %collective-permute-done.1.above = f32[22,2,8,128]{3,2,1,0:T(8,128)S(1)} collective-permute-done((f32[22,2,8,128]{3,2,1,0:T(8,128)S(1)}, f32[22,2,8,128]{3,2,1,0:T(8,128)S(1)}, u32[]{:S(2)}, u32[]{:S(2)}) %collective-permute-start.1) | collective-permute-done | bytes 180256 | tf_op jit(solution)/shard_map/ppermute | solution.py:870
  12.8 0.2 shard_map.70
  13.0 1.1 %collective-permute-start.2 = (f32[456,128]{1,0:T(8,128)S(1)}, f32[456,128]{1,0:T(8,128)S(1)}, u32[]{:S(2)}, u32[]{:S(2)}) collective-permute-start(f32[456,128]{1,0:T(8,128)S(1)} %get-tuple-element.73), channel_id=1, source_target_pairs={{0,4},{4,8},{8,12},{12,16},{16,20},{20,24},{24,28},{28,32},{32,36}... | collective-permute-start | bytes 700424 | tf_op jit(solution)/shard_map/ppermute | solution.py:869
  14.1 6.8 %collective-permute-start.3 = (f32[456,128]{1,0:T(8,128)S(1)}, f32[456,128]{1,0:T(8,128)S(1)}, u32[]{:S(2)}, u32[]{:S(2)}) collective-permute-start(f32[456,128]{1,0:T(8,128)S(1)} %get-tuple-element.74), channel_id=1, source_target_pairs={{4,0},{8,4},{12,8},{16,12},{20,16},{24,20},{28,24},{32,28},{36,32}... | collective-permute-start | bytes 700424 | tf_op jit(solution)/shard_map/ppermute | solution.py:870
  20.9 0.1 shard_map.71
  21.0 4.3 %collective-permute-done.2.refs_5_ = f32[456,128]{1,0:T(8,128)S(1)} collective-permute-done((f32[456,128]{1,0:T(8,128)S(1)}, f32[456,128]{1,0:T(8,128)S(1)}, u32[]{:S(2)}, u32[]{:S(2)}) %collective-permute-start.2) | collective-permute-done | bytes 233504 | tf_op jit(solution)/shard_map/ppermute | solution.py:869
  25.3 0.0 collective-permute-done.3.refs_6_
  25.3 1.1 %shard_map.72 = (f32[3,6,64,128]{3,2,1,0:T(8,128)S(1)}, f32[6,64,128]{2,1,0:T(8,128)S(1)}, f32[6,64,128]{2,1,0:T(8,128)S(1)}, f32[3,4,48,128]{3,2,1,0:T(8,128)S(...) custom-call(f32[19,2,48,128]{3,2,1,0:T(8,128)S(1)} %get-tuple-elemen, ...), custom_call_target="tpu_custom_call", output_to_operand_aliasing={{0}: (7, {}), {1}: (8, {}), {2}: (9, {})} | custom-call | bytes 2678784 | tf_op jit(solution)/shard_map/pallas_call | solution.py:849
  26.4 0.1 collective-permute-start.4
  26.5 6.1 %collective-permute-start.5 = (f32[376,128]{1,0:T(8,128)S(1)}, f32[376,128]{1,0:T(8,128)S(1)}, u32[]{:S(2)}, u32[]{:S(2)}) collective-permute-start(f32[376,128]{1,0:T(8,128)S(1)} %get-tuple-element.86), channel_id=1, source_target_pairs={{4,0},{8,4},{12,8},{16,12},{20,16},{24,20},{28,24},{32,28},{36,32}... | collective-permute-start | bytes 577544 | tf_op jit(solution)/shard_map/ppermute | solution.py:870
  32.6 0.3 shard_map.73
  32.9 4.3 %collective-permute-done.4.refs_6_ = f32[376,128]{1,0:T(8,128)S(1)} collective-permute-done((f32[376,128]{1,0:T(8,128)S(1)}, f32[376,128]{1,0:T(8,128)S(1)}, u32[]{:S(2)}, u32[]{:S(2)}) %collective-permute-start.4) | collective-permute-done | bytes 192544 | tf_op jit(solution)/shard_map/ppermute | solution.py:869
  37.3 0.0 collective-permute-done.5.refs_7_
  37.3 0.9 %shard_map.74 = (f32[6,64,128]{2,1,0:T(8,128)S(1)}, f32[6,64,128]{2,1,0:T(8,128)S(1)}, f32[3,4,48,128]{3,2,1,0:T(8,128)S(1)}, f32[3,2,48,128]{3,2,1,0:T(8,128)S(...) custom-call(f32[19,2,48,128]{3,2,1,0:T(8,128)S(1)} %get-tuple-elemen, ...), custom_call_target="tpu_custom_call", output_to_operand_aliasing={{0}: (8, {}), {1}: (9, {})} | custom-call | bytes 2596864 | tf_op jit(solution)/shard_map/pallas_call | solution.py:849
  38.1 0.1 collective-permute-start.6
  38.2 6.3 %collective-permute-start.7 = (f32[3,40,128]{2,1,0:T(8,128)S(1)}, f32[3,40,128]{2,1,0:T(8,128)S(1)}, u32[]{:S(2)}, u32[]{:S(2)}) collective-permute-start(f32[3,40,128]{2,1,0:T(8,128)S(1)} %get-tuple-element.90), channel_id=1, source_target_pairs={{4,0},{8,4},{12,8},{16,12},{20,16},{24,20},{28,24},{32,28},{36,32}... | collective-permute-start | bytes 184328 | tf_op jit(solution)/shard_map/ppermute | solution.py:870
  44.5 0.1 shard_map.75._
  44.6 1.9 %collective-permute-done.6.from_left = f32[3,40,128]{2,1,0:T(8,128)S(1)} collective-permute-done((f32[3,40,128]{2,1,0:T(8,128)S(1)}, f32[3,40,128]{2,1,0:T(8,128)S(1)}, u32[]{:S(2)}, u32[]{:S(2)}) %collective-permute-start.6) | collective-permute-done | bytes 61472 | tf_op jit(solution)/shard_map/ppermute | solution.py:869
  46.5 0.0 collective-permute-done.7.from_right
  46.5 1.1 %shard_map.76 = (f32[3,6,64,128]{3,2,1,0:T(8,128)S(1)}, f32[19,2,64,128]{3,2,1,0:T(8,128)S(1)}, f32[10,2,64,128]{3,2,1,0:T(8,128)S(1)}, f32[2,40,128]{2,1,0:T(8,...) custom-call(f32[3,40,128]{2,1,0:T(8,128)S(1)} %collective-permute-do, ...), custom_call_target="tpu_custom_call", output_to_operand_aliasing={{0}: (7, {})} | custom-call | bytes 2236416 | tf_op jit(solution)/shard_map/pallas_call | solution.py:849
  47.6 0.1 collective-permute-start.8
  47.7 5.7 %collective-permute-start.9 = (f32[280,128]{1,0:T(8,128)S(1)}, f32[280,128]{1,0:T(8,128)S(1)}, u32[]{:S(2)}, u32[]{:S(2)}) collective-permute-start(f32[280,128]{1,0:T(8,128)S(1)} %get-tuple-element.102), channel_id=1, source_target_pairs={{4,0},{8,4},{12,8},{16,12},{20,16},{24,20},{28,24},{32,28},{36,32}... | collective-permute-start | bytes 430088 | tf_op jit(solution)/shard_map/ppermute | solution.py:870
  53.3 2.9 %collective-permute-done.8.from_left = f32[280,128]{1,0:T(8,128)S(1)} collective-permute-done((f32[280,128]{1,0:T(8,128)S(1)}, f32[280,128]{1,0:T(8,128)S(1)}, u32[]{:S(2)}, u32[]{:S(2)}) %collective-permute-start.8) | collective-permute-done | bytes 143392 | tf_op jit(solution)/shard_map/ppermute | solution.py:869
  56.2 0.0 collective-permute-done.9.from_right
  56.2 0.6 shard_map.77
  56.9 1.9 %collective-permute-start.12 = (f32[1,256]{1,0:T(1,128)S(1)}, f32[1,256]{1,0:T(1,128)S(1)}, u32[]{:S(2)}, u32[]{:S(2)}) collective-permute-start(f32[1,256]{1,0:T(1,128)S(1)} %get-tuple-element.107), channel_id=1, source_target_pairs={{0,3},{1,0},{2,1},{3,2},{4,7},{5,4},{6,5},{7,6},{8,11},{9,8},{10,9... | collective-permute-start | bytes 3080 | tf_op jit(solution)/shard_map/ppermute | solution.py:951
  58.8 2.8 %collective-permute-start.11 = (f32[1,256]{1,0:T(1,128)S(1)}, f32[1,256]{1,0:T(1,128)S(1)}, u32[]{:S(2)}, u32[]{:S(2)}) collective-permute-start(f32[1,256]{1,0:T(1,128)S(1)} %get-tuple-element.107), channel_id=1, source_target_pairs={{0,2},{1,3},{2,0},{3,1},{4,6},{5,7},{6,4},{7,5},{8,10},{9,11},{10,... | collective-permute-start | bytes 3080 | tf_op jit(solution)/shard_map/ppermute | solution.py:951
  61.6 0.4 collective-permute-start.10
  62.0 1.3 %shard_map.78 = f32[19,2,32,128]{3,2,1,0:T(8,128)} custom-call(f32[19,2,64,128]{3,2,1,0:T(8,128)S(1)} %get-tuple-element.96.adjoint, f32[10,2,64,128]{3,2,1,0:T(8,128)S(1)} %get-tuple-element.97.turned, f32[2,32,128]{2,1,0:T(8,128)S(1)} %get-tuple-element.105.more, f32[280,128]{1,0:T(8,128)S(1)} %collective-permute-done.8.from_left, ...), custom_call_target="tpu_custom_call" | custom-call | bytes 3448832 | tf_op jit(solution)/shard_map/pallas_call | solution.py:849
  63.3 0.0 collective-permute-done.12
  63.3 0.0 collective-permute-done.11
  63.3 0.0 collective-permute-done.10
  63.3 0.6 add_add_fusion
Async XLA Ops:
  1.8 6.8 %collective-permute-start = (f32[22,2,8,128]{3,2,1,0:T(8,128)S(1)}, f32[22,2,8,128]{3,2,1,0:T(8,128)S(1)}, u32[]{:S(2)}, u32[]{:S(2)}) collective-permute-start(f32[22,2,8,128]{3,2,1,0:T(8,128)S(1)} %get-tuple-element.56), channel_id=1, source_target_pairs={{0,1},{1,2},{2,3},{3,0},{4,5},{5,6},{6,7},{7,4},{8,9},{9,10},{10,1... | collective-permute-start | bytes 540680 | tf_op jit(solution)/shard_map/ppermute | solution.py:869
  6.2 6.6 %collective-permute-start.1 = (f32[22,2,8,128]{3,2,1,0:T(8,128)S(1)}, f32[22,2,8,128]{3,2,1,0:T(8,128)S(1)}, u32[]{:S(2)}, u32[]{:S(2)}) collective-permute-start(f32[22,2,8,128]{3,2,1,0:T(8,128)S(1)} %get-tuple-element.57), channel_id=1, source_target_pairs={{1,0},{2,1},{3,2},{0,3},{5,4},{6,5},{7,6},{4,7},{9,8},{10,9},{11,1... | collective-permute-start | bytes 540680 | tf_op jit(solution)/shard_map/ppermute | solution.py:870
  6.2 1.1 %copy-start = (f32[19,2,32,128]{3,2,1,0:T(8,128)S(1)}, f32[19,2,32,128]{3,2,1,0:T(8,128)}, u32[]{:S(2)}) copy-start(f32[19,2,32,128]{3,2,1,0:T(8,128)} %pops.3) | copy-start | bytes 1867780
  13.0 12.3 %collective-permute-start.2 = (f32[456,128]{1,0:T(8,128)S(1)}, f32[456,128]{1,0:T(8,128)S(1)}, u32[]{:S(2)}, u32[]{:S(2)}) collective-permute-start(f32[456,128]{1,0:T(8,128)S(1)} %get-tuple-element.73), channel_id=1, source_target_pairs={{0,4},{4,8},{8,12},{12,16},{16,20},{20,24},{24,28},{28,32},{32,36}... | collective-permute-start | bytes 700424 | tf_op jit(solution)/shard_map/ppermute | solution.py:869
  14.1 11.2 %collective-permute-start.3 = (f32[456,128]{1,0:T(8,128)S(1)}, f32[456,128]{1,0:T(8,128)S(1)}, u32[]{:S(2)}, u32[]{:S(2)}) collective-permute-start(f32[456,128]{1,0:T(8,128)S(1)} %get-tuple-element.74), channel_id=1, source_target_pairs={{4,0},{8,4},{12,8},{16,12},{20,16},{24,20},{28,24},{32,28},{36,32}... | collective-permute-start | bytes 700424 | tf_op jit(solution)/shard_map/ppermute | solution.py:870
  26.4 10.9 %collective-permute-start.4 = (f32[376,128]{1,0:T(8,128)S(1)}, f32[376,128]{1,0:T(8,128)S(1)}, u32[]{:S(2)}, u32[]{:S(2)}) collective-permute-start(f32[376,128]{1,0:T(8,128)S(1)} %get-tuple-element.85), channel_id=1, source_target_pairs={{0,4},{4,8},{8,12},{12,16},{16,20},{20,24},{24,28},{28,32},{32,36}... | collective-permute-start | bytes 577544 | tf_op jit(solution)/shard_map/ppermute | solution.py:869
  26.5 10.8 %collective-permute-start.5 = (f32[376,128]{1,0:T(8,128)S(1)}, f32[376,128]{1,0:T(8,128)S(1)}, u32[]{:S(2)}, u32[]{:S(2)}) collective-permute-start(f32[376,128]{1,0:T(8,128)S(1)} %get-tuple-element.86), channel_id=1, source_target_pairs={{4,0},{8,4},{12,8},{16,12},{20,16},{24,20},{28,24},{32,28},{36,32}... | collective-permute-start | bytes 577544 | tf_op jit(solution)/shard_map/ppermute | solution.py:870
  38.1 8.4 %collective-permute-start.6 = (f32[3,40,128]{2,1,0:T(8,128)S(1)}, f32[3,40,128]{2,1,0:T(8,128)S(1)}, u32[]{:S(2)}, u32[]{:S(2)}) collective-permute-start(f32[3,40,128]{2,1,0:T(8,128)S(1)} %get-tuple-element.89), channel_id=1, source_target_pairs={{0,4},{4,8},{8,12},{12,16},{16,20},{20,24},{24,28},{28,32},{32,36}... | collective-permute-start | bytes 184328 | tf_op jit(solution)/shard_map/ppermute | solution.py:869
  38.2 8.3 %collective-permute-start.7 = (f32[3,40,128]{2,1,0:T(8,128)S(1)}, f32[3,40,128]{2,1,0:T(8,128)S(1)}, u32[]{:S(2)}, u32[]{:S(2)}) collective-permute-start(f32[3,40,128]{2,1,0:T(8,128)S(1)} %get-tuple-element.90), channel_id=1, source_target_pairs={{4,0},{8,4},{12,8},{16,12},{20,16},{24,20},{28,24},{32,28},{36,32}... | collective-permute-start | bytes 184328 | tf_op jit(solution)/shard_map/ppermute | solution.py:870
  47.6 8.7 %collective-permute-start.8 = (f32[280,128]{1,0:T(8,128)S(1)}, f32[280,128]{1,0:T(8,128)S(1)}, u32[]{:S(2)}, u32[]{:S(2)}) collective-permute-start(f32[280,128]{1,0:T(8,128)S(1)} %get-tuple-element.101), channel_id=1, source_target_pairs={{0,4},{4,8},{8,12},{12,16},{16,20},{20,24},{24,28},{28,32},{32,36}... | collective-permute-start | bytes 430088 | tf_op jit(solution)/shard_map/ppermute | solution.py:869
  47.7 8.6 %collective-permute-start.9 = (f32[280,128]{1,0:T(8,128)S(1)}, f32[280,128]{1,0:T(8,128)S(1)}, u32[]{:S(2)}, u32[]{:S(2)}) collective-permute-start(f32[280,128]{1,0:T(8,128)S(1)} %get-tuple-element.102), channel_id=1, source_target_pairs={{4,0},{8,4},{12,8},{16,12},{20,16},{24,20},{28,24},{32,28},{36,32}... | collective-permute-start | bytes 430088 | tf_op jit(solution)/shard_map/ppermute | solution.py:870
  56.9 6.4 %collective-permute-start.12 = (f32[1,256]{1,0:T(1,128)S(1)}, f32[1,256]{1,0:T(1,128)S(1)}, u32[]{:S(2)}, u32[]{:S(2)}) collective-permute-start(f32[1,256]{1,0:T(1,128)S(1)} %get-tuple-element.107), channel_id=1, source_target_pairs={{0,3},{1,0},{2,1},{3,2},{4,7},{5,4},{6,5},{7,6},{8,11},{9,8},{10,9... | collective-permute-start | bytes 3080 | tf_op jit(solution)/shard_map/ppermute | solution.py:951
  58.8 4.5 %collective-permute-start.11 = (f32[1,256]{1,0:T(1,128)S(1)}, f32[1,256]{1,0:T(1,128)S(1)}, u32[]{:S(2)}, u32[]{:S(2)}) collective-permute-start(f32[1,256]{1,0:T(1,128)S(1)} %get-tuple-element.107), channel_id=1, source_target_pairs={{0,2},{1,3},{2,0},{3,1},{4,6},{5,7},{6,4},{7,5},{8,10},{9,11},{10,... | collective-permute-start | bytes 3080 | tf_op jit(solution)/shard_map/ppermute | solution.py:951
  61.6 1.7 %collective-permute-start.10 = (f32[1,256]{1,0:T(1,128)S(1)}, f32[1,256]{1,0:T(1,128)S(1)}, u32[]{:S(2)}, u32[]{:S(2)}) collective-permute-start(f32[1,256]{1,0:T(1,128)S(1)} %get-tuple-element.107), channel_id=1, source_target_pairs={{0,1},{1,2},{2,3},{3,0},{4,5},{5,6},{6,7},{7,4},{8,9},{9,10},{10,1... | collective-permute-start | bytes 3080 | tf_op jit(solution)/shard_map/ppermute | solution.py:951
